TPU v7x, 128 devices: a whole 4x4x4 slice. The times are simulated.
128 devices in a mesh: row: 8 (over y, core), col: 16 (over x, z).
Axes of the slice: x: 4, y: 4, z: 4, core: 2. Of those that a mesh axis runs over, the one named last changes fastest.
Arguments:
- inputs: bfloat16 [1024, 12288], P('col', 'row'), may hold values from -6 to 6
- pre_act: bfloat16 [1024, 24576], P('row', 'col'), may hold values from -6 to 6
- out_grad: bfloat16 [1024, 12288], P('col', 'row'), may hold values from -6 to 6
- up_payload: bfloat16 [12288, 24576], P('row', 'col'), may hold values from -15 to 15, as said below
- up_scale: int32 [384, 24576], P('row', 'col'), may hold values from -10 to -8
- down_payload: bfloat16 [24576, 12288], P('col', 'row'), may hold values from -15 to 15, as said below
- down_scale: int32 [768, 12288], P('col', 'row'), may hold values from -11 to -9
Outputs:
- input_grad: bfloat16 [1024, 12288], P('col', 'row')
- up_grad: bfloat16 [12288, 24576], P('row', 'col')
- down_grad: bfloat16 [24576, 12288], P('col', 'row')
Inputs may be any that keep to these rules, and one draw needn't show every extreme that they name: `up_payload`: each entry is an FP8 E4M3 number: a sign times (1 + m / 8) times 2 ** e, m from 0 to 7, e from 0 to 3. `down_payload`: each entry is an FP8 E4M3 number: a sign times (1 + m / 8) times 2 ** e, m from 0 to 7, e from 0 to 3.
All inputs are finite; a program needn't handle non-finite values.
Results may differ from a plain program's by a relative error of at most 0.005.
Values may be sent and summed in bfloat16 or wider, within the bound.
No kernel may reach another device: no remote copies, remote signals or barrier semaphores. Data moves between devices by JAX's collectives and lax.ppermute only.
A program may use at most 128 MiB of HBM per device.

v0:
```python
import jax
import jax.numpy as jnp
from jax import lax
from jax.sharding import PartitionSpec as P


def dequantize(payload, scale):
    rows, cols = payload.shape
    blocks = payload.astype(jnp.float32).reshape(rows // 32, 32, cols)
    factor = jnp.exp2(scale.astype(jnp.float32))[:, None, :]
    return (blocks * factor).reshape(rows, cols).astype(jnp.bfloat16)


def gelu_terms(pre):
    values = pre.astype(jnp.float32)
    normal_cdf = 0.5 * (1.0 + jax.scipy.special.erf(values * 0.7071067811865476))
    activated = values * normal_cdf
    gelu_slope = normal_cdf + values * jnp.exp(-0.5 * values * values) * 0.3989422804014327
    return (activated, gelu_slope)


def contract(left, right, left_dim, right_dim):
    return lax.dot_general(
        left, right, (((left_dim,), (right_dim,)), ((), ())), preferred_element_type=jnp.float32
    )


def per_device(inputs, pre_act, out_grad, up_payload, up_scale, down_payload, down_scale):
    up_weight = dequantize(up_payload, up_scale)
    down_weight = dequantize(down_payload, down_scale)
    grad_full, input_full = (
        lax.all_gather(out_grad, "col", axis=0, tiled=True),
        lax.all_gather(inputs, "col", axis=0, tiled=True),
    )
    partial_value = contract(grad_full, down_weight, 1, 1)
    hidden_grad = lax.psum_scatter(partial_value, "row", scatter_dimension=0, tiled=True)
    activated, gelu_slope = gelu_terms(pre_act)
    gated_grad = (gelu_slope * hidden_grad).astype(jnp.bfloat16)
    activated = activated.astype(jnp.bfloat16)
    act_full, gated_full = (
        lax.all_gather(activated, "row", axis=0, tiled=True),
        lax.all_gather(gated_grad, "row", axis=0, tiled=True),
    )
    down_grad = contract(act_full, grad_full, 0, 0).astype(jnp.bfloat16)
    up_grad = contract(input_full, gated_full, 0, 0).astype(jnp.bfloat16)
    input_terms = contract(gated_full, up_weight, 1, 1)
    input_grad = lax.psum_scatter(input_terms, "col", scatter_dimension=0, tiled=True).astype(
        jnp.bfloat16
    )
    return (input_grad, up_grad, down_grad)


def solution(mesh):
    placed = (
        P("col", "row"),
        P("row", "col"),
        P("col", "row"),
        P("row", "col"),
        P("row", "col"),
        P("col", "row"),
        P("col", "row"),
    )
    return jax.shard_map(
        per_device,
        mesh=mesh,
        in_specs=placed,
        out_specs=(P("col", "row"), P("row", "col"), P("col", "row")),
        check_vma=False,
    )
```

profile of v0, /device:TPU:0, one launch (start us, length us, event | category | flops | bytes accessed | tf_op | source)
XLA Modules:
  0.0 323.5 jit_solution(11800606817663288305)
XLA Ops:
  7.2 0.0 all-gather.5.cloned.1.call-start
  7.2 0.7 all-gather.5.cloned.1.call-update
  7.9 0.0 reduce-scatter.3.cloned.1.call-start
  7.9 1.0 multiply_exponential_fusion.1
  9.0 5.4 %fusion.1 = bf16[1536,1536]{1,0:T(8,128)(2,1)} fusion(bf16[1536,1536]{1,0:T(8,128)(2,1)} %param.12, f32[48,1536]{1,0:T(8,128)S(1)} %multiply_exponential_fusion.1), kind=kLoop, calls=%fused_computation.3 | loop fusion | flops 7077888 | bytes 9732096 | tf_op jit(solution)/shard_map/convert_element_type | solution.py:11
  14.4 46.4 %all-gather.5.cloned.1.call-done = bf16[1024,1536]{1,0:T(8,128)(2,1)} async-done(((bf16[64,1536]{1,0:T(8,128)(2,1)}), bf16[1024,1536]{1,0:T(8,128)(2,1)}) %all-gather.5.cloned.1.call-update) | async-done | bytes 3145744 | tf_op jit(solution)/shard_map/all_gather | solution.py:32
  60.8 9.9 %convolution_bitcast_fusion = f32[1024,1536]{0,1:T(8,128)} fusion(bf16[1536,1536]{1,0:T(8,128)(2,1)} %fusion.1, bf16[1024,1536]{1,0:T(8,128)(2,1)} %all-gather.5.cloned.1.call-done), kind=kOutput, calls=%fused_computation.7 | convolution fusion | flops 4831838208 | bytes 14155776 | tf_op jit(solution)/shard_map/dot_general | solution.py:23
  70.6 0.0 copy-start
  70.6 0.0 copy-start.1
  70.6 0.0 reduce-scatter.3.cloned.1.call-update
  70.7 0.0 all-gather.7.cloned.1.call-start
  70.7 0.9 copy-done
  71.6 0.2 copy.10
  71.9 40.3 %reduce-scatter.3.cloned.1.call-done = f32[128,1536]{0,1:T(8,128)} async-done(((f32[1024,1536]{0,1:T(8,128)}), f32[128,1536]{0,1:T(8,128)}) %reduce-scatter.3.cloned.1.call-update) | async-done | bytes 786448 | tf_op jit(solution)/shard_map/reduce_scatter | solution.py:36
  112.1 2.4 fusion.11
  114.5 0.0 all-gather.7.cloned.1.call-update
  114.6 0.0 all-gather.9.cloned.1.call-start
  114.6 0.5 all-gather.9.cloned.1.call-update
  115.1 0.0 all-gather.11.cloned.1.call-start
  115.2 0.5 all-gather.11.cloned.1.call-update
  115.7 0.2 reduce-scatter.5.cloned.1.call-start
  116.0 0.0 copy-done.1
  116.0 5.4 %fusion = bf16[1536,1536]{1,0:T(8,128)(2,1)} fusion(bf16[1536,1536]{1,0:T(8,128)(2,1)} %param.10, f32[48,1536]{1,0:T(8,128)S(1)} %multiply_exponential_fusion), kind=kLoop, calls=%fused_computation.1 | loop fusion | flops 7077888 | bytes 9732096 | tf_op jit(solution)/shard_map/convert_element_type | solution.py:11
  121.4 24.7 %all-gather.7.cloned.1.call-done = bf16[1024,1536]{0,1:T(8,128)(2,1)} async-done(((bf16[128,1536]{0,1:T(8,128)(2,1)}), bf16[1024,1536]{0,1:T(8,128)(2,1)}) %all-gather.7.cloned.1.call-update) | async-done | bytes 3145744 | tf_op jit(solution)/shard_map/all_gather | solution.py:42
  146.1 9.9 %fusion.12 = f32[1024,1536]{1,0:T(8,128)} fusion(bf16[1024,1536]{0,1:T(8,128)(2,1)} %all-gather.7.cloned.1.call-done, bf16[1536,1536]{1,0:T(8,128)(2,1)} %fusion), kind=kOutput, calls=%fused_computation.24 | convolution fusion | flops 4831838208 | bytes 14155776 | tf_op jit(solution)/shard_map/dot_general | solution.py:23
  156.0 0.0 copy-start.3
  156.0 0.0 reduce-scatter.5.cloned.1.call-update
  156.0 41.2 %all-gather.9.cloned.1.call-done = bf16[1024,1536]{1,0:T(8,128)(2,1)} async-done(((bf16[64,1536]{1,0:T(8,128)(2,1)}), bf16[1024,1536]{1,0:T(8,128)(2,1)}) %all-gather.9.cloned.1.call-update) | async-done | bytes 3145744 | tf_op jit(solution)/shard_map/all_gather | solution.py:33
  197.2 0.0 copy-done.3
  197.2 8.5 %fusion.2 = bf16[1536,1536]{0,1:T(8,128)(2,1)} fusion(bf16[1024,1536]{0,1:T(8,128)(2,1)S(1)} %copy-done.3, bf16[1024,1536]{1,0:T(8,128)(2,1)} %all-gather.9.cloned.1.call-done), kind=kOutput, calls=%fused_computation.6 | convolution fusion | flops 4834197504 | bytes 11010048 | tf_op jit(solution)/shard_map/dot_general | solution.py:23
  205.7 0.0 copy-start.2
  205.7 6.9 %copy.11 = bf16[1536,1536]{1,0:T(8,128)(2,1)} copy(bf16[1536,1536]{0,1:T(8,128)(2,1)} %fusion.2) | data formatting | bytes 9437184
  212.6 16.7 %all-gather.11.cloned.1.call-done = bf16[1024,1536]{0,1:T(8,128)(2,1)} async-done(((bf16[128,1536]{0,1:T(8,128)(2,1)}), bf16[1024,1536]{0,1:T(8,128)(2,1)}) %all-gather.11.cloned.1.call-update) | async-done | bytes 3145744 | tf_op jit(solution)/shard_map/all_gather | solution.py:41
  229.3 0.0 copy-done.2
  229.3 8.6 %convolution_convert_fusion = bf16[1536,1536]{1,0:T(8,128)(2,1)} fusion(bf16[1024,1536]{0,1:T(8,128)(2,1)} %all-gather.11.cloned.1.call-done, bf16[1024,1536]{1,0:T(8,128)(2,1)S(1)} %copy-done.2), kind=kOutput, calls=%fused_computation.4 | convolution fusion | flops 4834197504 | bytes 11010048 | tf_op jit(solution)/shard_map/dot_general | solution.py:23
  237.8 77.2 %reduce-scatter.5.cloned.1.call-done = f32[64,1536]{1,0:T(8,128)} async-done(((f32[1024,1536]{1,0:T(8,128)}), f32[64,1536]{1,0:T(8,128)}) %reduce-scatter.5.cloned.1.call-update) | async-done | bytes 393232 | tf_op jit(solution)/shard_map/reduce_scatter | solution.py:47
  315.0 1.7 convert_element_type.47
  (1 shorter events, 0.0 us)
Async XLA Ops:
  7.2 53.6 %all-gather.5.cloned.1.call-start = ((), (), s32[]{:S(2)}) async-start(), calls=%async_computation.2 | async-start | bytes 3342336 | tf_op jit(solution)/shard_map/all_gather | solution.py:32
  7.9 104.2 %reduce-scatter.3.cloned.1.call-start = ((), (), s32[]{:S(2)}) async-start(), calls=%async_computation.3 | async-start | bytes 7077888 | tf_op jit(solution)/shard_map/reduce_scatter | solution.py:36
  70.6 1.0 copy-start
  70.6 45.3 %copy-start.1 = (s32[48,1536]{1,0:T(8,128)S(1)}, s32[48,1536]{1,0:T(8,128)}, u32[]{:S(2)}) copy-start(s32[48,1536]{1,0:T(8,128)} %param.11) | copy-start | bytes 884740
  70.7 75.4 %all-gather.7.cloned.1.call-start = ((), (), s32[]{:S(2)}) async-start(), calls=%async_computation.4 | async-start | bytes 3538944 | tf_op jit(solution)/shard_map/all_gather | solution.py:42
  114.6 82.6 %all-gather.9.cloned.1.call-start = ((), (), s32[]{:S(2)}) async-start(), calls=%async_computation.6 | async-start | bytes 3342336 | tf_op jit(solution)/shard_map/all_gather | solution.py:33
  115.1 114.1 %all-gather.11.cloned.1.call-start = ((), (), s32[]{:S(2)}) async-start(), calls=%async_computation.7 | async-start | bytes 3538944 | tf_op jit(solution)/shard_map/all_gather | solution.py:41
  115.7 199.2 %reduce-scatter.5.cloned.1.call-start = ((), (), s32[]{:S(2)}) async-start(), calls=%async_computation.5 | async-start | bytes 6684672 | tf_op jit(solution)/shard_map/reduce_scatter | solution.py:47
  156.0 41.2 %copy-start.3 = (bf16[1024,1536]{0,1:T(8,128)(2,1)S(1)}, bf16[1024,1536]{0,1:T(8,128)(2,1)}, u32[]{:S(2)}) copy-start(bf16[1024,1536]{0,1:T(8,128)(2,1)} %all-gather.7.cloned.1.call-done) | copy-start | bytes 9437188
  205.7 23.5 %copy-start.2 = (bf16[1024,1536]{1,0:T(8,128)(2,1)S(1)}, bf16[1024,1536]{1,0:T(8,128)(2,1)}, u32[]{:S(2)}) copy-start(bf16[1024,1536]{1,0:T(8,128)(2,1)} %all-gather.5.cloned.1.call-done) | copy-start | bytes 9437188
Sparse Core Ops, SparseCore 0:
  10.2 50.5 all-gather.4
  70.8 41.2 reduce-scatter.2
  114.7 31.3 all-gather.6
  148.1 49.0 all-gather.8
  198.7 30.4 all-gather.10
  232.5 82.3 reduce-scatter.4
where the time goes:
time: 324 us
  waiting for transfers between devices  248 us (77%)
  matrix products  36.8 us (11%)
  other arithmetic  16 us (5%)
  between operations  14.1 us (4%)
  local copies, waits for them, and re-layouts  8.02 us (2%)
    reduce_scatter x1, waiting for transfers between devices, per_device(): lax.psum_scatter(input_terms, 'col', scatter_dimension=0, tiled=True)  77.2 us
    all_gather x1, waiting for transfers between devices, per_device(): lax.all_gather(out_grad, 'col', axis=0, tiled=True)  46.4 us
    all_gather x1, waiting for transfers between devices, per_device(): lax.all_gather(inputs, 'col', axis=0, tiled=True)  41.2 us
    reduce_scatter x1, waiting for transfers between devices, per_device(): lax.psum_scatter(partial_value, 'row', scatter_dimension=0, tiled=True)  40.3 us
    dot_general x4, matrix products, contract(): lax.dot_general(left, right, (((left_dim,), (right_dim,)), ((), ())), pre...  36.8 us
    all_gather x1, waiting for transfers between devices, per_device(): lax.all_gather(gated_grad, 'row', axis=0, tiled=True)  24.7 us
    all_gather x1, waiting for transfers between devices, per_device(): lax.all_gather(activated, 'row', axis=0, tiled=True)  16.7 us
    convert_element_type x2, other arithmetic, dequantize(): return (blocks * factor).reshape(rows, cols).astype(jnp.bfloat16)  10.8 us
  transfers between devices with their start and end apart: 6, of which 6 were waited for; matrix products, arithmetic and copies ran while one was open for 14% of the time, Pallas kernels for 0%

commit v1 on v0

v1 whole, which is shorter than its diff:
```python
import jax
import jax.numpy as jnp
from jax import lax
from jax.experimental import pallas as pl
from jax.experimental.pallas import tpu as pltpu
from jax.sharding import Mesh
from jax.sharding import PartitionSpec as P

BF16, F32 = jnp.bfloat16, jnp.float32
TILE = 256


def dequantize(payload, scale):
    rows, cols = payload.shape
    blocks = payload.astype(F32).reshape(rows // 32, 32, cols)
    factor = jnp.exp2(scale.astype(F32))[:, None, :]
    return (blocks * factor).reshape(rows, cols).astype(BF16)


def gelu_terms(pre):
    values = pre.astype(F32)
    normal_cdf = 0.5 * (1.0 + jax.scipy.special.erf(values * 0.7071067811865476))
    activated = values * normal_cdf
    gelu_slope = normal_cdf + values * jnp.exp(-0.5 * values * values) * 0.3989422804014327
    return (activated, gelu_slope)


def shift_grid(first, step):
    pairs = []
    for k in range(2):
        for x in range(4):
            for z in range(4):
                along_x = (k == 0) == first
                to = (k, (x - step) % 4, z) if along_x else (k, x, (z - step) % 4)
                pairs.append((k * 16 + x * 4 + z, to[0] * 16 + to[1] * 4 + to[2]))
    return pairs


def from_grid(value, first, step):
    return lax.ppermute(value, ("k", "x", "z"), shift_grid(first, step))


def from_y(value, step):
    return lax.ppermute(value, "y", [(i, (i - step) % 4) for i in range(4)])


def swap_cores(value):
    return lax.ppermute(value, "k", [(0, 1), (1, 0)])


def gather_grid(block):
    stage = jnp.concatenate([block] + [from_grid(block, True, step) for step in (1, 2, 3)])
    return [stage] + [from_grid(stage, False, step) for step in (1, 2, 3)]


def gather_y(block):
    own = jnp.concatenate([block] + [from_y(block, step) for step in (1, 2, 3)])
    return own, swap_cores(own)


def place_of(x, z):
    k, y = lax.axis_index("k"), lax.axis_index("y")
    half = lax.rem(z // 2 + k, 2)
    return half * 8 + lax.rem(x - y + 4, 4) * 2 + lax.rem(z, 2)


def grid_position(i, j):
    k, x, z = lax.axis_index("k"), lax.axis_index("x"), lax.axis_index("z")
    x = lax.rem(x + jnp.where(k == 0, i, j), 4)
    z = lax.rem(z + jnp.where(k == 0, j, i), 4)
    return x, z


def collect(pieces, held, sems):
    copies = []
    for j in range(4):
        for i in range(4):
            place = place_of(*grid_position(i, j))
            rows = pl.ds(pl.multiple_of(place * 64, 64), 64)
            copies.append(
                pltpu.make_async_copy(pieces[j].at[pl.ds(i * 64, 64)], held.at[rows], sems.at[j * 4 + i])
            )
    for copy in copies:
        copy.start()
    for copy in copies:
        copy.wait()


NT = (((1,), (1,)), ((), ()))
TN = (((0,), (0,)), ((), ()))
ANY = pl.BlockSpec(memory_space=pl.ANY)


def params():
    return pltpu.CompilerParams(vmem_limit_bytes=32 * 1024 * 1024)


def cost(flops, moved):
    return pl.CostEstimate(flops=flops, bytes_accessed=moved, transcendentals=0)


def hidden_kernel(p0, p1, p2, p3, w, other, own, held, sems):
    @pl.when(pl.program_id(0) == 0)
    def _():
        collect([p0, p1, p2, p3], held, sems)

    weight = w[...]
    own[...] = lax.dot_general(held[:512], weight, NT, preferred_element_type=F32)
    other[...] = lax.dot_general(held[512:], weight, NT, preferred_element_type=F32).astype(BF16)


def hidden_partial(pieces, weight):
    n, depth = weight.shape
    return pl.pallas_call(
        hidden_kernel,
        grid=(n // TILE,),
        out_shape=(jax.ShapeDtypeStruct((512, n), BF16), jax.ShapeDtypeStruct((512, n), F32)),
        in_specs=[ANY] * 4 + [pl.BlockSpec((TILE, depth), lambda i: (i, 0))],
        out_specs=[pl.BlockSpec((512, TILE), lambda i: (0, i))] * 2,
        scratch_shapes=[pltpu.VMEM((1024, depth), BF16), pltpu.SemaphoreType.DMA((16,))],
        compiler_params=params(),
        cost_estimate=cost(2 * 1024 * n * depth, 2 * (1024 + n) * depth + 6 * 512 * n),
        name="hidden_partial",
    )(*pieces, weight)


def input_kernel(mine, theirs, w, o0, o1, o2, o3, held, sems):
    @pl.when(pl.program_id(0) == 0)
    def _():
        copies = []
        for j in range(4):
            for i in range(4):
                place = place_of(*grid_position(i, j))
                rows = pl.ds(pl.multiple_of(lax.rem(place, 8) * 64, 64), 64)
                to = held.at[pl.ds(i * 256 + j * 64, 64)]
                sem = sems.at[i * 4 + j]
                here = pltpu.make_async_copy(mine.at[rows], to, sem)
                there = pltpu.make_async_copy(theirs.at[rows], to, sem)
                pl.when(place < 8)(here.start)
                pl.when(place >= 8)(there.start)
                copies.append(here)
        for copy in copies:
            copy.wait()

    out = lax.dot_general(held[...], w[...], NT, preferred_element_type=F32)
    o0[...] = out[:256]
    o1[...] = out[256:512].astype(BF16)
    o2[...] = out[512:768].astype(BF16)
    o3[...] = out[768:].astype(BF16)


def input_partial(mine, theirs, weight):
    n, depth = weight.shape
    return pl.pallas_call(
        input_kernel,
        grid=(n // TILE,),
        out_shape=[jax.ShapeDtypeStruct((256, n), F32)] + [jax.ShapeDtypeStruct((256, n), BF16)] * 3,
        in_specs=[ANY] * 2 + [pl.BlockSpec((TILE, depth), lambda i: (i, 0))],
        out_specs=[pl.BlockSpec((256, TILE), lambda i: (0, i))] * 4,
        scratch_shapes=[pltpu.VMEM((1024, depth), BF16), pltpu.SemaphoreType.DMA((16,))],
        compiler_params=params(),
        cost_estimate=cost(2 * 1024 * n * depth, 2 * (1024 + n) * depth + 10 * 256 * n),
        name="input_partial",
    )(mine, theirs, weight)


def down_kernel(mine, theirs, p0, p1, p2, p3, out, held, sems):
    @pl.when(pl.program_id(0) == 0)
    def _():
        collect([p0, p1, p2, p3], held, sems)

    total = lax.dot_general(mine[...], held[:512], TN, preferred_element_type=F32)
    total += lax.dot_general(theirs[...], held[512:], TN, preferred_element_type=F32)
    out[...] = total.astype(BF16)


def down_gradient(mine, theirs, pieces):
    m, n = mine.shape[1], pieces[0].shape[1]
    return pl.pallas_call(
        down_kernel,
        grid=(m // TILE,),
        out_shape=jax.ShapeDtypeStruct((m, n), BF16),
        in_specs=[pl.BlockSpec((512, TILE), lambda i: (0, i))] * 2 + [ANY] * 4,
        out_specs=pl.BlockSpec((TILE, n), lambda i: (i, 0)),
        scratch_shapes=[pltpu.VMEM((1024, n), BF16), pltpu.SemaphoreType.DMA((16,))],
        compiler_params=params(),
        cost_estimate=cost(2 * 1024 * n * m, 2 * 1024 * (n + m) + 2 * n * m),
        name="down_gradient",
    )(mine, theirs, *pieces)


def up_kernel(mine, theirs, p0, p1, p2, p3, out, held, sems):
    @pl.when(pl.program_id(0) == 0)
    def _():
        collect([p0, p1, p2, p3], held, sems)

    columns = pl.ds(pl.multiple_of(pl.program_id(0) * TILE, TILE), TILE)
    total = lax.dot_general(held[:512, columns], mine[...], TN, preferred_element_type=F32)
    total += lax.dot_general(held[512:, columns], theirs[...], TN, preferred_element_type=F32)
    out[...] = total.astype(BF16)


def up_gradient(mine, theirs, pieces):
    m, n = pieces[0].shape[1], mine.shape[1]
    return pl.pallas_call(
        up_kernel,
        grid=(m // TILE,),
        out_shape=jax.ShapeDtypeStruct((m, n), BF16),
        in_specs=[pl.BlockSpec((512, n), lambda i: (0, 0))] * 2 + [ANY] * 4,
        out_specs=pl.BlockSpec((TILE, n), lambda i: (i, 0)),
        scratch_shapes=[pltpu.VMEM((1024, m), BF16), pltpu.SemaphoreType.DMA((16,))],
        compiler_params=params(),
        cost_estimate=cost(2 * 1024 * n * m, 2 * 1024 * (n + m) + 2 * n * m),
        name="up_gradient",
    )(mine, theirs, *pieces)


def per_device(inputs, pre_act, out_grad, up_payload, up_scale, down_payload, down_scale):
    grad_pieces = gather_grid(out_grad)
    down_weight = dequantize(down_payload, down_scale)
    up_weight = dequantize(up_payload, up_scale)
    activated, gelu_slope = gelu_terms(pre_act)
    activated = activated.astype(BF16)

    other, own = hidden_partial(grad_pieces, down_weight)
    chip = own + swap_cores(other).astype(F32)
    hidden_grad = chip[:128]
    for step in (1, 2, 3):
        sent = chip[step * 128 : (step + 1) * 128].astype(BF16)
        hidden_grad = hidden_grad + from_y(sent, -step).astype(F32)
    gated_grad = (gelu_slope * hidden_grad).astype(BF16)

    gated_mine, gated_theirs = gather_y(gated_grad)
    parts = input_partial(gated_mine, gated_theirs, up_weight)
    rest = parts[0]
    for step in (1, 2, 3):
        rest = rest + from_grid(parts[step], True, -step).astype(F32)
    input_grad = rest[:64]
    for step in (1, 2, 3):
        sent = rest[step * 64 : (step + 1) * 64].astype(BF16)
        input_grad = input_grad + from_grid(sent, False, -step).astype(F32)
    input_grad = input_grad.astype(BF16)

    act_mine, act_theirs = gather_y(activated)
    down_grad = down_gradient(act_mine, act_theirs, grad_pieces)
    up_grad = up_gradient(gated_mine, gated_theirs, gather_grid(inputs))
    return (input_grad, up_grad, down_grad)


def solution(mesh):
    grid = Mesh(mesh.devices.reshape(4, 2, 4, 4), ("y", "k", "x", "z"))
    tokens, hidden = P(("x", "z"), ("y", "k")), P(("y", "k"), ("x", "z"))
    return jax.shard_map(
        per_device,
        mesh=grid,
        in_specs=(tokens, hidden, tokens, hidden, hidden, tokens, tokens),
        out_specs=(tokens, hidden, tokens),
        check_vma=False,
    )
```

time: 324 us -> 188 us (0.58)
  waiting for transfers between devices: 248 us -> 99.5 us
  Pallas kernels: 0 us -> 47.4 us
  matrix products: 36.8 us -> 0 us
  starting transfers between devices: 0.42 us -> 30.6 us
  between operations: 14.1 us -> 0.95 us
  other arithmetic: 16 us -> 7.62 us
  local copies, waits for them, and re-layouts: 8.02 us -> 1.23 us
    all_gather x4 -> x0, waiting for transfers between devices: 129 us -> none  [the longest x1 46.4 us: per_device(): lax.all_gather(out_grad, 'col', axis=0, tiled=True)]
    reduce_scatter x2 -> x0, waiting for transfers between devices: 117 us -> none  [the longest x1 77.2 us: per_device(): lax.psum_scatter(input_terms, 'col', scatter_dimension=0, tiled=True)]
    ppermute x0 -> x30, waiting for transfers between devices: none -> 99.5 us  [the longest x9 49.7 us: from_y(): return lax.ppermute(value, 'y', [(i, (i - step) % 4) for i in range(4)])]
    pallas_call x0 -> x4, Pallas kernels: none -> 47.4 us  [the longest x1 12.6 us: down_gradient(): pl.pallas_call(down_kernel, grid=(m // TILE,), out_shape=jax.ShapeDtypeSt...]
    dot_general x4 -> x0, matrix products: 36.8 us -> none  [contract(): lax.dot_general(left, right, (((left_dim,), (right_dim,)), ((), ())), pre...]
    ppermute x0 -> x30, starting transfers between devices: none -> 30.6 us  [the longest x18 19.3 us: from_grid(): return lax.ppermute(value, ('k', 'x', 'z'), shift_grid(first, step))]
    convert_element_type x4, other arithmetic: 14.9 us -> 5.4 us  [the longest x2 4.1 us: dequantize(): return (blocks * factor).reshape(rows, cols).astype(BF16)]
    unnamed x10 -> x16, local copies, waits for them, and re-layouts: 8.02 us -> 1.07 us
  transfers between devices with their start and end apart: 6 -> 30, of which waited for: 6 -> 14; matrix products, arithmetic and copies ran while one was open for 14% -> 4% of each run, Pallas kernels for 0% -> 19%
where the time goes in v1:
time: 188 us; the launch traced here: 187 us
  waiting for transfers between devices  99.5 us (53%)
  Pallas kernels  47.4 us (25%)
  starting transfers between devices  30.6 us (16%)
  other arithmetic  7.62 us (4%)
    ppermute x9, waiting for transfers between devices, from_y(): return lax.ppermute(value, 'y', [(i, (i - step) % 4) for i in range(4)])  49.7 us
    ppermute x18, waiting for transfers between devices, from_grid(): return lax.ppermute(value, ('k', 'x', 'z'), shift_grid(first, step))  46.4 us
    ppermute x18, starting transfers between devices, from_grid(): return lax.ppermute(value, ('k', 'x', 'z'), shift_grid(first, step))  19.3 us
    pallas_call x1, Pallas kernels, down_gradient(): pl.pallas_call(down_kernel, grid=(m // TILE,), out_shape=jax.ShapeDtypeSt...  12.6 us
    pallas_call x1, Pallas kernels, up_gradient(): pl.pallas_call(up_kernel, grid=(m // TILE,), out_shape=jax.ShapeDtypeStru...  12.1 us
    pallas_call x1, Pallas kernels, hidden_partial(): pl.pallas_call(hidden_kernel, grid=(n // TILE,), out_shape=(jax.ShapeDtyp...  11.6 us
    pallas_call x1, Pallas kernels, input_partial(): pl.pallas_call(input_kernel, grid=(n // TILE,), out_shape=[jax.ShapeDtype...  11.1 us
    ppermute x9, starting transfers between devices, from_y(): return lax.ppermute(value, 'y', [(i, (i - step) % 4) for i in range(4)])  10.9 us
  transfers between devices with their start and end apart: 30, of which 14 were waited for; matrix products, arithmetic and copies ran while one was open for 4% of the time, Pallas kernels for 19%

profile of v1, /device:TPU:0, one launch (start us, length us, event | category | flops | bytes accessed | tf_op | source)
XLA Modules:
  0.0 187.4 jit_solution(6137426940839922634)
XLA Ops:
  0.6 2.9 %collective-permute-start = (bf16[64,1536]{1,0:T(8,128)(2,1)}, bf16[64,1536]{1,0:T(8,128)(2,1)S(1)}, u32[]{:S(2)}, u32[]{:S(2)}) collective-permute-start(bf16[64,1536]{1,0:T(8,128)(2,1)} %param.9), channel_id=1, source_target_pairs={{0,12},{1,13},{2,14},{3,15},{4,0},{5,1},{6,2},{7,3},{8,4},{9,5},{1... | collective-permute-start | bytes 589832 | tf_op jit(solution)/shard_map/ppermute | solution.py:40
  3.5 0.8 collective-permute-start.1
  4.3 0.9 collective-permute-start.2
  5.2 1.0 constant_dynamic-update-slice_fusion.3
  6.2 3.0 %collective-permute-done = bf16[64,1536]{1,0:T(8,128)(2,1)S(1)} collective-permute-done((bf16[64,1536]{1,0:T(8,128)(2,1)}, bf16[64,1536]{1,0:T(8,128)(2,1)S(1)}, u32[]{:S(2)}, u32[]{:S(2)}) %collective-permute-start) | collective-permute-done | bytes 196640 | tf_op jit(solution)/shard_map/ppermute | solution.py:40
  9.2 1.8 collective-permute-done.1
  11.0 2.0 %collective-permute-done.2 = bf16[64,1536]{1,0:T(8,128)(2,1)S(1)} collective-permute-done((bf16[64,1536]{1,0:T(8,128)(2,1)}, bf16[64,1536]{1,0:T(8,128)(2,1)S(1)}, u32[]{:S(2)}, u32[]{:S(2)}) %collective-permute-start.2) | collective-permute-done | bytes 196640 | tf_op jit(solution)/shard_map/ppermute | solution.py:40
  13.1 4.1 %collective-permute-start.3 = (bf16[256,1536]{1,0:T(8,128)(2,1)S(1)}, bf16[256,1536]{1,0:T(8,128)(2,1)S(1)}, u32[]{:S(2)}, u32[]{:S(2)}) collective-permute-start(bf16[256,1536]{1,0:T(8,128)(2,1)S(1)} %constant_dynamic-update-slice_fusion.p0), channel_id=1, source_target_pairs={{0,3},{1,0},{2,1},{3,2},{4,7},{5,4},{6,5},{7,6},{8,11},{9,8},{10,9... | collective-permute-start | bytes 2359304 | tf_op jit(solution)/shard_map/ppermute | solution.py:40
  17.2 1.3 collective-permute-start.5
  18.4 1.0 multiply_exponential_fusion.1
  19.4 3.2 %fusion.1.w = bf16[1536,1536]{1,0:T(8,128)(2,1)S(1)} fusion(bf16[1536,1536]{1,0:T(8,128)(2,1)} %param.12, f32[48,1536]{1,0:T(8,128)S(1)} %multiply_exponential_fusion.1), kind=kLoop, calls=%fused_computation.3 | loop fusion | flops 7077888 | bytes 9732096 | tf_op jit(solution)/shard_map/convert_element_type | solution.py:17
  22.7 12.4 %collective-permute-done.3.p1 = bf16[256,1536]{1,0:T(8,128)(2,1)S(1)} collective-permute-done((bf16[256,1536]{1,0:T(8,128)(2,1)S(1)}, bf16[256,1536]{1,0:T(8,128)(2,1)S(1)}, u32[]{:S(2)}, u32[]{:S(2)}) %collective-permute-start.3) | collective-permute-done | bytes 786464 | tf_op jit(solution)/shard_map/ppermute | solution.py:40
  35.1 3.7 %collective-permute-done.5.p3 = bf16[256,1536]{1,0:T(8,128)(2,1)S(1)} collective-permute-done((bf16[256,1536]{1,0:T(8,128)(2,1)S(1)}, bf16[256,1536]{1,0:T(8,128)(2,1)S(1)}, u32[]{:S(2)}, u32[]{:S(2)}) %collective-permute-start.5) | collective-permute-done | bytes 786464 | tf_op jit(solution)/shard_map/ppermute | solution.py:40
  38.8 11.6 %hidden_partial.1 = (bf16[512,1536]{1,0:T(8,128)(2,1)S(1)}, f32[512,1536]{1,0:T(8,128)S(1)}) custom-call(bf16[256,1536]{1,0:T(8,128)(2,1)S(1)} %constant_dynamic-update-slice_fusion.p0, bf16[256,1536]{1,0:T(8,128)(2,1)S(1)} %collective-permute-done.3.p1, bf16[256,1536]{1,0:T(8,128)(2,1)S(1)} %collective-permute-done.4.p2, ...), custom_call_target="tpu_custom_call" | custom-call | flops 4831838208 | bytes 12582912 | tf_op jit(solution)/shard_map/hidden_partial/pallas_call | solution.py:114
  50.5 3.4 %collective-permute-done.6 = bf16[512,1536]{1,0:T(8,128)(2,1)S(1)} collective-permute-done((bf16[512,1536]{1,0:T(8,128)(2,1)S(1)}, bf16[512,1536]{1,0:T(8,128)(2,1)S(1)}, u32[]{:S(2)}, u32[]{:S(2)}) %collective-permute-start.6) | collective-permute-done | bytes 1572896 | tf_op jit(solution)/shard_map/ppermute | solution.py:48
  53.9 0.6 fusion.17
  54.6 3.1 %collective-permute-start.9 = (bf16[128,1536]{1,0:T(8,128)(2,1)S(1)}, bf16[128,1536]{1,0:T(8,128)(2,1)S(1)}, u32[]{:S(2)}, u32[]{:S(2)}) collective-permute-start(bf16[128,1536]{1,0:T(8,128)(2,1)S(1)} %get-tuple-element.20), channel_id=1, source_target_pairs={{0,96},{32,0},{64,32},{96,64},{1,97},{33,1},{65,33},{97,65},{2,98}... | collective-permute-start | bytes 1179656 | tf_op jit(solution)/shard_map/ppermute | solution.py:44
  57.6 0.6 collective-permute-start.8
  58.3 1.0 collective-permute-start.7
  59.2 15.5 %collective-permute-done.9 = bf16[128,1536]{1,0:T(8,128)(2,1)S(1)} collective-permute-done((bf16[128,1536]{1,0:T(8,128)(2,1)S(1)}, bf16[128,1536]{1,0:T(8,128)(2,1)S(1)}, u32[]{:S(2)}, u32[]{:S(2)}) %collective-permute-start.9) | collective-permute-done | bytes 393248 | tf_op jit(solution)/shard_map/ppermute | solution.py:44
  74.7 3.7 %collective-permute-done.7 = bf16[128,1536]{1,0:T(8,128)(2,1)S(1)} collective-permute-done((bf16[128,1536]{1,0:T(8,128)(2,1)S(1)}, bf16[128,1536]{1,0:T(8,128)(2,1)S(1)}, u32[]{:S(2)}, u32[]{:S(2)}) %collective-permute-start.7) | collective-permute-done | bytes 393248 | tf_op jit(solution)/shard_map/ppermute | solution.py:44
  78.4 0.5 fusion.10
  79.1 2.1 %collective-permute-start.11 = (bf16[128,1536]{1,0:T(8,128)(2,1)S(1)}, bf16[128,1536]{1,0:T(8,128)(2,1)S(1)}, u32[]{:S(2)}, u32[]{:S(2)}) collective-permute-start(bf16[128,1536]{1,0:T(8,128)(2,1)S(1)} %get-tuple-element.26), channel_id=1, source_target_pairs={{0,64},{32,96},{64,0},{96,32},{1,65},{33,97},{65,1},{97,33},{2,66}... | collective-permute-start | bytes 1179656 | tf_op jit(solution)/shard_map/ppermute | solution.py:44
  81.1 1.2 collective-permute-start.10
  82.3 0.8 collective-permute-start.28
  83.1 2.1 %collective-permute-start.27 = (bf16[128,1536]{1,0:T(8,128)(2,1)S(1)}, bf16[128,1536]{1,0:T(8,128)(2,1)S(1)}, u32[]{:S(2)}, u32[]{:S(2)}) collective-permute-start(bf16[128,1536]{1,0:T(8,128)(2,1)S(1)} %get-tuple-element.25), channel_id=1, source_target_pairs={{0,64},{32,96},{64,0},{96,32},{1,65},{33,97},{65,1},{97,33},{2,66}... | collective-permute-start | bytes 1179656 | tf_op jit(solution)/shard_map/ppermute | solution.py:44
  85.2 15.4 %collective-permute-done.12 = bf16[128,1536]{1,0:T(8,128)(2,1)S(1)} collective-permute-done((bf16[128,1536]{1,0:T(8,128)(2,1)S(1)}, bf16[128,1536]{1,0:T(8,128)(2,1)S(1)}, u32[]{:S(2)}, u32[]{:S(2)}) %collective-permute-start.12) | collective-permute-done | bytes 393248 | tf_op jit(solution)/shard_map/ppermute | solution.py:44
  100.7 0.9 collective-permute-done.10
  101.6 0.1 pad_maximum_fusion.mine
  101.8 0.7 collective-permute-start.20
  102.4 14.1 %collective-permute-done.28 = bf16[128,1536]{1,0:T(8,128)(2,1)S(1)} collective-permute-done((bf16[128,1536]{1,0:T(8,128)(2,1)S(1)}, bf16[128,1536]{1,0:T(8,128)(2,1)S(1)}, u32[]{:S(2)}, u32[]{:S(2)}) %collective-permute-start.28) | collective-permute-done | bytes 393248 | tf_op jit(solution)/shard_map/ppermute | solution.py:44
  116.6 0.8 collective-permute-start.21
  117.4 0.6 collective-permute-start.22
  118.0 0.1 pad_maximum_fusion.1.mine
  118.1 0.3 collective-permute-start.29
  118.5 0.9 fusion.w
  119.5 11.1 %input_partial.1 = (f32[256,1536]{1,0:T(8,128)S(1)}, bf16[256,1536]{1,0:T(8,128)(2,1)S(1)}, bf16[256,1536]{1,0:T(8,128)(2,1)S(1)}, bf16[256,1536]{1,0:T(8,128)(2,1)S(1)}) custom-call(bf16[512,1536]{1,0:T(8,128)(2,1)S(1)} %pad_maximum_fusion.mine, bf16[512,1536]{1,0:T(8,128)(2,1)S(1)} %collective-permute-done.13.theirs, bf16[1536,1536]{1,0:T(8,128)(2,1)S(1)} %fusion.w), custom_call_target="tpu_custom_call" | custom-call | flops 4831838208 | bytes 11796480 | tf_op jit(solution)/shard_map/input_partial/pallas_call | solution.py:154
  130.6 2.7 %collective-permute-start.16 = (bf16[256,1536]{1,0:T(8,128)(2,1)S(1)}, bf16[256,1536]{1,0:T(8,128)(2,1)S(1)}, u32[]{:S(2)}, u32[]{:S(2)}) collective-permute-start(bf16[256,1536]{1,0:T(8,128)(2,1)S(1)} %get-tuple-element.14), channel_id=1, source_target_pairs={{0,12},{1,13},{2,14},{3,15},{4,0},{5,1},{6,2},{7,3},{8,4},{9,5},{1... | collective-permute-start | bytes 2359304 | tf_op jit(solution)/shard_map/ppermute | solution.py:40
  133.2 1.5 collective-permute-start.15
  134.8 1.0 collective-permute-start.23
  135.8 12.6 %down_gradient.1 = bf16[1536,1536]{1,0:T(8,128)(2,1)} custom-call(bf16[512,1536]{1,0:T(8,128)(2,1)S(1)} %pad_maximum_fusion.1.mine, bf16[512,1536]{1,0:T(8,128)(2,1)S(1)} %collective-permute-done.29.theirs, bf16[256,1536]{1,0:T(8,128)(2,1)S(1)} %constant_dynamic-update-slice_fusion.p0, bf16[256,1536]{1,0:T(8,128)(2,1)S(1)} %collective-permute-done.3.p1, ...), custom_call_target="tpu_custom_call" | custom-call | flops 4831838208 | bytes 11010048 | tf_op jit(solution)/shard_map/down_gradient/pallas_call | solution.py:179
  148.4 2.5 %collective-permute-done.16 = bf16[256,1536]{1,0:T(8,128)(2,1)S(1)} collective-permute-done((bf16[256,1536]{1,0:T(8,128)(2,1)S(1)}, bf16[256,1536]{1,0:T(8,128)(2,1)S(1)}, u32[]{:S(2)}, u32[]{:S(2)}) %collective-permute-start.16) | collective-permute-done | bytes 786464 | tf_op jit(solution)/shard_map/ppermute | solution.py:40
  151.0 3.5 %collective-permute-done.15 = bf16[256,1536]{1,0:T(8,128)(2,1)S(1)} collective-permute-done((bf16[256,1536]{1,0:T(8,128)(2,1)S(1)}, bf16[256,1536]{1,0:T(8,128)(2,1)S(1)}, u32[]{:S(2)}, u32[]{:S(2)}) %collective-permute-start.15) | collective-permute-done | bytes 786464 | tf_op jit(solution)/shard_map/ppermute | solution.py:40
  154.4 17.5 %collective-permute-done.14 = bf16[256,1536]{1,0:T(8,128)(2,1)S(1)} collective-permute-done((bf16[256,1536]{1,0:T(8,128)(2,1)S(1)}, bf16[256,1536]{1,0:T(8,128)(2,1)S(1)}, u32[]{:S(2)}, u32[]{:S(2)}) %collective-permute-start.14) | collective-permute-done | bytes 786464 | tf_op jit(solution)/shard_map/ppermute | solution.py:40
  171.9 0.4 fusion.16
  172.6 1.9 %collective-permute-start.17 = (bf16[64,1536]{1,0:T(8,128)(2,1)S(1)}, bf16[64,1536]{1,0:T(8,128)(2,1)S(1)}, u32[]{:S(2)}, u32[]{:S(2)}) collective-permute-start(bf16[64,1536]{1,0:T(8,128)(2,1)S(1)} %get-tuple-element.22), channel_id=1, source_target_pairs={{0,1},{1,2},{2,3},{3,0},{4,5},{5,6},{6,7},{7,4},{8,9},{9,10},{10,1... | collective-permute-start | bytes 589832 | tf_op jit(solution)/shard_map/ppermute | solution.py:40
  174.5 12.1 %up_gradient.1 = bf16[1536,1536]{1,0:T(8,128)(2,1)} custom-call(bf16[512,1536]{1,0:T(8,128)(2,1)S(1)} %pad_maximum_fusion.mine, bf16[512,1536]{1,0:T(8,128)(2,1)S(1)} %collective-permute-done.13.theirs, bf16[256,1536]{1,0:T(8,128)(2,1)S(1)} %constant_dynamic-update-slice_fusion.4.p0, bf16[256,1536]{1,0:T(8,128)(2,1)S(1)} %collective-permute-done.23.p1, ...), custom_call_target="tpu_custom_call" | custom-call | flops 4831838208 | bytes 11010048 | tf_op jit(solution)/shard_map/up_gradient/pallas_call | solution.py:205
  186.6 0.8 fusion.15
  (47 shorter events, 0.8 us)
Async XLA Ops:
  0.6 8.6 %collective-permute-start = (bf16[64,1536]{1,0:T(8,128)(2,1)}, bf16[64,1536]{1,0:T(8,128)(2,1)S(1)}, u32[]{:S(2)}, u32[]{:S(2)}) collective-permute-start(bf16[64,1536]{1,0:T(8,128)(2,1)} %param.9), channel_id=1, source_target_pairs={{0,12},{1,13},{2,14},{3,15},{4,0},{5,1},{6,2},{7,3},{8,4},{9,5},{1... | collective-permute-start | bytes 589832 | tf_op jit(solution)/shard_map/ppermute | solution.py:40
  3.5 7.5 %collective-permute-start.1 = (bf16[64,1536]{1,0:T(8,128)(2,1)}, bf16[64,1536]{1,0:T(8,128)(2,1)S(1)}, u32[]{:S(2)}, u32[]{:S(2)}) collective-permute-start(bf16[64,1536]{1,0:T(8,128)(2,1)} %param.9), channel_id=1, source_target_pairs={{0,8},{1,9},{2,10},{3,11},{4,12},{5,13},{6,14},{7,15},{8,0},{9,1},... | collective-permute-start | bytes 589832 | tf_op jit(solution)/shard_map/ppermute | solution.py:40
  4.3 8.7 %collective-permute-start.2 = (bf16[64,1536]{1,0:T(8,128)(2,1)}, bf16[64,1536]{1,0:T(8,128)(2,1)S(1)}, u32[]{:S(2)}, u32[]{:S(2)}) collective-permute-start(bf16[64,1536]{1,0:T(8,128)(2,1)} %param.9), channel_id=1, source_target_pairs={{0,4},{1,5},{2,6},{3,7},{4,8},{5,9},{6,10},{7,11},{8,12},{9,13},{1... | collective-permute-start | bytes 589832 | tf_op jit(solution)/shard_map/ppermute | solution.py:40
  13.1 22.0 %collective-permute-start.3 = (bf16[256,1536]{1,0:T(8,128)(2,1)S(1)}, bf16[256,1536]{1,0:T(8,128)(2,1)S(1)}, u32[]{:S(2)}, u32[]{:S(2)}) collective-permute-start(bf16[256,1536]{1,0:T(8,128)(2,1)S(1)} %constant_dynamic-update-slice_fusion.p0), channel_id=1, source_target_pairs={{0,3},{1,0},{2,1},{3,2},{4,7},{5,4},{6,5},{7,6},{8,11},{9,8},{10,9... | collective-permute-start | bytes 2359304 | tf_op jit(solution)/shard_map/ppermute | solution.py:40
  17.2 17.9 %collective-permute-start.4 = (bf16[256,1536]{1,0:T(8,128)(2,1)S(1)}, bf16[256,1536]{1,0:T(8,128)(2,1)S(1)}, u32[]{:S(2)}, u32[]{:S(2)}) collective-permute-start(bf16[256,1536]{1,0:T(8,128)(2,1)S(1)} %constant_dynamic-update-slice_fusion.p0), channel_id=1, source_target_pairs={{0,2},{1,3},{2,0},{3,1},{4,6},{5,7},{6,4},{7,5},{8,10},{9,11},{10,... | collective-permute-start | bytes 2359304 | tf_op jit(solution)/shard_map/ppermute | solution.py:40
  17.2 21.6 %collective-permute-start.5 = (bf16[256,1536]{1,0:T(8,128)(2,1)S(1)}, bf16[256,1536]{1,0:T(8,128)(2,1)S(1)}, u32[]{:S(2)}, u32[]{:S(2)}) collective-permute-start(bf16[256,1536]{1,0:T(8,128)(2,1)S(1)} %constant_dynamic-update-slice_fusion.p0), channel_id=1, source_target_pairs={{0,1},{1,2},{2,3},{3,0},{4,5},{5,6},{6,7},{7,4},{8,9},{9,10},{10,1... | collective-permute-start | bytes 2359304 | tf_op jit(solution)/shard_map/ppermute | solution.py:40
  50.4 3.5 %collective-permute-start.6 = (bf16[512,1536]{1,0:T(8,128)(2,1)S(1)}, bf16[512,1536]{1,0:T(8,128)(2,1)S(1)}, u32[]{:S(2)}, u32[]{:S(2)}) collective-permute-start(bf16[512,1536]{1,0:T(8,128)(2,1)S(1)} %get-tuple-element.10), channel_id=1, source_target_pairs={{0,16},{16,0},{1,17},{17,1},{2,18},{18,2},{3,19},{19,3},{4,20},{20... | collective-permute-start | bytes 4718600 | tf_op jit(solution)/shard_map/ppermute | solution.py:48
  53.9 24.6 %copy-start = (bf16[128,1536]{1,0:T(8,128)(2,1)S(1)}, bf16[128,1536]{1,0:T(8,128)(2,1)}, u32[]{:S(2)}) copy-start(bf16[128,1536]{1,0:T(8,128)(2,1)} %param.8) | copy-start | bytes 1179652
  53.9 64.6 %slice-start = ((s8[4718592]{0:T(1024)(128)(4,1)}), s8[4194304]{0:T(1024)(128)(4,1)S(1)}, s32[]{:S(2)}) async-start(s8[4718592]{0:T(1024)(128)(4,1)} %bitcast.8), calls=%async_computation | async-start | bytes 8388608
  54.4 64.0 %slice-start.1 = ((s8[4718592]{0:T(1024)(128)(4,1)}), s8[524288]{0:T(1024)(128)(4,1)S(1)}, s32[]{:S(2)}) async-start(s8[4718592]{0:T(1024)(128)(4,1)} %bitcast.8), calls=%async_computation.1 | async-start | bytes 1048576
  54.6 20.2 %collective-permute-start.9 = (bf16[128,1536]{1,0:T(8,128)(2,1)S(1)}, bf16[128,1536]{1,0:T(8,128)(2,1)S(1)}, u32[]{:S(2)}, u32[]{:S(2)}) collective-permute-start(bf16[128,1536]{1,0:T(8,128)(2,1)S(1)} %get-tuple-element.20), channel_id=1, source_target_pairs={{0,96},{32,0},{64,32},{96,64},{1,97},{33,1},{65,33},{97,65},{2,98}... | collective-permute-start | bytes 1179656 | tf_op jit(solution)/shard_map/ppermute | solution.py:44
  57.6 17.1 %collective-permute-start.8 = (bf16[128,1536]{1,0:T(8,128)(2,1)S(1)}, bf16[128,1536]{1,0:T(8,128)(2,1)S(1)}, u32[]{:S(2)}, u32[]{:S(2)}) collective-permute-start(bf16[128,1536]{1,0:T(8,128)(2,1)S(1)} %get-tuple-element.21), channel_id=1, source_target_pairs={{0,64},{32,96},{64,0},{96,32},{1,65},{33,97},{65,1},{97,33},{2,66}... | collective-permute-start | bytes 1179656 | tf_op jit(solution)/shard_map/ppermute | solution.py:44
  58.3 20.2 %collective-permute-start.7 = (bf16[128,1536]{1,0:T(8,128)(2,1)S(1)}, bf16[128,1536]{1,0:T(8,128)(2,1)S(1)}, u32[]{:S(2)}, u32[]{:S(2)}) collective-permute-start(bf16[128,1536]{1,0:T(8,128)(2,1)S(1)} %get-tuple-element.19), channel_id=1, source_target_pairs={{0,32},{32,64},{64,96},{96,0},{1,33},{33,65},{65,97},{97,1},{2,34}... | collective-permute-start | bytes 1179656 | tf_op jit(solution)/shard_map/ppermute | solution.py:44
  78.4 23.3 %copy-start.2 = (bf16[64,1536]{1,0:T(8,128)(2,1)S(1)}, bf16[64,1536]{1,0:T(8,128)(2,1)}, u32[]{:S(2)}) copy-start(bf16[64,1536]{1,0:T(8,128)(2,1)} %param.7) | copy-start | bytes 589828
  79.0 21.7 %collective-permute-start.12 = (bf16[128,1536]{1,0:T(8,128)(2,1)S(1)}, bf16[128,1536]{1,0:T(8,128)(2,1)S(1)}, u32[]{:S(2)}, u32[]{:S(2)}) collective-permute-start(bf16[128,1536]{1,0:T(8,128)(2,1)S(1)} %get-tuple-element.26), channel_id=1, source_target_pairs={{0,32},{32,64},{64,96},{96,0},{1,33},{33,65},{65,97},{97,1},{2,34}... | collective-permute-start | bytes 1179656 | tf_op jit(solution)/shard_map/ppermute | solution.py:44
  79.1 21.6 %collective-permute-start.11 = (bf16[128,1536]{1,0:T(8,128)(2,1)S(1)}, bf16[128,1536]{1,0:T(8,128)(2,1)S(1)}, u32[]{:S(2)}, u32[]{:S(2)}) collective-permute-start(bf16[128,1536]{1,0:T(8,128)(2,1)S(1)} %get-tuple-element.26), channel_id=1, source_target_pairs={{0,64},{32,96},{64,0},{96,32},{1,65},{33,97},{65,1},{97,33},{2,66}... | collective-permute-start | bytes 1179656 | tf_op jit(solution)/shard_map/ppermute | solution.py:44
  81.1 20.4 %collective-permute-start.10 = (bf16[128,1536]{1,0:T(8,128)(2,1)S(1)}, bf16[128,1536]{1,0:T(8,128)(2,1)S(1)}, u32[]{:S(2)}, u32[]{:S(2)}) collective-permute-start(bf16[128,1536]{1,0:T(8,128)(2,1)S(1)} %get-tuple-element.26), channel_id=1, source_target_pairs={{0,96},{32,0},{64,32},{96,64},{1,97},{33,1},{65,33},{97,65},{2,98}... | collective-permute-start | bytes 1179656 | tf_op jit(solution)/shard_map/ppermute | solution.py:44
  82.3 36.1 %copy-start.1 = (s32[48,1536]{1,0:T(8,128)S(1)}, s32[48,1536]{1,0:T(8,128)}, u32[]{:S(2)}) copy-start(s32[48,1536]{1,0:T(8,128)} %param.11) | copy-start | bytes 884740
  82.3 34.2 %collective-permute-start.28 = (bf16[128,1536]{1,0:T(8,128)(2,1)S(1)}, bf16[128,1536]{1,0:T(8,128)(2,1)S(1)}, u32[]{:S(2)}, u32[]{:S(2)}) collective-permute-start(bf16[128,1536]{1,0:T(8,128)(2,1)S(1)} %get-tuple-element.25), channel_id=1, source_target_pairs={{0,32},{32,64},{64,96},{96,0},{1,33},{33,65},{65,97},{97,1},{2,34}... | collective-permute-start | bytes 1179656 | tf_op jit(solution)/shard_map/ppermute | solution.py:44
  83.1 34.2 %collective-permute-start.27 = (bf16[128,1536]{1,0:T(8,128)(2,1)S(1)}, bf16[128,1536]{1,0:T(8,128)(2,1)S(1)}, u32[]{:S(2)}, u32[]{:S(2)}) collective-permute-start(bf16[128,1536]{1,0:T(8,128)(2,1)S(1)} %get-tuple-element.25), channel_id=1, source_target_pairs={{0,64},{32,96},{64,0},{96,32},{1,65},{33,97},{65,1},{97,33},{2,66}... | collective-permute-start | bytes 1179656 | tf_op jit(solution)/shard_map/ppermute | solution.py:44
  100.7 17.4 %collective-permute-start.26 = (bf16[128,1536]{1,0:T(8,128)(2,1)S(1)}, bf16[128,1536]{1,0:T(8,128)(2,1)S(1)}, u32[]{:S(2)}, u32[]{:S(2)}) collective-permute-start(bf16[128,1536]{1,0:T(8,128)(2,1)S(1)} %get-tuple-element.25), channel_id=1, source_target_pairs={{0,96},{32,0},{64,32},{96,64},{1,97},{33,1},{65,33},{97,65},{2,98}... | collective-permute-start | bytes 1179656 | tf_op jit(solution)/shard_map/ppermute | solution.py:44
  101.7 17.8 %collective-permute-start.13 = (bf16[512,1536]{1,0:T(8,128)(2,1)S(1)}, bf16[512,1536]{1,0:T(8,128)(2,1)S(1)}, u32[]{:S(2)}, u32[]{:S(2)}) collective-permute-start(bf16[512,1536]{1,0:T(8,128)(2,1)S(1)} %pad_maximum_fusion.mine), channel_id=1, source_target_pairs={{0,16},{16,0},{1,17},{17,1},{2,18},{18,2},{3,19},{19,3},{4,20},{20... | collective-permute-start | bytes 4718600 | tf_op jit(solution)/shard_map/ppermute | solution.py:48
  101.8 17.7 %collective-permute-start.20 = (bf16[64,1536]{1,0:T(8,128)(2,1)S(1)}, bf16[64,1536]{1,0:T(8,128)(2,1)S(1)}, u32[]{:S(2)}, u32[]{:S(2)}) collective-permute-start(bf16[64,1536]{1,0:T(8,128)(2,1)S(1)} %copy-done.2), channel_id=1, source_target_pairs={{0,12},{1,13},{2,14},{3,15},{4,0},{5,1},{6,2},{7,3},{8,4},{9,5},{1... | collective-permute-start | bytes 589832 | tf_op jit(solution)/shard_map/ppermute | solution.py:40
  116.6 18.2 %collective-permute-start.21 = (bf16[64,1536]{1,0:T(8,128)(2,1)S(1)}, bf16[64,1536]{1,0:T(8,128)(2,1)S(1)}, u32[]{:S(2)}, u32[]{:S(2)}) collective-permute-start(bf16[64,1536]{1,0:T(8,128)(2,1)S(1)} %copy-done.2), channel_id=1, source_target_pairs={{0,8},{1,9},{2,10},{3,11},{4,12},{5,13},{6,14},{7,15},{8,0},{9,1},... | collective-permute-start | bytes 589832 | tf_op jit(solution)/shard_map/ppermute | solution.py:40
  117.4 17.4 %collective-permute-start.22 = (bf16[64,1536]{1,0:T(8,128)(2,1)S(1)}, bf16[64,1536]{1,0:T(8,128)(2,1)S(1)}, u32[]{:S(2)}, u32[]{:S(2)}) collective-permute-start(bf16[64,1536]{1,0:T(8,128)(2,1)S(1)} %copy-done.2), channel_id=1, source_target_pairs={{0,4},{1,5},{2,6},{3,7},{4,8},{5,9},{6,10},{7,11},{8,12},{9,13},{1... | collective-permute-start | bytes 589832 | tf_op jit(solution)/shard_map/ppermute | solution.py:40
  118.1 17.7 %collective-permute-start.29 = (bf16[512,1536]{1,0:T(8,128)(2,1)S(1)}, bf16[512,1536]{1,0:T(8,128)(2,1)S(1)}, u32[]{:S(2)}, u32[]{:S(2)}) collective-permute-start(bf16[512,1536]{1,0:T(8,128)(2,1)S(1)} %pad_maximum_fusion.1.mine), channel_id=1, source_target_pairs={{0,16},{16,0},{1,17},{17,1},{2,18},{18,2},{3,19},{19,3},{4,20},{20... | collective-permute-start | bytes 4718600 | tf_op jit(solution)/shard_map/ppermute | solution.py:48
  130.6 20.4 %collective-permute-start.16 = (bf16[256,1536]{1,0:T(8,128)(2,1)S(1)}, bf16[256,1536]{1,0:T(8,128)(2,1)S(1)}, u32[]{:S(2)}, u32[]{:S(2)}) collective-permute-start(bf16[256,1536]{1,0:T(8,128)(2,1)S(1)} %get-tuple-element.14), channel_id=1, source_target_pairs={{0,12},{1,13},{2,14},{3,15},{4,0},{5,1},{6,2},{7,3},{8,4},{9,5},{1... | collective-permute-start | bytes 2359304 | tf_op jit(solution)/shard_map/ppermute | solution.py:40
  133.2 21.2 %collective-permute-start.15 = (bf16[256,1536]{1,0:T(8,128)(2,1)S(1)}, bf16[256,1536]{1,0:T(8,128)(2,1)S(1)}, u32[]{:S(2)}, u32[]{:S(2)}) collective-permute-start(bf16[256,1536]{1,0:T(8,128)(2,1)S(1)} %get-tuple-element.13), channel_id=1, source_target_pairs={{0,8},{1,9},{2,10},{3,11},{4,12},{5,13},{6,14},{7,15},{8,0},{9,1},... | collective-permute-start | bytes 2359304 | tf_op jit(solution)/shard_map/ppermute | solution.py:40
  134.7 37.2 %collective-permute-start.14 = (bf16[256,1536]{1,0:T(8,128)(2,1)S(1)}, bf16[256,1536]{1,0:T(8,128)(2,1)S(1)}, u32[]{:S(2)}, u32[]{:S(2)}) collective-permute-start(bf16[256,1536]{1,0:T(8,128)(2,1)S(1)} %get-tuple-element.12), channel_id=1, source_target_pairs={{0,4},{1,5},{2,6},{3,7},{4,8},{5,9},{6,10},{7,11},{8,12},{9,13},{1... | collective-permute-start | bytes 2359304 | tf_op jit(solution)/shard_map/ppermute | solution.py:40
  134.8 37.7 %collective-permute-start.23 = (bf16[256,1536]{1,0:T(8,128)(2,1)S(1)}, bf16[256,1536]{1,0:T(8,128)(2,1)S(1)}, u32[]{:S(2)}, u32[]{:S(2)}) collective-permute-start(bf16[256,1536]{1,0:T(8,128)(2,1)S(1)} %constant_dynamic-update-slice_fusion.4.p0), channel_id=1, source_target_pairs={{0,3},{1,0},{2,1},{3,2},{4,7},{5,4},{6,5},{7,6},{8,11},{9,8},{10,9... | collective-permute-start | bytes 2359304 | tf_op jit(solution)/shard_map/ppermute | solution.py:40
  135.8 38.7 %collective-permute-start.24 = (bf16[256,1536]{1,0:T(8,128)(2,1)S(1)}, bf16[256,1536]{1,0:T(8,128)(2,1)S(1)}, u32[]{:S(2)}, u32[]{:S(2)}) collective-permute-start(bf16[256,1536]{1,0:T(8,128)(2,1)S(1)} %constant_dynamic-update-slice_fusion.4.p0), channel_id=1, source_target_pairs={{0,2},{1,3},{2,0},{3,1},{4,6},{5,7},{6,4},{7,5},{8,10},{9,11},{10,... | collective-permute-start | bytes 2359304 | tf_op jit(solution)/shard_map/ppermute | solution.py:40
  151.0 23.5 %collective-permute-start.25 = (bf16[256,1536]{1,0:T(8,128)(2,1)S(1)}, bf16[256,1536]{1,0:T(8,128)(2,1)S(1)}, u32[]{:S(2)}, u32[]{:S(2)}) collective-permute-start(bf16[256,1536]{1,0:T(8,128)(2,1)S(1)} %constant_dynamic-update-slice_fusion.4.p0), channel_id=1, source_target_pairs={{0,1},{1,2},{2,3},{3,0},{4,5},{5,6},{6,7},{7,4},{8,9},{9,10},{10,1... | collective-permute-start | bytes 2359304 | tf_op jit(solution)/shard_map/ppermute | solution.py:40
  172.4 14.2 %collective-permute-start.19 = (bf16[64,1536]{1,0:T(8,128)(2,1)S(1)}, bf16[64,1536]{1,0:T(8,128)(2,1)S(1)}, u32[]{:S(2)}, u32[]{:S(2)}) collective-permute-start(bf16[64,1536]{1,0:T(8,128)(2,1)S(1)} %get-tuple-element.23), channel_id=1, source_target_pairs={{0,3},{1,0},{2,1},{3,2},{4,7},{5,4},{6,5},{7,6},{8,11},{9,8},{10,9... | collective-permute-start | bytes 589832 | tf_op jit(solution)/shard_map/ppermute | solution.py:40
  172.4 14.2 %collective-permute-start.18 = (bf16[64,1536]{1,0:T(8,128)(2,1)S(1)}, bf16[64,1536]{1,0:T(8,128)(2,1)S(1)}, u32[]{:S(2)}, u32[]{:S(2)}) collective-permute-start(bf16[64,1536]{1,0:T(8,128)(2,1)S(1)} %get-tuple-element.24), channel_id=1, source_target_pairs={{0,2},{1,3},{2,0},{3,1},{4,6},{5,7},{6,4},{7,5},{8,10},{9,11},{10,... | collective-permute-start | bytes 589832 | tf_op jit(solution)/shard_map/ppermute | solution.py:40
  172.6 14.1 %collective-permute-start.17 = (bf16[64,1536]{1,0:T(8,128)(2,1)S(1)}, bf16[64,1536]{1,0:T(8,128)(2,1)S(1)}, u32[]{:S(2)}, u32[]{:S(2)}) collective-permute-start(bf16[64,1536]{1,0:T(8,128)(2,1)S(1)} %get-tuple-element.22), channel_id=1, source_target_pairs={{0,1},{1,2},{2,3},{3,0},{4,5},{5,6},{6,7},{7,4},{8,9},{9,10},{10,1... | collective-permute-start | bytes 589832 | tf_op jit(solution)/shard_map/ppermute | solution.py:40

commit v2 on v0

v2 whole, which is shorter than its diff:
```python
import jax
import jax.numpy as jnp
from jax import lax
from jax.experimental import pallas as pl
from jax.experimental.pallas import tpu as pltpu
from jax.sharding import Mesh
from jax.sharding import PartitionSpec as P

BF16, F32 = jnp.bfloat16, jnp.float32
TILE = 256


def dequantize(payload, scale):
    rows, cols = payload.shape
    blocks = payload.astype(F32).reshape(rows // 32, 32, cols)
    factor = jnp.exp2(scale.astype(F32))[:, None, :]
    return (blocks * factor).reshape(rows, cols).astype(BF16)


def gelu_terms(pre):
    values = pre.astype(F32)
    normal_cdf = 0.5 * (1.0 + jax.scipy.special.erf(values * 0.7071067811865476))
    activated = values * normal_cdf
    gelu_slope = normal_cdf + values * jnp.exp(-0.5 * values * values) * 0.3989422804014327
    return (activated, gelu_slope)


def shift_grid(first, step):
    pairs = []
    for k in range(2):
        for x in range(4):
            for z in range(4):
                along_x = (k == 0) == first
                to = (k, (x - step) % 4, z) if along_x else (k, x, (z - step) % 4)
                pairs.append((k * 16 + x * 4 + z, to[0] * 16 + to[1] * 4 + to[2]))
    return pairs


def from_grid(value, first, step):
    return lax.ppermute(value, ("k", "x", "z"), shift_grid(first, step))


def pair_y(value, step):
    pairs = []
    for y in range(4):
        for k in range(2):
            pairs.append((y * 2 + k, (y ^ (1 if (k == 0) == (step == 0) else 3)) * 2 + k))
    return lax.ppermute(value, ("y", "k"), pairs)


def pair_grid(value, step):
    pairs = []
    for k in range(2):
        for x in range(4):
            for z in range(4):
                flip = 3 if step % 2 else 1
                to = (x ^ flip, z) if (k == 0) == (step < 2) else (x, z ^ flip)
                pairs.append((k * 16 + x * 4 + z, k * 16 + to[0] * 4 + to[1]))
    return lax.ppermute(value, ("k", "x", "z"), pairs)


def swap_cores(value):
    return lax.ppermute(value, "k", [(0, 1), (1, 0)])


def gather_first(block):
    return jnp.concatenate([block] + [from_grid(block, True, step) for step in (1, 2, 3)])


def gather_second(stage):
    received = {step: from_grid(stage, False, step) for step in (2, 1, 3)}
    return [stage] + [received[step] for step in (1, 2, 3)]


def after(value, *others):
    return lax.optimization_barrier((value,) + others)[0]


FLIPS = (0, 1, 3, 2)


def place_of(x, z):
    k, y = lax.axis_index("k"), lax.axis_index("y")
    core, flip = z // 2, lax.bitwise_xor(x, y)
    near = jnp.where(core == 0, 3, 1)
    slot = jnp.where(flip == 0, 0, jnp.where(flip == 2, 3, jnp.where(flip == near, 1, 2)))
    return lax.rem(core + k, 2), slot * 2 + lax.rem(z, 2)


def grid_position(i, j):
    k, x, z = lax.axis_index("k"), lax.axis_index("x"), lax.axis_index("z")
    x = lax.rem(x + jnp.where(k == 0, i, j), 4)
    z = lax.rem(z + jnp.where(k == 0, j, i), 4)
    return x, z


def flipped_position(i, j):
    k, x, z = lax.axis_index("k"), lax.axis_index("x"), lax.axis_index("z")
    x = lax.bitwise_xor(x, jnp.where(k == 0, i, j))
    z = lax.bitwise_xor(z, jnp.where(k == 0, j, i))
    return x, z


NT = (((1,), (1,)), ((), ()))
TN = (((0,), (0,)), ((), ()))
WHOLE = pl.BlockSpec(memory_space=pltpu.VMEM)


def rows_at(start, count):
    return pl.ds(pl.multiple_of(start, 32), count)


def params(mib):
    return pltpu.CompilerParams(vmem_limit_bytes=mib * 1024 * 1024)


def cost(flops, moved):
    return pl.CostEstimate(flops=flops, bytes_accessed=moved, transcendentals=0)


def hidden_other_kernel(p0, p1, p2, p3, w, other, held):
    for j, piece in enumerate((p0, p1, p2, p3)):
        for i in range(4):
            half, place = place_of(*grid_position(i, j))
            held[rows_at(half * 512 + place * 64, 64)] = piece[i * 64 : (i + 1) * 64]

    @pl.loop(0, w.shape[0] // TILE, unroll=True)
    def _(n):
        columns = pl.ds(pl.multiple_of(n * TILE, TILE), TILE)
        out = lax.dot_general(held[512:], w[columns], NT, preferred_element_type=F32)
        other[:, columns] = out.astype(BF16)


def hidden_other(pieces, weight):
    n, depth = weight.shape
    return pl.pallas_call(
        hidden_other_kernel,
        out_shape=[jax.ShapeDtypeStruct((512, n), BF16), jax.ShapeDtypeStruct((1024, depth), BF16)],
        in_specs=[WHOLE] * 5,
        out_specs=[WHOLE] * 2,
        compiler_params=params(24),
        cost_estimate=cost(2 * 512 * n * depth, 2 * (1024 + n) * depth + 2 * 512 * n),
        name="hidden_other",
    )(*pieces, weight)


def hidden_own_kernel(held, w, own):
    @pl.loop(0, w.shape[0] // TILE, unroll=True)
    def _(n):
        columns = pl.ds(pl.multiple_of(n * TILE, TILE), TILE)
        own[:, columns] = lax.dot_general(held[:512], w[columns], NT, preferred_element_type=F32)


def hidden_own(ordered, weight):
    n, depth = weight.shape
    return pl.pallas_call(
        hidden_own_kernel,
        out_shape=jax.ShapeDtypeStruct((512, n), F32),
        in_specs=[WHOLE] * 2,
        out_specs=WHOLE,
        compiler_params=params(24),
        cost_estimate=cost(2 * 512 * n * depth, 2 * (1024 + n) * depth + 4 * 512 * n),
        name="hidden_own",
    )(ordered, weight)


def input_own_kernel(mine, w, own):
    @pl.loop(0, w.shape[0] // TILE, unroll=True)
    def _(n):
        columns = pl.ds(pl.multiple_of(n * TILE, TILE), TILE)
        own[:, columns] = lax.dot_general(mine[...], w[columns], NT, preferred_element_type=F32)


def input_own(mine, weight):
    n, depth = weight.shape
    return pl.pallas_call(
        input_own_kernel,
        out_shape=jax.ShapeDtypeStruct((512, n), F32),
        in_specs=[WHOLE] * 2,
        out_specs=WHOLE,
        compiler_params=params(24),
        cost_estimate=cost(2 * 512 * n * depth, 2 * (512 + n) * depth + 4 * 512 * n),
        name="input_own",
    )(mine, weight)


def input_all_kernel(theirs, w, own, o0, o1, o2, o3, both):
    @pl.loop(0, w.shape[0] // TILE, unroll=True)
    def _(n):
        columns = pl.ds(pl.multiple_of(n * TILE, TILE), TILE)
        both[:512] = own[:, columns]
        both[512:] = lax.dot_general(theirs[...], w[columns], NT, preferred_element_type=F32)
        for i, part in enumerate((o0, o1, o2, o3)):
            for j in range(4):
                half, place = place_of(*grid_position(i, j))
                part[pl.ds(j * 64, 64), columns] = both[rows_at(half * 512 + place * 64, 64)].astype(part.dtype)


def input_all(theirs, weight, own):
    n, depth = weight.shape
    return pl.pallas_call(
        input_all_kernel,
        out_shape=[jax.ShapeDtypeStruct((256, n), F32)] + [jax.ShapeDtypeStruct((256, n), BF16)] * 3,
        in_specs=[WHOLE] * 3,
        out_specs=[WHOLE] * 4,
        scratch_shapes=[pltpu.VMEM((1024, TILE), F32)],
        compiler_params=params(28),
        cost_estimate=cost(2 * 512 * n * depth, 2 * (512 + n) * depth + 4 * 1024 * n),
        name="input_all",
    )(theirs, weight, own)


def down_kernel(*refs):
    acts, (grad, out) = refs[:-2], refs[-2:]
    columns = pl.ds(pl.multiple_of(pl.program_id(0) * TILE, TILE), TILE)
    total, at = None, 0
    for act in acts:
        rows = slice(at, at + act.shape[0])
        part = lax.dot_general(act[:, columns], grad[rows], TN, preferred_element_type=F32)
        total = part if total is None else total + part
        at += act.shape[0]
    out[...] = total.astype(BF16)


def down_gradient(acts, grad):
    m, n = acts[0].shape[1], grad.shape[1]
    return pl.pallas_call(
        down_kernel,
        grid=(m // TILE,),
        out_shape=jax.ShapeDtypeStruct((m, n), BF16),
        in_specs=[WHOLE] * (len(acts) + 1),
        out_specs=pl.BlockSpec((TILE, n), lambda i: (i, 0)),
        compiler_params=params(24),
        cost_estimate=cost(2 * 1024 * n * m, 2 * 1024 * (n + m) + 2 * n * m),
        name="down_gradient",
    )(*acts, grad)


def up_kernel(mine, theirs, *rest):
    blocks, (out, held) = rest[:-2], rest[-2:]

    @pl.when(pl.program_id(0) == 0)
    def _():
        at = 0
        for block in blocks:
            for row in range(0, block.shape[0], 64):
                half, place = place_of(*flipped_position(FLIPS[at % 4], FLIPS[at // 4]))
                held[rows_at(half * 512 + place * 64, 64)] = block[row : row + 64]
                at += 1

    columns = pl.ds(pl.multiple_of(pl.program_id(0) * TILE, TILE), TILE)
    total = lax.dot_general(held[:512, columns], mine[...], TN, preferred_element_type=F32)
    total += lax.dot_general(held[512:, columns], theirs[...], TN, preferred_element_type=F32)
    out[...] = total.astype(BF16)


def up_gradient(mine, theirs, blocks):
    m, n = blocks[0].shape[1], mine.shape[1]
    return pl.pallas_call(
        up_kernel,
        grid=(m // TILE,),
        out_shape=jax.ShapeDtypeStruct((m, n), BF16),
        in_specs=[WHOLE] * (2 + len(blocks)),
        out_specs=pl.BlockSpec((TILE, n), lambda i: (i, 0)),
        scratch_shapes=[pltpu.VMEM((1024, m), BF16)],
        compiler_params=params(24),
        cost_estimate=cost(2 * 1024 * n * m, 2 * 1024 * (n + m) + 2 * n * m),
        name="up_gradient",
    )(mine, theirs, *blocks)


def together(*values):
    return lax.optimization_barrier(values)


def scatter_first(parts):
    rest = parts[0]
    received = {step: from_grid(parts[step], True, -step) for step in (2, 1, 3)}
    for step in (1, 2, 3):
        rest = rest + received[step].astype(F32)
    return rest


def scatter_second(rest):
    total, received = rest[:64], {}
    for step in (2, 1, 3):
        received[step] = from_grid(rest[step * 64 : (step + 1) * 64].astype(BF16), False, -step)
    for step in (1, 2, 3):
        total = total + received[step].astype(F32)
    return total.astype(BF16)


def per_device(inputs, pre_act, out_grad, up_payload, up_scale, down_payload, down_scale):
    down_weight = dequantize(down_payload, down_scale)
    up_weight = dequantize(up_payload, up_scale)
    activated, gelu_slope = gelu_terms(pre_act)
    activated = activated.astype(BF16)

    stage = gather_first(out_grad)
    pieces = gather_second(stage)
    act0, inputs = after(activated, stage), after(inputs, stage)
    act1 = pair_y(act0, 1)
    act2, act3 = pair_y(act0, 0), pair_y(act1, 0)
    in0 = jnp.concatenate([inputs, pair_grid(inputs, 0)])
    pieces[1], in0, act1, act2, act3, up_weight = together(pieces[1], in0, act1, act2, act3, up_weight)
    other, ordered = hidden_other(pieces, down_weight)
    chip = hidden_own(ordered, down_weight) + swap_cores(other).astype(F32)
    onward = chip[128:256] + pair_y(chip[384:].astype(BF16), 0).astype(F32)
    in0 = after(in0, chip)
    onward, in2, in1 = together(onward, pair_grid(in0, 2), pair_grid(in0, 1))
    hidden_grad = chip[:128] + pair_y(chip[256:384].astype(BF16), 0).astype(F32)
    hidden_grad = hidden_grad + pair_y(onward.astype(BF16), 1).astype(F32)
    hidden_grad, in3, in4 = together(hidden_grad, pair_grid(in1, 2), pair_grid(after(in0, onward), 3))
    gated = (gelu_slope * hidden_grad).astype(BF16)
    near, in5 = together(pair_y(gated, 1), pair_grid(after(in1, hidden_grad), 3))
    act = jnp.concatenate([act0, act1, act2, act3])
    mine = jnp.concatenate([gated, near, pair_y(gated, 0), pair_y(near, 0)])
    mine, in6, act_theirs = together(mine, pair_grid(after(in2, near), 3), swap_cores(act))
    theirs = swap_cores(mine)
    parts = list(input_all(theirs, up_weight, input_own(mine, up_weight)))
    parts[0], in7 = together(parts[0], pair_grid(after(in3, mine), 3))
    rest = scatter_first(parts)

    up_grad = up_gradient(mine, theirs, [in0, in1, in2, in3, in4, in5, in6, in7])
    rest, up_grad = together(rest, up_grad)
    down_grad = down_gradient([act, act_theirs], ordered)
    return (scatter_second(rest), up_grad, down_grad)


def solution(mesh):
    grid = Mesh(mesh.devices.reshape(4, 2, 4, 4), ("y", "k", "x", "z"))
    tokens, hidden = P(("x", "z"), ("y", "k")), P(("y", "k"), ("x", "z"))
    return jax.shard_map(
        per_device,
        mesh=grid,
        in_specs=(tokens, hidden, tokens, hidden, hidden, tokens, tokens),
        out_specs=(tokens, hidden, tokens),
        check_vma=False,
    )
```

time: 324 us -> 134 us (0.41)
  waiting for transfers between devices: 248 us -> 56.4 us
  starting transfers between devices: 0.42 us -> 41.2 us
  matrix products: 36.8 us -> 0 us
  Pallas kernels: 0 us -> 25.9 us
  between operations: 14.1 us -> 0.94 us
  other arithmetic: 16 us -> 7.93 us
  local copies, waits for them, and re-layouts: 8.02 us -> 1.5 us
    all_gather x4 -> x0, waiting for transfers between devices: 129 us -> none  [the longest x1 46.4 us: per_device(): lax.all_gather(out_grad, 'col', axis=0, tiled=True)]
    reduce_scatter x2 -> x0, waiting for transfers between devices: 117 us -> none  [the longest x1 77.2 us: per_device(): lax.psum_scatter(input_terms, 'col', scatter_dimension=0, tiled=True)]
    ppermute x0 -> x32, waiting for transfers between devices: none -> 56.4 us  [the longest x9 26.7 us: pair_y(): return lax.ppermute(value, ('y', 'k'), pairs)]
    ppermute x0 -> x32, starting transfers between devices: none -> 41.2 us  [the longest x12 18.9 us: from_grid(): return lax.ppermute(value, ('k', 'x', 'z'), shift_grid(first, step))]
    dot_general x4 -> x0, matrix products: 36.8 us -> none  [contract(): lax.dot_general(left, right, (((left_dim,), (right_dim,)), ((), ())), pre...]
    pallas_call x0 -> x6, Pallas kernels: none -> 25.9 us  [the longest x1 7.35 us: up_gradient(): pl.pallas_call(up_kernel, grid=(m // TILE,), out_shape=jax.ShapeDtypeStru...]
    convert_element_type x4 -> x5, other arithmetic: 14.9 us -> 6.52 us  [the longest x2 4.24 us: dequantize(): return (blocks * factor).reshape(rows, cols).astype(BF16)]
    unnamed x10 -> x18, local copies, waits for them, and re-layouts: 8.02 us -> 1.36 us
  transfers between devices with their start and end apart: 6 -> 32, of which waited for: 6 -> 17; matrix products, arithmetic and copies ran while one was open for 14% -> 5% of each run, Pallas kernels for 0% -> 17%
where the time goes in v2:
time: 134 us
  waiting for transfers between devices  56.4 us (42%)
  starting transfers between devices  41.2 us (31%)
  Pallas kernels  25.9 us (19%)
  other arithmetic  7.93 us (6%)
  local copies, waits for them, and re-layouts  1.5 us (1%)
    ppermute x9, waiting for transfers between devices, pair_y(): return lax.ppermute(value, ('y', 'k'), pairs)  26.7 us
    ppermute x12, starting transfers between devices, from_grid(): return lax.ppermute(value, ('k', 'x', 'z'), shift_grid(first, step))  18.9 us
    ppermute x12, waiting for transfers between devices, from_grid(): return lax.ppermute(value, ('k', 'x', 'z'), shift_grid(first, step))  15.7 us
    ppermute x9, starting transfers between devices, pair_y(): return lax.ppermute(value, ('y', 'k'), pairs)  13.3 us
    ppermute x8, waiting for transfers between devices, pair_grid(): return lax.ppermute(value, ('k', 'x', 'z'), pairs)  13.2 us
    ppermute x8, starting transfers between devices, pair_grid(): return lax.ppermute(value, ('k', 'x', 'z'), pairs)  8.84 us
    pallas_call x1, Pallas kernels, up_gradient(): pl.pallas_call(up_kernel, grid=(m // TILE,), out_shape=jax.ShapeDtypeStru...  7.35 us
    pallas_call x1, Pallas kernels, down_gradient(): pl.pallas_call(down_kernel, grid=(m // TILE,), out_shape=jax.ShapeDtypeSt...  6.97 us
  transfers between devices with their start and end apart: 32, of which 17 were waited for; matrix products, arithmetic and copies ran while one was open for 5% of the time, Pallas kernels for 17%

profile of v2, /device:TPU:0, one launch (start us, length us, event | category | flops | bytes accessed | tf_op | source)
XLA Modules:
  0.0 133.8 jit_solution(17226661159832428443)
XLA Ops:
  0.7 3.2 %collective-permute-start.1 = (bf16[64,1536]{1,0:T(8,128)(2,1)}, bf16[64,1536]{1,0:T(8,128)(2,1)S(1)}, u32[]{:S(2)}, u32[]{:S(2)}) collective-permute-start(bf16[64,1536]{1,0:T(8,128)(2,1)} %param.9), channel_id=1, source_target_pairs={{0,8},{1,9},{2,10},{3,11},{4,12},{5,13},{6,14},{7,15},{8,0},{9,1},... | collective-permute-start | bytes 589832 | tf_op jit(solution)/shard_map/ppermute | solution.py:40
  3.8 1.1 collective-permute-start
  5.0 0.9 collective-permute-start.2
  5.9 1.2 fusion.10
  7.0 0.9 constant_dynamic-update-slice_fusion.3
  8.0 2.4 %collective-permute-done = bf16[64,1536]{1,0:T(8,128)(2,1)S(1)} collective-permute-done((bf16[64,1536]{1,0:T(8,128)(2,1)}, bf16[64,1536]{1,0:T(8,128)(2,1)S(1)}, u32[]{:S(2)}, u32[]{:S(2)}) %collective-permute-start) | collective-permute-done | bytes 196640 | tf_op jit(solution)/shard_map/ppermute | solution.py:40
  10.5 1.6 %collective-permute-done.2 = bf16[64,1536]{1,0:T(8,128)(2,1)S(1)} collective-permute-done((bf16[64,1536]{1,0:T(8,128)(2,1)}, bf16[64,1536]{1,0:T(8,128)(2,1)S(1)}, u32[]{:S(2)}, u32[]{:S(2)}) %collective-permute-start.2) | collective-permute-done | bytes 196640 | tf_op jit(solution)/shard_map/ppermute | solution.py:40
  12.1 2.0 %collective-permute-start.9 = (bf16[256,1536]{1,0:T(8,128)(2,1)S(1)}, bf16[256,1536]{1,0:T(8,128)(2,1)S(1)}, u32[]{:S(2)}, u32[]{:S(2)}) collective-permute-start(bf16[256,1536]{1,0:T(8,128)(2,1)S(1)} %constant_dynamic-update-slice_fusion.p0), channel_id=1, source_target_pairs={{0,1},{1,2},{2,3},{3,0},{4,5},{5,6},{6,7},{7,4},{8,9},{9,10},{10,1... | collective-permute-start | bytes 2359304 | tf_op jit(solution)/shard_map/ppermute | solution.py:40
  14.1 3.6 %collective-permute-start.8 = (bf16[256,1536]{1,0:T(8,128)(2,1)S(1)}, bf16[256,1536]{1,0:T(8,128)(2,1)S(1)}, u32[]{:S(2)}, u32[]{:S(2)}) collective-permute-start(bf16[256,1536]{1,0:T(8,128)(2,1)S(1)} %constant_dynamic-update-slice_fusion.p0), channel_id=1, source_target_pairs={{0,2},{1,3},{2,0},{3,1},{4,6},{5,7},{6,4},{7,5},{8,10},{9,11},{10,... | collective-permute-start | bytes 2359304 | tf_op jit(solution)/shard_map/ppermute | solution.py:40
  17.7 1.0 collective-permute-start.3
  18.7 3.0 %collective-permute-start.5 = (bf16[128,1536]{1,0:T(8,128)(2,1)S(1)}, bf16[128,1536]{1,0:T(8,128)(2,1)S(1)}, u32[]{:S(2)}, u32[]{:S(2)}) collective-permute-start(bf16[128,1536]{1,0:T(8,128)(2,1)S(1)} %fusion.10), channel_id=1, source_target_pairs={{0,96},{16,48},{32,64},{48,16},{64,32},{80,112},{96,0},{112,80},{1... | collective-permute-start | bytes 1179656 | tf_op jit(solution)/shard_map/ppermute | solution.py:48
  21.8 4.8 %collective-permute-done.4 = bf16[64,1536]{1,0:T(8,128)(2,1)S(1)} collective-permute-done((bf16[64,1536]{1,0:T(8,128)(2,1)S(1)}, bf16[64,1536]{1,0:T(8,128)(2,1)S(1)}, u32[]{:S(2)}, u32[]{:S(2)}) %collective-permute-start.4) | collective-permute-done | bytes 196640 | tf_op jit(solution)/shard_map/ppermute | solution.py:59
  26.5 1.6 %collective-permute-start.6 = (bf16[128,1536]{1,0:T(8,128)(2,1)S(1)}, bf16[128,1536]{1,0:T(8,128)(2,1)S(1)}, u32[]{:S(2)}, u32[]{:S(2)}) collective-permute-start(bf16[128,1536]{1,0:T(8,128)(2,1)S(1)} %fusion.10), channel_id=1, source_target_pairs={{0,32},{16,112},{32,0},{48,80},{64,96},{80,48},{96,64},{112,16},{1... | collective-permute-start | bytes 1179656 | tf_op jit(solution)/shard_map/ppermute | solution.py:48
  28.1 1.4 %collective-permute-done.5 = bf16[128,1536]{1,0:T(8,128)(2,1)S(1)} collective-permute-done((bf16[128,1536]{1,0:T(8,128)(2,1)S(1)}, bf16[128,1536]{1,0:T(8,128)(2,1)S(1)}, u32[]{:S(2)}, u32[]{:S(2)}) %collective-permute-start.5) | collective-permute-done | bytes 393248 | tf_op jit(solution)/shard_map/ppermute | solution.py:48
  29.9 3.4 %fusion.w = bf16[1536,1536]{1,0:T(8,128)(2,1)S(1)} fusion(bf16[1536,1536]{1,0:T(8,128)(2,1)} %param.12, f32[48,1536]{1,0:T(8,128)S(1)} %multiply_exponential_fusion), kind=kLoop, calls=%fused_computation.1 | loop fusion | flops 7077888 | bytes 9732096 | tf_op jit(solution)/shard_map/convert_element_type | solution.py:17
  33.6 0.9 fusion.1.w
  34.5 4.0 %collective-permute-done.7 = bf16[128,1536]{1,0:T(8,128)(2,1)S(1)} collective-permute-done((bf16[128,1536]{1,0:T(8,128)(2,1)S(1)}, bf16[128,1536]{1,0:T(8,128)(2,1)S(1)}, u32[]{:S(2)}, u32[]{:S(2)}) %collective-permute-start.7) | collective-permute-done | bytes 393248 | tf_op jit(solution)/shard_map/ppermute | solution.py:48
  38.5 2.9 %hidden_other.1 = (bf16[512,1536]{1,0:T(8,128)(2,1)S(1)}, bf16[1024,1536]{1,0:T(8,128)(2,1)S(1)}) custom-call(bf16[256,1536]{1,0:T(8,128)(2,1)S(1)} %constant_dynamic-update-slice_fusion.p0, bf16[256,1536]{1,0:T(8,128)(2,1)S(1)} %collective-permute-done.3.p1, bf16[256,1536]{1,0:T(8,128)(2,1)S(1)} %collective-permute-done.8.p2, ...), custom_call_target="tpu_custom_call" | custom-call | flops 2415919104 | bytes 9437184 | tf_op jit(solution)/shard_map/hidden_other/pallas_call | solution.py:136
  41.5 2.6 %hidden_own.1 = f32[512,1536]{1,0:T(8,128)S(1)} custom-call(bf16[1024,1536]{1,0:T(8,128)(2,1)S(1)} %get-tuple-element.40.held.refs_2_, bf16[1536,1536]{1,0:T(8,128)(2,1)S(1)} %fusion.w), custom_call_target="tpu_custom_call" | custom-call | flops 2415919104 | bytes 11010048 | tf_op jit(solution)/shard_map/hidden_own/pallas_call | solution.py:156
  44.1 0.8 collective-permute-done.10
  44.9 0.6 fusion.12
  45.5 1.7 %collective-permute-start.12 = (bf16[128,1536]{1,0:T(8,128)(2,1)S(1)}, bf16[128,1536]{1,0:T(8,128)(2,1)S(1)}, u32[]{:S(2)}, u32[]{:S(2)}) collective-permute-start(bf16[128,1536]{1,0:T(8,128)(2,1)S(1)} %get-tuple-element.74), channel_id=1, source_target_pairs={{0,32},{16,112},{32,0},{48,80},{64,96},{80,48},{96,64},{112,16},{1... | collective-permute-start | bytes 1179656 | tf_op jit(solution)/shard_map/ppermute | solution.py:48
  47.3 1.8 %collective-permute-start.14 = (bf16[128,1536]{1,0:T(8,128)(2,1)S(1)}, bf16[128,1536]{1,0:T(8,128)(2,1)S(1)}, u32[]{:S(2)}, u32[]{:S(2)}) collective-permute-start(bf16[128,1536]{1,0:T(8,128)(2,1)S(1)} %pad_maximum_fusion.1.rest_0_), channel_id=1, source_target_pairs={{0,12},{1,13},{2,14},{3,15},{4,8},{5,9},{6,10},{7,11},{8,4},{9,5},... | collective-permute-start | bytes 1179656 | tf_op jit(solution)/shard_map/ppermute | solution.py:59
  49.4 1.3 %collective-permute-start.11 = (bf16[128,1536]{1,0:T(8,128)(2,1)S(1)}, bf16[128,1536]{1,0:T(8,128)(2,1)S(1)}, u32[]{:S(2)}, u32[]{:S(2)}) collective-permute-start(bf16[128,1536]{1,0:T(8,128)(2,1)S(1)} %get-tuple-element.73), channel_id=1, source_target_pairs={{0,32},{16,112},{32,0},{48,80},{64,96},{80,48},{96,64},{112,16},{1... | collective-permute-start | bytes 1179656 | tf_op jit(solution)/shard_map/ppermute | solution.py:48
  50.8 2.6 %collective-permute-done.12 = bf16[128,1536]{1,0:T(8,128)(2,1)S(1)} collective-permute-done((bf16[128,1536]{1,0:T(8,128)(2,1)S(1)}, bf16[128,1536]{1,0:T(8,128)(2,1)S(1)}, u32[]{:S(2)}, u32[]{:S(2)}) %collective-permute-start.12) | collective-permute-done | bytes 393248 | tf_op jit(solution)/shard_map/ppermute | solution.py:48
  53.5 2.9 %collective-permute-done.14.rest_1_ = bf16[128,1536]{1,0:T(8,128)(2,1)S(1)} collective-permute-done((bf16[128,1536]{1,0:T(8,128)(2,1)S(1)}, bf16[128,1536]{1,0:T(8,128)(2,1)S(1)}, u32[]{:S(2)}, u32[]{:S(2)}) %collective-permute-start.14) | collective-permute-done | bytes 393248 | tf_op jit(solution)/shard_map/ppermute | solution.py:59
  56.9 2.7 %collective-permute-start.15 = (bf16[128,1536]{1,0:T(8,128)(2,1)S(1)}, bf16[128,1536]{1,0:T(8,128)(2,1)S(1)}, u32[]{:S(2)}, u32[]{:S(2)}) collective-permute-start(bf16[128,1536]{1,0:T(8,128)(2,1)S(1)} %slice_add_fusion), channel_id=1, source_target_pairs={{0,96},{16,48},{32,64},{48,16},{64,32},{80,112},{96,0},{112,80},{1... | collective-permute-start | bytes 1179656 | tf_op jit(solution)/shard_map/ppermute | solution.py:48
  60.1 5.8 %collective-permute-done.15 = bf16[128,1536]{1,0:T(8,128)(2,1)S(1)} collective-permute-done((bf16[128,1536]{1,0:T(8,128)(2,1)S(1)}, bf16[128,1536]{1,0:T(8,128)(2,1)S(1)}, u32[]{:S(2)}, u32[]{:S(2)}) %collective-permute-start.15) | collective-permute-done | bytes 393248 | tf_op jit(solution)/shard_map/ppermute | solution.py:48
  66.0 2.8 %collective-permute-done.17.rest_4_ = bf16[128,1536]{1,0:T(8,128)(2,1)S(1)} collective-permute-done((bf16[128,1536]{1,0:T(8,128)(2,1)S(1)}, bf16[128,1536]{1,0:T(8,128)(2,1)S(1)}, u32[]{:S(2)}, u32[]{:S(2)}) %collective-permute-start.17) | collective-permute-done | bytes 393248 | tf_op jit(solution)/shard_map/ppermute | solution.py:59
  69.1 0.6 collective-permute-start.18
  69.8 2.0 %collective-permute-start.19 = (bf16[128,1536]{1,0:T(8,128)(2,1)S(1)}, bf16[128,1536]{1,0:T(8,128)(2,1)S(1)}, u32[]{:S(2)}, u32[]{:S(2)}) collective-permute-start(bf16[128,1536]{1,0:T(8,128)(2,1)S(1)} %collective-permute-done.14.rest_1_), channel_id=1, source_target_pairs={{0,3},{1,2},{2,1},{3,0},{4,7},{5,6},{6,5},{7,4},{8,11},{9,10},{10,... | collective-permute-start | bytes 1179656 | tf_op jit(solution)/shard_map/ppermute | solution.py:59
  71.8 0.9 collective-permute-start.20
  72.7 8.5 %collective-permute-done.18 = bf16[128,1536]{1,0:T(8,128)(2,1)S(1)} collective-permute-done((bf16[128,1536]{1,0:T(8,128)(2,1)S(1)}, bf16[128,1536]{1,0:T(8,128)(2,1)S(1)}, u32[]{:S(2)}, u32[]{:S(2)}) %collective-permute-start.18) | collective-permute-done | bytes 393248 | tf_op jit(solution)/shard_map/ppermute | solution.py:48
  81.2 1.1 collective-permute-start.21
  82.3 2.1 %collective-permute-start.22 = (bf16[128,1536]{1,0:T(8,128)(2,1)S(1)}, bf16[128,1536]{1,0:T(8,128)(2,1)S(1)}, u32[]{:S(2)}, u32[]{:S(2)}) collective-permute-start(bf16[128,1536]{1,0:T(8,128)(2,1)S(1)} %collective-permute-done.13.rest_2_), channel_id=1, source_target_pairs={{0,3},{1,2},{2,1},{3,0},{4,7},{5,6},{6,5},{7,4},{8,11},{9,10},{10,... | collective-permute-start | bytes 1179656 | tf_op jit(solution)/shard_map/ppermute | solution.py:59
  84.5 4.5 %collective-permute-done.21 = bf16[128,1536]{1,0:T(8,128)(2,1)S(1)} collective-permute-done((bf16[128,1536]{1,0:T(8,128)(2,1)S(1)}, bf16[128,1536]{1,0:T(8,128)(2,1)S(1)}, u32[]{:S(2)}, u32[]{:S(2)}) %collective-permute-start.21) | collective-permute-done | bytes 393248 | tf_op jit(solution)/shard_map/ppermute | solution.py:48
  89.1 2.2 %collective-permute-done.22.rest_6_ = bf16[128,1536]{1,0:T(8,128)(2,1)S(1)} collective-permute-done((bf16[128,1536]{1,0:T(8,128)(2,1)S(1)}, bf16[128,1536]{1,0:T(8,128)(2,1)S(1)}, u32[]{:S(2)}, u32[]{:S(2)}) %collective-permute-start.22) | collective-permute-done | bytes 393248 | tf_op jit(solution)/shard_map/ppermute | solution.py:59
  91.3 2.1 %collective-permute-start.25 = (bf16[128,1536]{1,0:T(8,128)(2,1)S(1)}, bf16[128,1536]{1,0:T(8,128)(2,1)S(1)}, u32[]{:S(2)}, u32[]{:S(2)}) collective-permute-start(bf16[128,1536]{1,0:T(8,128)(2,1)S(1)} %collective-permute-done.16.rest_3_), channel_id=1, source_target_pairs={{0,3},{1,2},{2,1},{3,0},{4,7},{5,6},{6,5},{7,4},{8,11},{9,10},{10,... | collective-permute-start | bytes 1179656 | tf_op jit(solution)/shard_map/ppermute | solution.py:59
  93.4 2.6 %input_own.1.own = f32[512,1536]{1,0:T(8,128)S(1)} custom-call(bf16[512,1536]{1,0:T(8,128)(2,1)S(1)} %pad_maximum_fusion.mine, bf16[1536,1536]{1,0:T(8,128)(2,1)S(1)} %fusion.1.w), custom_call_target="tpu_custom_call" | custom-call | flops 2415919104 | bytes 9437184 | tf_op jit(solution)/shard_map/input_own/pallas_call | solution.py:176
  96.1 3.4 %input_all.1 = (f32[256,1536]{1,0:T(8,128)S(1)}, bf16[256,1536]{1,0:T(8,128)(2,1)S(1)}, bf16[256,1536]{1,0:T(8,128)(2,1)S(1)}, bf16[256,1536]{1,0:T(8,128)(2,1)S(1)}) custom-call(bf16[512,1536]{1,0:T(8,128)(2,1)S(1)} %collective-permute-done.24.theirs, bf16[1536,1536]{1,0:T(8,128)(2,1)S(1)} %fusion.1.w, f32[512,1536]{1,0:T(8,128)S(1)} %input_own.1.own), custom_call_target="tpu_custom_call" | custom-call | flops 2415919104 | bytes 12582912 | tf_op jit(solution)/shard_map/input_all/pallas_call | solution.py:201
  99.9 2.5 %collective-permute-start.27 = (bf16[256,1536]{1,0:T(8,128)(2,1)S(1)}, bf16[256,1536]{1,0:T(8,128)(2,1)S(1)}, u32[]{:S(2)}, u32[]{:S(2)}) collective-permute-start(bf16[256,1536]{1,0:T(8,128)(2,1)S(1)} %get-tuple-element.62), channel_id=1, source_target_pairs={{0,8},{1,9},{2,10},{3,11},{4,12},{5,13},{6,14},{7,15},{8,0},{9,1},... | collective-permute-start | bytes 2359304 | tf_op jit(solution)/shard_map/ppermute | solution.py:40
  102.5 0.8 collective-permute-start.28
  103.3 7.4 %up_gradient.1 = bf16[1536,1536]{1,0:T(8,128)(2,1)} custom-call(bf16[512,1536]{1,0:T(8,128)(2,1)S(1)} %pad_maximum_fusion.mine, bf16[512,1536]{1,0:T(8,128)(2,1)S(1)} %collective-permute-done.24.theirs, bf16[128,1536]{1,0:T(8,128)(2,1)S(1)} %pad_maximum_fusion.1.rest_0_, bf16[128,1536]{1,0:T(8,128)(2,1)S(1)} %collective-permute-done.14.rest_1_, ...), custom_call_target="tpu_custom_call" | custom-call | flops 4831838208 | bytes 11010048 | tf_op jit(solution)/shard_map/up_gradient/pallas_call | solution.py:259
  110.7 10.5 %collective-permute-done.26 = bf16[256,1536]{1,0:T(8,128)(2,1)S(1)} collective-permute-done((bf16[256,1536]{1,0:T(8,128)(2,1)S(1)}, bf16[256,1536]{1,0:T(8,128)(2,1)S(1)}, u32[]{:S(2)}, u32[]{:S(2)}) %collective-permute-start.26) | collective-permute-done | bytes 786464 | tf_op jit(solution)/shard_map/ppermute | solution.py:40
  121.2 0.9 collective-permute-done.28
  122.7 3.2 %collective-permute-start.31 = (bf16[64,1536]{1,0:T(8,128)(2,1)S(1)}, bf16[64,1536]{1,0:T(8,128)(2,1)S(1)}, u32[]{:S(2)}, u32[]{:S(2)}) collective-permute-start(bf16[64,1536]{1,0:T(8,128)(2,1)S(1)} %get-tuple-element.76), channel_id=1, source_target_pairs={{0,3},{1,0},{2,1},{3,2},{4,7},{5,4},{6,5},{7,6},{8,11},{9,8},{10,9... | collective-permute-start | bytes 589832 | tf_op jit(solution)/shard_map/ppermute | solution.py:40
  125.9 7.0 %down_gradient.1 = bf16[1536,1536]{1,0:T(8,128)(2,1)} custom-call(bf16[512,1536]{1,0:T(8,128)(2,1)S(1)} %constant_dynamic-update-slice_fusion.4.refs_0_, bf16[512,1536]{1,0:T(8,128)(2,1)S(1)} %collective-permute-done.23.refs_1_, bf16[1024,1536]{1,0:T(8,128)(2,1)S(1)} %get-tuple-element.40.held.refs_2_), custom_call_target="tpu_custom_call" | custom-call | flops 4831838208 | bytes 11010048 | tf_op jit(solution)/shard_map/down_gradient/pallas_call | solution.py:227
  133.1 0.8 add_convert_fusion
  (59 shorter events, 4.3 us)
Async XLA Ops:
  0.6 18.0 %copy-start.3 = (bf16[64,1536]{1,0:T(8,128)(2,1)S(1)}, bf16[64,1536]{1,0:T(8,128)(2,1)}, u32[]{:S(2)}) copy-start(bf16[64,1536]{1,0:T(8,128)(2,1)} %param.7) | copy-start | bytes 589828
  0.6 21.1 %copy-start.1 = (s32[48,1536]{1,0:T(8,128)S(1)}, s32[48,1536]{1,0:T(8,128)}, u32[]{:S(2)}) copy-start(s32[48,1536]{1,0:T(8,128)} %param.11) | copy-start | bytes 884740
  0.7 29.2 %copy-start.2 = (s32[48,1536]{1,0:T(8,128)S(1)}, s32[48,1536]{1,0:T(8,128)}, u32[]{:S(2)}) copy-start(s32[48,1536]{1,0:T(8,128)} %param.13) | copy-start | bytes 884740
  0.7 9.8 %collective-permute-start.1 = (bf16[64,1536]{1,0:T(8,128)(2,1)}, bf16[64,1536]{1,0:T(8,128)(2,1)S(1)}, u32[]{:S(2)}, u32[]{:S(2)}) collective-permute-start(bf16[64,1536]{1,0:T(8,128)(2,1)} %param.9), channel_id=1, source_target_pairs={{0,8},{1,9},{2,10},{3,11},{4,12},{5,13},{6,14},{7,15},{8,0},{9,1},... | collective-permute-start | bytes 589832 | tf_op jit(solution)/shard_map/ppermute | solution.py:40
  3.8 6.6 %collective-permute-start = (bf16[64,1536]{1,0:T(8,128)(2,1)}, bf16[64,1536]{1,0:T(8,128)(2,1)S(1)}, u32[]{:S(2)}, u32[]{:S(2)}) collective-permute-start(bf16[64,1536]{1,0:T(8,128)(2,1)} %param.9), channel_id=1, source_target_pairs={{0,12},{1,13},{2,14},{3,15},{4,0},{5,1},{6,2},{7,3},{8,4},{9,5},{1... | collective-permute-start | bytes 589832 | tf_op jit(solution)/shard_map/ppermute | solution.py:40
  5.0 7.1 %collective-permute-start.2 = (bf16[64,1536]{1,0:T(8,128)(2,1)}, bf16[64,1536]{1,0:T(8,128)(2,1)S(1)}, u32[]{:S(2)}, u32[]{:S(2)}) collective-permute-start(bf16[64,1536]{1,0:T(8,128)(2,1)} %param.9), channel_id=1, source_target_pairs={{0,4},{1,5},{2,6},{3,7},{4,8},{5,9},{6,10},{7,11},{8,12},{9,13},{1... | collective-permute-start | bytes 589832 | tf_op jit(solution)/shard_map/ppermute | solution.py:40
  12.1 26.4 %collective-permute-start.9 = (bf16[256,1536]{1,0:T(8,128)(2,1)S(1)}, bf16[256,1536]{1,0:T(8,128)(2,1)S(1)}, u32[]{:S(2)}, u32[]{:S(2)}) collective-permute-start(bf16[256,1536]{1,0:T(8,128)(2,1)S(1)} %constant_dynamic-update-slice_fusion.p0), channel_id=1, source_target_pairs={{0,1},{1,2},{2,3},{3,0},{4,5},{5,6},{6,7},{7,4},{8,9},{9,10},{10,1... | collective-permute-start | bytes 2359304 | tf_op jit(solution)/shard_map/ppermute | solution.py:40
  14.1 24.4 %collective-permute-start.8 = (bf16[256,1536]{1,0:T(8,128)(2,1)S(1)}, bf16[256,1536]{1,0:T(8,128)(2,1)S(1)}, u32[]{:S(2)}, u32[]{:S(2)}) collective-permute-start(bf16[256,1536]{1,0:T(8,128)(2,1)S(1)} %constant_dynamic-update-slice_fusion.p0), channel_id=1, source_target_pairs={{0,2},{1,3},{2,0},{3,1},{4,6},{5,7},{6,4},{7,5},{8,10},{9,11},{10,... | collective-permute-start | bytes 2359304 | tf_op jit(solution)/shard_map/ppermute | solution.py:40
  17.7 20.8 %collective-permute-start.3 = (bf16[256,1536]{1,0:T(8,128)(2,1)S(1)}, bf16[256,1536]{1,0:T(8,128)(2,1)S(1)}, u32[]{:S(2)}, u32[]{:S(2)}) collective-permute-start(bf16[256,1536]{1,0:T(8,128)(2,1)S(1)} %constant_dynamic-update-slice_fusion.p0), channel_id=1, source_target_pairs={{0,3},{1,0},{2,1},{3,2},{4,7},{5,4},{6,5},{7,6},{8,11},{9,8},{10,9... | collective-permute-start | bytes 2359304 | tf_op jit(solution)/shard_map/ppermute | solution.py:40
  18.7 7.8 %collective-permute-start.4 = (bf16[64,1536]{1,0:T(8,128)(2,1)S(1)}, bf16[64,1536]{1,0:T(8,128)(2,1)S(1)}, u32[]{:S(2)}, u32[]{:S(2)}) collective-permute-start(bf16[64,1536]{1,0:T(8,128)(2,1)S(1)} %copy-done.3), channel_id=1, source_target_pairs={{0,4},{1,5},{2,6},{3,7},{4,0},{5,1},{6,2},{7,3},{8,12},{9,13},{10,... | collective-permute-start | bytes 589832 | tf_op jit(solution)/shard_map/ppermute | solution.py:59
  18.7 10.8 %collective-permute-start.5 = (bf16[128,1536]{1,0:T(8,128)(2,1)S(1)}, bf16[128,1536]{1,0:T(8,128)(2,1)S(1)}, u32[]{:S(2)}, u32[]{:S(2)}) collective-permute-start(bf16[128,1536]{1,0:T(8,128)(2,1)S(1)} %fusion.10), channel_id=1, source_target_pairs={{0,96},{16,48},{32,64},{48,16},{64,32},{80,112},{96,0},{112,80},{1... | collective-permute-start | bytes 1179656 | tf_op jit(solution)/shard_map/ppermute | solution.py:48
  26.5 8.0 %collective-permute-start.6 = (bf16[128,1536]{1,0:T(8,128)(2,1)S(1)}, bf16[128,1536]{1,0:T(8,128)(2,1)S(1)}, u32[]{:S(2)}, u32[]{:S(2)}) collective-permute-start(bf16[128,1536]{1,0:T(8,128)(2,1)S(1)} %fusion.10), channel_id=1, source_target_pairs={{0,32},{16,112},{32,0},{48,80},{64,96},{80,48},{96,64},{112,16},{1... | collective-permute-start | bytes 1179656 | tf_op jit(solution)/shard_map/ppermute | solution.py:48
  29.4 9.1 %collective-permute-start.7 = (bf16[128,1536]{1,0:T(8,128)(2,1)S(1)}, bf16[128,1536]{1,0:T(8,128)(2,1)S(1)}, u32[]{:S(2)}, u32[]{:S(2)}) collective-permute-start(bf16[128,1536]{1,0:T(8,128)(2,1)S(1)} %collective-permute-done.5), channel_id=1, source_target_pairs={{0,32},{16,112},{32,0},{48,80},{64,96},{80,48},{96,64},{112,16},{1... | collective-permute-start | bytes 1179656 | tf_op jit(solution)/shard_map/ppermute | solution.py:48
  29.9 3.6 %slice-start = ((s8[4718592]{0:T(1024)(128)(4,1)}), s8[4194304]{0:T(1024)(128)(4,1)S(1)}, s32[]{:S(2)}) async-start(s8[4718592]{0:T(1024)(128)(4,1)} %bitcast.8), calls=%async_computation | async-start | bytes 8388608
  29.9 3.7 %slice-start.1 = ((s8[4718592]{0:T(1024)(128)(4,1)}), s8[524288]{0:T(1024)(128)(4,1)S(1)}, s32[]{:S(2)}) async-start(s8[4718592]{0:T(1024)(128)(4,1)} %bitcast.8), calls=%async_computation.1 | async-start | bytes 1048576
  41.4 3.5 %collective-permute-start.10 = (bf16[512,1536]{1,0:T(8,128)(2,1)S(1)}, bf16[512,1536]{1,0:T(8,128)(2,1)S(1)}, u32[]{:S(2)}, u32[]{:S(2)}) collective-permute-start(bf16[512,1536]{1,0:T(8,128)(2,1)S(1)} %get-tuple-element.41), channel_id=1, source_target_pairs={{0,16},{16,0},{1,17},{17,1},{2,18},{18,2},{3,19},{19,3},{4,20},{20... | collective-permute-start | bytes 4718600 | tf_op jit(solution)/shard_map/ppermute | solution.py:63
  45.5 7.9 %collective-permute-start.12 = (bf16[128,1536]{1,0:T(8,128)(2,1)S(1)}, bf16[128,1536]{1,0:T(8,128)(2,1)S(1)}, u32[]{:S(2)}, u32[]{:S(2)}) collective-permute-start(bf16[128,1536]{1,0:T(8,128)(2,1)S(1)} %get-tuple-element.74), channel_id=1, source_target_pairs={{0,32},{16,112},{32,0},{48,80},{64,96},{80,48},{96,64},{112,16},{1... | collective-permute-start | bytes 1179656 | tf_op jit(solution)/shard_map/ppermute | solution.py:48
  47.3 9.1 %collective-permute-start.14 = (bf16[128,1536]{1,0:T(8,128)(2,1)S(1)}, bf16[128,1536]{1,0:T(8,128)(2,1)S(1)}, u32[]{:S(2)}, u32[]{:S(2)}) collective-permute-start(bf16[128,1536]{1,0:T(8,128)(2,1)S(1)} %pad_maximum_fusion.1.rest_0_), channel_id=1, source_target_pairs={{0,12},{1,13},{2,14},{3,15},{4,8},{5,9},{6,10},{7,11},{8,4},{9,5},... | collective-permute-start | bytes 1179656 | tf_op jit(solution)/shard_map/ppermute | solution.py:59
  49.1 7.8 %collective-permute-start.13 = (bf16[128,1536]{1,0:T(8,128)(2,1)S(1)}, bf16[128,1536]{1,0:T(8,128)(2,1)S(1)}, u32[]{:S(2)}, u32[]{:S(2)}) collective-permute-start(bf16[128,1536]{1,0:T(8,128)(2,1)S(1)} %pad_maximum_fusion.1.rest_0_), channel_id=1, source_target_pairs={{0,1},{1,0},{2,3},{3,2},{4,5},{5,4},{6,7},{7,6},{8,9},{9,8},{10,11... | collective-permute-start | bytes 1179656 | tf_op jit(solution)/shard_map/ppermute | solution.py:59
  49.4 10.7 %collective-permute-start.11 = (bf16[128,1536]{1,0:T(8,128)(2,1)S(1)}, bf16[128,1536]{1,0:T(8,128)(2,1)S(1)}, u32[]{:S(2)}, u32[]{:S(2)}) collective-permute-start(bf16[128,1536]{1,0:T(8,128)(2,1)S(1)} %get-tuple-element.73), channel_id=1, source_target_pairs={{0,32},{16,112},{32,0},{48,80},{64,96},{80,48},{96,64},{112,16},{1... | collective-permute-start | bytes 1179656 | tf_op jit(solution)/shard_map/ppermute | solution.py:48
  56.9 9.0 %collective-permute-start.15 = (bf16[128,1536]{1,0:T(8,128)(2,1)S(1)}, bf16[128,1536]{1,0:T(8,128)(2,1)S(1)}, u32[]{:S(2)}, u32[]{:S(2)}) collective-permute-start(bf16[128,1536]{1,0:T(8,128)(2,1)S(1)} %slice_add_fusion), channel_id=1, source_target_pairs={{0,96},{16,48},{32,64},{48,16},{64,32},{80,112},{96,0},{112,80},{1... | collective-permute-start | bytes 1179656 | tf_op jit(solution)/shard_map/ppermute | solution.py:48
  59.6 9.2 %copy-start = (bf16[128,1536]{1,0:T(8,128)(2,1)S(1)}, bf16[128,1536]{1,0:T(8,128)(2,1)}, u32[]{:S(2)}) copy-start(bf16[128,1536]{1,0:T(8,128)(2,1)} %param.8) | copy-start | bytes 1179652
  59.6 29.5 %collective-permute-start.23 = (bf16[512,1536]{1,0:T(8,128)(2,1)S(1)}, bf16[512,1536]{1,0:T(8,128)(2,1)S(1)}, u32[]{:S(2)}, u32[]{:S(2)}) collective-permute-start(bf16[512,1536]{1,0:T(8,128)(2,1)S(1)} %constant_dynamic-update-slice_fusion.4.refs_0_), channel_id=1, source_target_pairs={{0,16},{16,0},{1,17},{17,1},{2,18},{18,2},{3,19},{19,3},{4,20},{20... | collective-permute-start | bytes 4718600 | tf_op jit(solution)/shard_map/ppermute | solution.py:63
  59.7 9.1 %collective-permute-start.17 = (bf16[128,1536]{1,0:T(8,128)(2,1)S(1)}, bf16[128,1536]{1,0:T(8,128)(2,1)S(1)}, u32[]{:S(2)}, u32[]{:S(2)}) collective-permute-start(bf16[128,1536]{1,0:T(8,128)(2,1)S(1)} %pad_maximum_fusion.1.rest_0_), channel_id=1, source_target_pairs={{0,3},{1,2},{2,1},{3,0},{4,7},{5,6},{6,5},{7,4},{8,11},{9,10},{10,... | collective-permute-start | bytes 1179656 | tf_op jit(solution)/shard_map/ppermute | solution.py:59
  59.8 9.0 %collective-permute-start.16 = (bf16[128,1536]{1,0:T(8,128)(2,1)S(1)}, bf16[128,1536]{1,0:T(8,128)(2,1)S(1)}, u32[]{:S(2)}, u32[]{:S(2)}) collective-permute-start(bf16[128,1536]{1,0:T(8,128)(2,1)S(1)} %collective-permute-done.14.rest_1_), channel_id=1, source_target_pairs={{0,1},{1,0},{2,3},{3,2},{4,5},{5,4},{6,7},{7,6},{8,9},{9,8},{10,11... | collective-permute-start | bytes 1179656 | tf_op jit(solution)/shard_map/ppermute | solution.py:59
  69.1 12.1 %collective-permute-start.18 = (bf16[128,1536]{1,0:T(8,128)(2,1)S(1)}, bf16[128,1536]{1,0:T(8,128)(2,1)S(1)}, u32[]{:S(2)}, u32[]{:S(2)}) collective-permute-start(bf16[128,1536]{1,0:T(8,128)(2,1)S(1)} %fusion.9), channel_id=1, source_target_pairs={{0,96},{16,48},{32,64},{48,16},{64,32},{80,112},{96,0},{112,80},{1... | collective-permute-start | bytes 1179656 | tf_op jit(solution)/shard_map/ppermute | solution.py:48
  69.8 11.4 %collective-permute-start.19 = (bf16[128,1536]{1,0:T(8,128)(2,1)S(1)}, bf16[128,1536]{1,0:T(8,128)(2,1)S(1)}, u32[]{:S(2)}, u32[]{:S(2)}) collective-permute-start(bf16[128,1536]{1,0:T(8,128)(2,1)S(1)} %collective-permute-done.14.rest_1_), channel_id=1, source_target_pairs={{0,3},{1,2},{2,1},{3,0},{4,7},{5,6},{6,5},{7,4},{8,11},{9,10},{10,... | collective-permute-start | bytes 1179656 | tf_op jit(solution)/shard_map/ppermute | solution.py:59
  71.8 12.6 %collective-permute-start.20 = (bf16[128,1536]{1,0:T(8,128)(2,1)S(1)}, bf16[128,1536]{1,0:T(8,128)(2,1)S(1)}, u32[]{:S(2)}, u32[]{:S(2)}) collective-permute-start(bf16[128,1536]{1,0:T(8,128)(2,1)S(1)} %fusion.9), channel_id=1, source_target_pairs={{0,32},{16,112},{32,0},{48,80},{64,96},{80,48},{96,64},{112,16},{1... | collective-permute-start | bytes 1179656 | tf_op jit(solution)/shard_map/ppermute | solution.py:48
  81.2 7.8 %collective-permute-start.21 = (bf16[128,1536]{1,0:T(8,128)(2,1)S(1)}, bf16[128,1536]{1,0:T(8,128)(2,1)S(1)}, u32[]{:S(2)}, u32[]{:S(2)}) collective-permute-start(bf16[128,1536]{1,0:T(8,128)(2,1)S(1)} %collective-permute-done.18), channel_id=1, source_target_pairs={{0,32},{16,112},{32,0},{48,80},{64,96},{80,48},{96,64},{112,16},{1... | collective-permute-start | bytes 1179656 | tf_op jit(solution)/shard_map/ppermute | solution.py:48
  82.3 9.0 %collective-permute-start.22 = (bf16[128,1536]{1,0:T(8,128)(2,1)S(1)}, bf16[128,1536]{1,0:T(8,128)(2,1)S(1)}, u32[]{:S(2)}, u32[]{:S(2)}) collective-permute-start(bf16[128,1536]{1,0:T(8,128)(2,1)S(1)} %collective-permute-done.13.rest_2_), channel_id=1, source_target_pairs={{0,3},{1,2},{2,1},{3,0},{4,7},{5,6},{6,5},{7,4},{8,11},{9,10},{10,... | collective-permute-start | bytes 1179656 | tf_op jit(solution)/shard_map/ppermute | solution.py:59
  91.3 4.8 %collective-permute-start.24 = (bf16[512,1536]{1,0:T(8,128)(2,1)S(1)}, bf16[512,1536]{1,0:T(8,128)(2,1)S(1)}, u32[]{:S(2)}, u32[]{:S(2)}) collective-permute-start(bf16[512,1536]{1,0:T(8,128)(2,1)S(1)} %pad_maximum_fusion.mine), channel_id=1, source_target_pairs={{0,16},{16,0},{1,17},{17,1},{2,18},{18,2},{3,19},{19,3},{4,20},{20... | collective-permute-start | bytes 4718600 | tf_op jit(solution)/shard_map/ppermute | solution.py:63
  91.3 12.0 %collective-permute-start.25 = (bf16[128,1536]{1,0:T(8,128)(2,1)S(1)}, bf16[128,1536]{1,0:T(8,128)(2,1)S(1)}, u32[]{:S(2)}, u32[]{:S(2)}) collective-permute-start(bf16[128,1536]{1,0:T(8,128)(2,1)S(1)} %collective-permute-done.16.rest_3_), channel_id=1, source_target_pairs={{0,3},{1,2},{2,1},{3,0},{4,7},{5,6},{6,5},{7,4},{8,11},{9,10},{10,... | collective-permute-start | bytes 1179656 | tf_op jit(solution)/shard_map/ppermute | solution.py:59
  99.5 21.7 %collective-permute-start.26 = (bf16[256,1536]{1,0:T(8,128)(2,1)S(1)}, bf16[256,1536]{1,0:T(8,128)(2,1)S(1)}, u32[]{:S(2)}, u32[]{:S(2)}) collective-permute-start(bf16[256,1536]{1,0:T(8,128)(2,1)S(1)} %get-tuple-element.61), channel_id=1, source_target_pairs={{0,4},{1,5},{2,6},{3,7},{4,8},{5,9},{6,10},{7,11},{8,12},{9,13},{1... | collective-permute-start | bytes 2359304 | tf_op jit(solution)/shard_map/ppermute | solution.py:40
  99.9 21.3 %collective-permute-start.27 = (bf16[256,1536]{1,0:T(8,128)(2,1)S(1)}, bf16[256,1536]{1,0:T(8,128)(2,1)S(1)}, u32[]{:S(2)}, u32[]{:S(2)}) collective-permute-start(bf16[256,1536]{1,0:T(8,128)(2,1)S(1)} %get-tuple-element.62), channel_id=1, source_target_pairs={{0,8},{1,9},{2,10},{3,11},{4,12},{5,13},{6,14},{7,15},{8,0},{9,1},... | collective-permute-start | bytes 2359304 | tf_op jit(solution)/shard_map/ppermute | solution.py:40
  102.5 19.6 %collective-permute-start.28 = (bf16[256,1536]{1,0:T(8,128)(2,1)S(1)}, bf16[256,1536]{1,0:T(8,128)(2,1)S(1)}, u32[]{:S(2)}, u32[]{:S(2)}) collective-permute-start(bf16[256,1536]{1,0:T(8,128)(2,1)S(1)} %get-tuple-element.63), channel_id=1, source_target_pairs={{0,12},{1,13},{2,14},{3,15},{4,0},{5,1},{6,2},{7,3},{8,4},{9,5},{1... | collective-permute-start | bytes 2359304 | tf_op jit(solution)/shard_map/ppermute | solution.py:40
  122.6 10.3 %collective-permute-start.29 = (bf16[64,1536]{1,0:T(8,128)(2,1)S(1)}, bf16[64,1536]{1,0:T(8,128)(2,1)S(1)}, u32[]{:S(2)}, u32[]{:S(2)}) collective-permute-start(bf16[64,1536]{1,0:T(8,128)(2,1)S(1)} %get-tuple-element.75), channel_id=1, source_target_pairs={{0,1},{1,2},{2,3},{3,0},{4,5},{5,6},{6,7},{7,4},{8,9},{9,10},{10,1... | collective-permute-start | bytes 589832 | tf_op jit(solution)/shard_map/ppermute | solution.py:40
  122.7 10.2 %collective-permute-start.31 = (bf16[64,1536]{1,0:T(8,128)(2,1)S(1)}, bf16[64,1536]{1,0:T(8,128)(2,1)S(1)}, u32[]{:S(2)}, u32[]{:S(2)}) collective-permute-start(bf16[64,1536]{1,0:T(8,128)(2,1)S(1)} %get-tuple-element.76), channel_id=1, source_target_pairs={{0,3},{1,0},{2,1},{3,2},{4,7},{5,4},{6,5},{7,6},{8,11},{9,8},{10,9... | collective-permute-start | bytes 589832 | tf_op jit(solution)/shard_map/ppermute | solution.py:40
  125.9 7.2 %collective-permute-start.30 = (bf16[64,1536]{1,0:T(8,128)(2,1)S(1)}, bf16[64,1536]{1,0:T(8,128)(2,1)S(1)}, u32[]{:S(2)}, u32[]{:S(2)}) collective-permute-start(bf16[64,1536]{1,0:T(8,128)(2,1)S(1)} %get-tuple-element.77), channel_id=1, source_target_pairs={{0,2},{1,3},{2,0},{3,1},{4,6},{5,7},{6,4},{7,5},{8,10},{9,11},{10,... | collective-permute-start | bytes 589832 | tf_op jit(solution)/shard_map/ppermute | solution.py:40

commit v3 on v2

--- a/solution.py
+++ b/solution.py
@@ -306,24 +306,25 @@
     other, ordered = hidden_other(pieces, down_weight)
     chip = hidden_own(ordered, down_weight) + swap_cores(other).astype(F32)
     onward = chip[128:256] + pair_y(chip[384:].astype(BF16), 0).astype(F32)
-    in0 = after(in0, chip)
-    onward, in2, in1 = together(onward, pair_grid(in0, 2), pair_grid(in0, 1))
+    onward, in1 = together(onward, pair_grid(after(in0, chip), 1))
     hidden_grad = chip[:128] + pair_y(chip[256:384].astype(BF16), 0).astype(F32)
     hidden_grad = hidden_grad + pair_y(onward.astype(BF16), 1).astype(F32)
-    hidden_grad, in3, in4 = together(hidden_grad, pair_grid(in1, 2), pair_grid(after(in0, onward), 3))
+
     gated = (gelu_slope * hidden_grad).astype(BF16)
-    near, in5 = together(pair_y(gated, 1), pair_grid(after(in1, hidden_grad), 3))
-    act = jnp.concatenate([act0, act1, act2, act3])
+    in01 = jnp.concatenate([in0, in1])
+    near, in2, in3 = together(pair_y(gated, 1), pair_grid(in01, 2), pair_grid(in01, 3))
+    act = after(jnp.concatenate([act0, act1, act2, act3]), onward)
     mine = jnp.concatenate([gated, near, pair_y(gated, 0), pair_y(near, 0)])
-    mine, in6, act_theirs = together(mine, pair_grid(after(in2, near), 3), swap_cores(act))
-    theirs = swap_cores(mine)
+    mine, act_theirs = together(mine, swap_cores(act))
+
+    theirs, in4 = swap_cores(mine), pair_grid(in2, 3)
     parts = list(input_all(theirs, up_weight, input_own(mine, up_weight)))
-    parts[0], in7 = together(parts[0], pair_grid(after(in3, mine), 3))
     rest = scatter_first(parts)
 
-    up_grad = up_gradient(mine, theirs, [in0, in1, in2, in3, in4, in5, in6, in7])
-    rest, up_grad = together(rest, up_grad)
+    act, in01 = after(act, parts[0]), after(in01, parts[0])
     down_grad = down_gradient([act, act_theirs], ordered)
+    up_grad = up_gradient(mine, theirs, [in01, in2, in3, in4])
+    rest, down_grad, up_grad = together(rest, down_grad, up_grad)
     return (scatter_second(rest), up_grad, down_grad)
 
 

time: 134 us -> 128 us (0.955)
  starting transfers between devices: 41.2 us -> 35.3 us
    ppermute x8 -> x5, starting transfers between devices: 8.84 us -> 4.99 us  [pair_grid(): return lax.ppermute(value, ('k', 'x', 'z'), pairs)]
    ppermute x12, waiting for transfers between devices: 15.7 us -> 13.3 us  [from_grid(): return lax.ppermute(value, ('k', 'x', 'z'), shift_grid(first, step))]
    ppermute x8 -> x5, waiting for transfers between devices: 13.2 us -> 15 us  [pair_grid(): return lax.ppermute(value, ('k', 'x', 'z'), pairs)]
    ppermute x9, starting transfers between devices: 13.3 us -> 11.6 us  [pair_y(): return lax.ppermute(value, ('y', 'k'), pairs)]
  transfers between devices with their start and end apart: 32 -> 29, of which waited for: 17 -> 20; matrix products, arithmetic and copies ran while one was open for 5% -> 6% of each run, Pallas kernels for 17% -> 18%
where the time goes in v3:
time: 128 us
  waiting for transfers between devices  55.3 us (43%)
  starting transfers between devices  35.3 us (28%)
  Pallas kernels  25.9 us (20%)
  other arithmetic  9 us (7%)
  local copies, waits for them, and re-layouts  1.48 us (1%)
    ppermute x9, waiting for transfers between devices, pair_y(): return lax.ppermute(value, ('y', 'k'), pairs)  26.3 us
    ppermute x12, starting transfers between devices, from_grid(): return lax.ppermute(value, ('k', 'x', 'z'), shift_grid(first, step))  18.5 us
    ppermute x5, waiting for transfers between devices, pair_grid(): return lax.ppermute(value, ('k', 'x', 'z'), pairs)  15 us
    ppermute x12, waiting for transfers between devices, from_grid(): return lax.ppermute(value, ('k', 'x', 'z'), shift_grid(first, step))  13.3 us
    ppermute x9, starting transfers between devices, pair_y(): return lax.ppermute(value, ('y', 'k'), pairs)  11.6 us
    pallas_call x1, Pallas kernels, up_gradient(): pl.pallas_call(up_kernel, grid=(m // TILE,), out_shape=jax.ShapeDtypeStru...  7.36 us
    pallas_call x1, Pallas kernels, down_gradient(): pl.pallas_call(down_kernel, grid=(m // TILE,), out_shape=jax.ShapeDtypeSt...  6.97 us
    ppermute x5, starting transfers between devices, pair_grid(): return lax.ppermute(value, ('k', 'x', 'z'), pairs)  4.99 us
  transfers between devices with their start and end apart: 29, of which 20 were waited for; matrix products, arithmetic and copies ran while one was open for 6% of the time, Pallas kernels for 18%

profile of v3, /device:TPU:0, one launch (start us, length us, event | category | flops | bytes accessed | tf_op | source)
XLA Modules:
  0.0 127.8 jit_solution(8199735613239041009)
XLA Ops:
  0.6 2.9 %collective-permute-start = (bf16[64,1536]{1,0:T(8,128)(2,1)}, bf16[64,1536]{1,0:T(8,128)(2,1)S(1)}, u32[]{:S(2)}, u32[]{:S(2)}) collective-permute-start(bf16[64,1536]{1,0:T(8,128)(2,1)} %param.9), channel_id=1, source_target_pairs={{0,12},{1,13},{2,14},{3,15},{4,0},{5,1},{6,2},{7,3},{8,4},{9,5},{1... | collective-permute-start | bytes 589832 | tf_op jit(solution)/shard_map/ppermute | solution.py:40
  3.6 0.8 collective-permute-start.1
  4.4 0.9 collective-permute-start.2
  5.2 1.2 fusion.10
  6.4 0.9 constant_dynamic-update-slice_fusion.3
  7.3 1.8 %collective-permute-done = bf16[64,1536]{1,0:T(8,128)(2,1)S(1)} collective-permute-done((bf16[64,1536]{1,0:T(8,128)(2,1)}, bf16[64,1536]{1,0:T(8,128)(2,1)S(1)}, u32[]{:S(2)}, u32[]{:S(2)}) %collective-permute-start) | collective-permute-done | bytes 196640 | tf_op jit(solution)/shard_map/ppermute | solution.py:40
  9.2 1.8 %collective-permute-done.1 = bf16[64,1536]{1,0:T(8,128)(2,1)S(1)} collective-permute-done((bf16[64,1536]{1,0:T(8,128)(2,1)}, bf16[64,1536]{1,0:T(8,128)(2,1)S(1)}, u32[]{:S(2)}, u32[]{:S(2)}) %collective-permute-start.1) | collective-permute-done | bytes 196640 | tf_op jit(solution)/shard_map/ppermute | solution.py:40
  11.1 2.0 %collective-permute-done.2 = bf16[64,1536]{1,0:T(8,128)(2,1)S(1)} collective-permute-done((bf16[64,1536]{1,0:T(8,128)(2,1)}, bf16[64,1536]{1,0:T(8,128)(2,1)S(1)}, u32[]{:S(2)}, u32[]{:S(2)}) %collective-permute-start.2) | collective-permute-done | bytes 196640 | tf_op jit(solution)/shard_map/ppermute | solution.py:40
  13.1 4.1 %collective-permute-start.3 = (bf16[256,1536]{1,0:T(8,128)(2,1)S(1)}, bf16[256,1536]{1,0:T(8,128)(2,1)S(1)}, u32[]{:S(2)}, u32[]{:S(2)}) collective-permute-start(bf16[256,1536]{1,0:T(8,128)(2,1)S(1)} %constant_dynamic-update-slice_fusion.p0), channel_id=1, source_target_pairs={{0,3},{1,0},{2,1},{3,2},{4,7},{5,4},{6,5},{7,6},{8,11},{9,8},{10,9... | collective-permute-start | bytes 2359304 | tf_op jit(solution)/shard_map/ppermute | solution.py:40
  17.2 1.3 collective-permute-start.9
  18.4 3.0 %collective-permute-start.5 = (bf16[128,1536]{1,0:T(8,128)(2,1)S(1)}, bf16[128,1536]{1,0:T(8,128)(2,1)S(1)}, u32[]{:S(2)}, u32[]{:S(2)}) collective-permute-start(bf16[128,1536]{1,0:T(8,128)(2,1)S(1)} %fusion.10), channel_id=1, source_target_pairs={{0,96},{16,48},{32,64},{48,16},{64,32},{80,112},{96,0},{112,80},{1... | collective-permute-start | bytes 1179656 | tf_op jit(solution)/shard_map/ppermute | solution.py:48
  21.4 1.0 multiply_exponential_fusion.1
  22.5 4.0 %collective-permute-done.4 = bf16[64,1536]{1,0:T(8,128)(2,1)S(1)} collective-permute-done((bf16[64,1536]{1,0:T(8,128)(2,1)}, bf16[64,1536]{1,0:T(8,128)(2,1)S(1)}, u32[]{:S(2)}, u32[]{:S(2)}) %collective-permute-start.4) | collective-permute-done | bytes 196640 | tf_op jit(solution)/shard_map/ppermute | solution.py:59
  26.5 1.6 %collective-permute-start.6 = (bf16[128,1536]{1,0:T(8,128)(2,1)S(1)}, bf16[128,1536]{1,0:T(8,128)(2,1)S(1)}, u32[]{:S(2)}, u32[]{:S(2)}) collective-permute-start(bf16[128,1536]{1,0:T(8,128)(2,1)S(1)} %fusion.10), channel_id=1, source_target_pairs={{0,32},{16,112},{32,0},{48,80},{64,96},{80,48},{96,64},{112,16},{1... | collective-permute-start | bytes 1179656 | tf_op jit(solution)/shard_map/ppermute | solution.py:48
  28.6 3.4 %fusion.1.w = bf16[1536,1536]{1,0:T(8,128)(2,1)S(1)} fusion(bf16[1536,1536]{1,0:T(8,128)(2,1)} %param.10, f32[48,1536]{1,0:T(8,128)S(1)} %multiply_exponential_fusion.1), kind=kLoop, calls=%fused_computation.3 | loop fusion | flops 7077888 | bytes 9732096 | tf_op jit(solution)/shard_map/convert_element_type | solution.py:17
  32.2 0.9 fusion.w
  33.2 1.1 collective-permute-done.6
  34.3 4.2 %collective-permute-done.7 = bf16[128,1536]{1,0:T(8,128)(2,1)S(1)} collective-permute-done((bf16[128,1536]{1,0:T(8,128)(2,1)S(1)}, bf16[128,1536]{1,0:T(8,128)(2,1)S(1)}, u32[]{:S(2)}, u32[]{:S(2)}) %collective-permute-start.7) | collective-permute-done | bytes 393248 | tf_op jit(solution)/shard_map/ppermute | solution.py:48
  38.8 2.9 %hidden_other.1 = (bf16[512,1536]{1,0:T(8,128)(2,1)S(1)}, bf16[1024,1536]{1,0:T(8,128)(2,1)S(1)}) custom-call(bf16[256,1536]{1,0:T(8,128)(2,1)S(1)} %constant_dynamic-update-slice_fusion.p0, bf16[256,1536]{1,0:T(8,128)(2,1)S(1)} %collective-permute-done.3.p1, bf16[256,1536]{1,0:T(8,128)(2,1)S(1)} %collective-permute-done.8.p2, ...), custom_call_target="tpu_custom_call" | custom-call | flops 2415919104 | bytes 9437184 | tf_op jit(solution)/shard_map/hidden_other/pallas_call | solution.py:136
  41.8 2.6 %hidden_own.1 = f32[512,1536]{1,0:T(8,128)S(1)} custom-call(bf16[1024,1536]{1,0:T(8,128)(2,1)S(1)} %get-tuple-element.34.held.refs_2_, bf16[1536,1536]{1,0:T(8,128)(2,1)S(1)} %fusion.w), custom_call_target="tpu_custom_call" | custom-call | flops 2415919104 | bytes 11010048 | tf_op jit(solution)/shard_map/hidden_own/pallas_call | solution.py:156
  44.4 0.8 collective-permute-done.10
  45.8 1.7 %collective-permute-start.12 = (bf16[128,1536]{1,0:T(8,128)(2,1)S(1)}, bf16[128,1536]{1,0:T(8,128)(2,1)S(1)}, u32[]{:S(2)}, u32[]{:S(2)}) collective-permute-start(bf16[128,1536]{1,0:T(8,128)(2,1)S(1)} %get-tuple-element.62), channel_id=1, source_target_pairs={{0,32},{16,112},{32,0},{48,80},{64,96},{80,48},{96,64},{112,16},{1... | collective-permute-start | bytes 1179656 | tf_op jit(solution)/shard_map/ppermute | solution.py:48
  48.7 5.0 %collective-permute-done.12 = bf16[128,1536]{1,0:T(8,128)(2,1)S(1)} collective-permute-done((bf16[128,1536]{1,0:T(8,128)(2,1)S(1)}, bf16[128,1536]{1,0:T(8,128)(2,1)S(1)}, u32[]{:S(2)}, u32[]{:S(2)}) %collective-permute-start.12) | collective-permute-done | bytes 393248 | tf_op jit(solution)/shard_map/ppermute | solution.py:48
  53.8 2.9 %collective-permute-done.13 = bf16[128,1536]{1,0:T(8,128)(2,1)S(1)} collective-permute-done((bf16[128,1536]{1,0:T(8,128)(2,1)S(1)}, bf16[128,1536]{1,0:T(8,128)(2,1)S(1)}, u32[]{:S(2)}, u32[]{:S(2)}) %collective-permute-start.13) | collective-permute-done | bytes 393248 | tf_op jit(solution)/shard_map/ppermute | solution.py:59
  56.7 2.2 %collective-permute-start.14 = (bf16[128,1536]{1,0:T(8,128)(2,1)S(1)}, bf16[128,1536]{1,0:T(8,128)(2,1)S(1)}, u32[]{:S(2)}, u32[]{:S(2)}) collective-permute-start(bf16[128,1536]{1,0:T(8,128)(2,1)S(1)} %slice_add_fusion), channel_id=1, source_target_pairs={{0,96},{16,48},{32,64},{48,16},{64,32},{80,112},{96,0},{112,80},{1... | collective-permute-start | bytes 1179656 | tf_op jit(solution)/shard_map/ppermute | solution.py:48
  58.9 2.0 %collective-permute-start.16 = (bf16[256,1536]{1,0:T(8,128)(2,1)S(1)}, bf16[256,1536]{1,0:T(8,128)(2,1)S(1)}, u32[]{:S(2)}, u32[]{:S(2)}) collective-permute-start(bf16[256,1536]{1,0:T(8,128)(2,1)S(1)} %constant_dynamic-update-slice_fusion.4.rest_0_), channel_id=1, source_target_pairs={{0,1},{1,0},{2,3},{3,2},{4,5},{5,4},{6,7},{7,6},{8,9},{9,8},{10,11... | collective-permute-start | bytes 2359304 | tf_op jit(solution)/shard_map/ppermute | solution.py:59
  61.5 4.1 %collective-permute-done.14 = bf16[128,1536]{1,0:T(8,128)(2,1)S(1)} collective-permute-done((bf16[128,1536]{1,0:T(8,128)(2,1)S(1)}, bf16[128,1536]{1,0:T(8,128)(2,1)S(1)}, u32[]{:S(2)}, u32[]{:S(2)}) %collective-permute-start.14) | collective-permute-done | bytes 393248 | tf_op jit(solution)/shard_map/ppermute | solution.py:48
  66.1 2.3 %collective-permute-start.15 = (bf16[128,1536]{1,0:T(8,128)(2,1)S(1)}, bf16[128,1536]{1,0:T(8,128)(2,1)S(1)}, u32[]{:S(2)}, u32[]{:S(2)}) collective-permute-start(bf16[128,1536]{1,0:T(8,128)(2,1)S(1)} %fusion.9), channel_id=1, source_target_pairs={{0,96},{16,48},{32,64},{48,16},{64,32},{80,112},{96,0},{112,80},{1... | collective-permute-start | bytes 1179656 | tf_op jit(solution)/shard_map/ppermute | solution.py:48
  68.4 2.6 %collective-permute-done.16.rest_1_ = bf16[256,1536]{1,0:T(8,128)(2,1)S(1)} collective-permute-done((bf16[256,1536]{1,0:T(8,128)(2,1)S(1)}, bf16[256,1536]{1,0:T(8,128)(2,1)S(1)}, u32[]{:S(2)}, u32[]{:S(2)}) %collective-permute-start.16) | collective-permute-done | bytes 786464 | tf_op jit(solution)/shard_map/ppermute | solution.py:59
  71.0 3.1 %collective-permute-done.17.rest_2_ = bf16[256,1536]{1,0:T(8,128)(2,1)S(1)} collective-permute-done((bf16[256,1536]{1,0:T(8,128)(2,1)S(1)}, bf16[256,1536]{1,0:T(8,128)(2,1)S(1)}, u32[]{:S(2)}, u32[]{:S(2)}) %collective-permute-start.17) | collective-permute-done | bytes 786464 | tf_op jit(solution)/shard_map/ppermute | solution.py:59
  74.1 4.1 %collective-permute-done.15 = bf16[128,1536]{1,0:T(8,128)(2,1)S(1)} collective-permute-done((bf16[128,1536]{1,0:T(8,128)(2,1)S(1)}, bf16[128,1536]{1,0:T(8,128)(2,1)S(1)}, u32[]{:S(2)}, u32[]{:S(2)}) %collective-permute-start.15) | collective-permute-done | bytes 393248 | tf_op jit(solution)/shard_map/ppermute | solution.py:48
  78.2 7.8 %collective-permute-done.19 = bf16[128,1536]{1,0:T(8,128)(2,1)S(1)} collective-permute-done((bf16[128,1536]{1,0:T(8,128)(2,1)S(1)}, bf16[128,1536]{1,0:T(8,128)(2,1)S(1)}, u32[]{:S(2)}, u32[]{:S(2)}) %collective-permute-start.19) | collective-permute-done | bytes 393248 | tf_op jit(solution)/shard_map/ppermute | solution.py:48
  86.2 1.7 %collective-permute-start.25 = (bf16[256,1536]{1,0:T(8,128)(2,1)S(1)}, bf16[256,1536]{1,0:T(8,128)(2,1)S(1)}, u32[]{:S(2)}, u32[]{:S(2)}) collective-permute-start(bf16[256,1536]{1,0:T(8,128)(2,1)S(1)} %collective-permute-done.16.rest_1_), channel_id=1, source_target_pairs={{0,3},{1,2},{2,1},{3,0},{4,7},{5,6},{6,5},{7,4},{8,11},{9,10},{10,... | collective-permute-start | bytes 2359304 | tf_op jit(solution)/shard_map/ppermute | solution.py:59
  87.9 2.6 %input_own.1.own = f32[512,1536]{1,0:T(8,128)S(1)} custom-call(bf16[512,1536]{1,0:T(8,128)(2,1)S(1)} %pad_maximum_fusion.mine, bf16[1536,1536]{1,0:T(8,128)(2,1)S(1)} %fusion.1.w), custom_call_target="tpu_custom_call" | custom-call | flops 2415919104 | bytes 9437184 | tf_op jit(solution)/shard_map/input_own/pallas_call | solution.py:176
  90.6 3.4 %input_all.1 = (f32[256,1536]{1,0:T(8,128)S(1)}, bf16[256,1536]{1,0:T(8,128)(2,1)S(1)}, bf16[256,1536]{1,0:T(8,128)(2,1)S(1)}, bf16[256,1536]{1,0:T(8,128)(2,1)S(1)}) custom-call(bf16[512,1536]{1,0:T(8,128)(2,1)S(1)} %collective-permute-done.21.theirs, bf16[1536,1536]{1,0:T(8,128)(2,1)S(1)} %fusion.1.w, f32[512,1536]{1,0:T(8,128)S(1)} %input_own.1.own), custom_call_target="tpu_custom_call" | custom-call | flops 2415919104 | bytes 12582912 | tf_op jit(solution)/shard_map/input_all/pallas_call | solution.py:201
  94.1 2.3 %collective-permute-start.23 = (bf16[256,1536]{1,0:T(8,128)(2,1)S(1)}, bf16[256,1536]{1,0:T(8,128)(2,1)S(1)}, u32[]{:S(2)}, u32[]{:S(2)}) collective-permute-start(bf16[256,1536]{1,0:T(8,128)(2,1)S(1)} %get-tuple-element.49), channel_id=1, source_target_pairs={{0,8},{1,9},{2,10},{3,11},{4,12},{5,13},{6,14},{7,15},{8,0},{9,1},... | collective-permute-start | bytes 2359304 | tf_op jit(solution)/shard_map/ppermute | solution.py:40
  96.5 0.8 collective-permute-start.24
  97.3 7.0 %down_gradient.1 = bf16[1536,1536]{1,0:T(8,128)(2,1)} custom-call(bf16[512,1536]{1,0:T(8,128)(2,1)S(1)} %pad_maximum_fusion.1.refs_0_, bf16[512,1536]{1,0:T(8,128)(2,1)S(1)} %collective-permute-done.20.refs_1_, bf16[1024,1536]{1,0:T(8,128)(2,1)S(1)} %get-tuple-element.34.held.refs_2_), custom_call_target="tpu_custom_call" | custom-call | flops 4831838208 | bytes 11010048 | tf_op jit(solution)/shard_map/down_gradient/pallas_call | solution.py:227
  104.3 2.3 %collective-permute-done.25.rest_3_ = bf16[256,1536]{1,0:T(8,128)(2,1)S(1)} collective-permute-done((bf16[256,1536]{1,0:T(8,128)(2,1)S(1)}, bf16[256,1536]{1,0:T(8,128)(2,1)S(1)}, u32[]{:S(2)}, u32[]{:S(2)}) %collective-permute-start.25) | collective-permute-done | bytes 786464 | tf_op jit(solution)/shard_map/ppermute | solution.py:59
  106.6 7.4 %up_gradient.1 = bf16[1536,1536]{1,0:T(8,128)(2,1)} custom-call(bf16[512,1536]{1,0:T(8,128)(2,1)S(1)} %pad_maximum_fusion.mine, bf16[512,1536]{1,0:T(8,128)(2,1)S(1)} %collective-permute-done.21.theirs, bf16[256,1536]{1,0:T(8,128)(2,1)S(1)} %constant_dynamic-update-slice_fusion.4.rest_0_, bf16[256,1536]{1,0:T(8,128)(2,1)S(1)} %collective-permute-done.16.rest_1_, ...), custom_call_target="tpu_custom_call" | custom-call | flops 4831838208 | bytes 11010048 | tf_op jit(solution)/shard_map/up_gradient/pallas_call | solution.py:259
  113.9 1.8 %collective-permute-done.22 = bf16[256,1536]{1,0:T(8,128)(2,1)S(1)} collective-permute-done((bf16[256,1536]{1,0:T(8,128)(2,1)S(1)}, bf16[256,1536]{1,0:T(8,128)(2,1)S(1)}, u32[]{:S(2)}, u32[]{:S(2)}) %collective-permute-start.22) | collective-permute-done | bytes 786464 | tf_op jit(solution)/shard_map/ppermute | solution.py:40
  115.8 0.8 collective-permute-done.24
  117.1 1.4 %collective-permute-start.26 = (bf16[64,1536]{1,0:T(8,128)(2,1)S(1)}, bf16[64,1536]{1,0:T(8,128)(2,1)S(1)}, u32[]{:S(2)}, u32[]{:S(2)}) collective-permute-start(bf16[64,1536]{1,0:T(8,128)(2,1)S(1)} %get-tuple-element.63), channel_id=1, source_target_pairs={{0,1},{1,2},{2,3},{3,0},{4,5},{5,6},{6,7},{7,4},{8,9},{9,10},{10,1... | collective-permute-start | bytes 589832 | tf_op jit(solution)/shard_map/ppermute | solution.py:40
  118.5 1.7 %collective-permute-start.27 = (bf16[64,1536]{1,0:T(8,128)(2,1)S(1)}, bf16[64,1536]{1,0:T(8,128)(2,1)S(1)}, u32[]{:S(2)}, u32[]{:S(2)}) collective-permute-start(bf16[64,1536]{1,0:T(8,128)(2,1)S(1)} %get-tuple-element.65), channel_id=1, source_target_pairs={{0,2},{1,3},{2,0},{3,1},{4,6},{5,7},{6,4},{7,5},{8,10},{9,11},{10,... | collective-permute-start | bytes 589832 | tf_op jit(solution)/shard_map/ppermute | solution.py:40
  120.2 2.1 %collective-permute-start.28 = (bf16[64,1536]{1,0:T(8,128)(2,1)S(1)}, bf16[64,1536]{1,0:T(8,128)(2,1)S(1)}, u32[]{:S(2)}, u32[]{:S(2)}) collective-permute-start(bf16[64,1536]{1,0:T(8,128)(2,1)S(1)} %get-tuple-element.64), channel_id=1, source_target_pairs={{0,3},{1,0},{2,1},{3,2},{4,7},{5,4},{6,5},{7,6},{8,11},{9,8},{10,9... | collective-permute-start | bytes 589832 | tf_op jit(solution)/shard_map/ppermute | solution.py:40
  122.4 3.8 %collective-permute-done.26 = bf16[64,1536]{1,0:T(8,128)(2,1)S(1)} collective-permute-done((bf16[64,1536]{1,0:T(8,128)(2,1)S(1)}, bf16[64,1536]{1,0:T(8,128)(2,1)S(1)}, u32[]{:S(2)}, u32[]{:S(2)}) %collective-permute-start.26) | collective-permute-done | bytes 196640 | tf_op jit(solution)/shard_map/ppermute | solution.py:40
  126.2 0.9 collective-permute-done.28
  127.0 0.8 add_convert_fusion
  (49 shorter events, 5.2 us)
Async XLA Ops:
  0.6 27.9 %copy-start.1 = (s32[48,1536]{1,0:T(8,128)S(1)}, s32[48,1536]{1,0:T(8,128)}, u32[]{:S(2)}) copy-start(s32[48,1536]{1,0:T(8,128)} %param.13) | copy-start | bytes 884740
  0.6 8.6 %collective-permute-start = (bf16[64,1536]{1,0:T(8,128)(2,1)}, bf16[64,1536]{1,0:T(8,128)(2,1)S(1)}, u32[]{:S(2)}, u32[]{:S(2)}) collective-permute-start(bf16[64,1536]{1,0:T(8,128)(2,1)} %param.9), channel_id=1, source_target_pairs={{0,12},{1,13},{2,14},{3,15},{4,0},{5,1},{6,2},{7,3},{8,4},{9,5},{1... | collective-permute-start | bytes 589832 | tf_op jit(solution)/shard_map/ppermute | solution.py:40
  3.6 7.5 %collective-permute-start.1 = (bf16[64,1536]{1,0:T(8,128)(2,1)}, bf16[64,1536]{1,0:T(8,128)(2,1)S(1)}, u32[]{:S(2)}, u32[]{:S(2)}) collective-permute-start(bf16[64,1536]{1,0:T(8,128)(2,1)} %param.9), channel_id=1, source_target_pairs={{0,8},{1,9},{2,10},{3,11},{4,12},{5,13},{6,14},{7,15},{8,0},{9,1},... | collective-permute-start | bytes 589832 | tf_op jit(solution)/shard_map/ppermute | solution.py:40
  4.4 8.7 %collective-permute-start.2 = (bf16[64,1536]{1,0:T(8,128)(2,1)}, bf16[64,1536]{1,0:T(8,128)(2,1)S(1)}, u32[]{:S(2)}, u32[]{:S(2)}) collective-permute-start(bf16[64,1536]{1,0:T(8,128)(2,1)} %param.9), channel_id=1, source_target_pairs={{0,4},{1,5},{2,6},{3,7},{4,8},{5,9},{6,10},{7,11},{8,12},{9,13},{1... | collective-permute-start | bytes 589832 | tf_op jit(solution)/shard_map/ppermute | solution.py:40
  13.1 25.4 %collective-permute-start.3 = (bf16[256,1536]{1,0:T(8,128)(2,1)S(1)}, bf16[256,1536]{1,0:T(8,128)(2,1)S(1)}, u32[]{:S(2)}, u32[]{:S(2)}) collective-permute-start(bf16[256,1536]{1,0:T(8,128)(2,1)S(1)} %constant_dynamic-update-slice_fusion.p0), channel_id=1, source_target_pairs={{0,3},{1,0},{2,1},{3,2},{4,7},{5,4},{6,5},{7,6},{8,11},{9,8},{10,9... | collective-permute-start | bytes 2359304 | tf_op jit(solution)/shard_map/ppermute | solution.py:40
  17.2 21.3 %collective-permute-start.8 = (bf16[256,1536]{1,0:T(8,128)(2,1)S(1)}, bf16[256,1536]{1,0:T(8,128)(2,1)S(1)}, u32[]{:S(2)}, u32[]{:S(2)}) collective-permute-start(bf16[256,1536]{1,0:T(8,128)(2,1)S(1)} %constant_dynamic-update-slice_fusion.p0), channel_id=1, source_target_pairs={{0,2},{1,3},{2,0},{3,1},{4,6},{5,7},{6,4},{7,5},{8,10},{9,11},{10,... | collective-permute-start | bytes 2359304 | tf_op jit(solution)/shard_map/ppermute | solution.py:40
  17.2 21.6 %collective-permute-start.9 = (bf16[256,1536]{1,0:T(8,128)(2,1)S(1)}, bf16[256,1536]{1,0:T(8,128)(2,1)S(1)}, u32[]{:S(2)}, u32[]{:S(2)}) collective-permute-start(bf16[256,1536]{1,0:T(8,128)(2,1)S(1)} %constant_dynamic-update-slice_fusion.p0), channel_id=1, source_target_pairs={{0,1},{1,2},{2,3},{3,0},{4,5},{5,6},{6,7},{7,4},{8,9},{9,10},{10,1... | collective-permute-start | bytes 2359304 | tf_op jit(solution)/shard_map/ppermute | solution.py:40
  18.4 8.0 %collective-permute-start.4 = (bf16[64,1536]{1,0:T(8,128)(2,1)}, bf16[64,1536]{1,0:T(8,128)(2,1)S(1)}, u32[]{:S(2)}, u32[]{:S(2)}) collective-permute-start(bf16[64,1536]{1,0:T(8,128)(2,1)} %param.7), channel_id=1, source_target_pairs={{0,4},{1,5},{2,6},{3,7},{4,0},{5,1},{6,2},{7,3},{8,12},{9,13},{10,... | collective-permute-start | bytes 589832 | tf_op jit(solution)/shard_map/ppermute | solution.py:59
  18.4 9.6 %collective-permute-start.5 = (bf16[128,1536]{1,0:T(8,128)(2,1)S(1)}, bf16[128,1536]{1,0:T(8,128)(2,1)S(1)}, u32[]{:S(2)}, u32[]{:S(2)}) collective-permute-start(bf16[128,1536]{1,0:T(8,128)(2,1)S(1)} %fusion.10), channel_id=1, source_target_pairs={{0,96},{16,48},{32,64},{48,16},{64,32},{80,112},{96,0},{112,80},{1... | collective-permute-start | bytes 1179656 | tf_op jit(solution)/shard_map/ppermute | solution.py:48
  26.5 7.8 %collective-permute-start.6 = (bf16[128,1536]{1,0:T(8,128)(2,1)S(1)}, bf16[128,1536]{1,0:T(8,128)(2,1)S(1)}, u32[]{:S(2)}, u32[]{:S(2)}) collective-permute-start(bf16[128,1536]{1,0:T(8,128)(2,1)S(1)} %fusion.10), channel_id=1, source_target_pairs={{0,32},{16,112},{32,0},{48,80},{64,96},{80,48},{96,64},{112,16},{1... | collective-permute-start | bytes 1179656 | tf_op jit(solution)/shard_map/ppermute | solution.py:48
  28.1 10.4 %collective-permute-start.7 = (bf16[128,1536]{1,0:T(8,128)(2,1)S(1)}, bf16[128,1536]{1,0:T(8,128)(2,1)S(1)}, u32[]{:S(2)}, u32[]{:S(2)}) collective-permute-start(bf16[128,1536]{1,0:T(8,128)(2,1)S(1)} %collective-permute-done.5), channel_id=1, source_target_pairs={{0,32},{16,112},{32,0},{48,80},{64,96},{80,48},{96,64},{112,16},{1... | collective-permute-start | bytes 1179656 | tf_op jit(solution)/shard_map/ppermute | solution.py:48
  28.5 3.6 %slice-start = ((s8[4718592]{0:T(1024)(128)(4,1)}), s8[4194304]{0:T(1024)(128)(4,1)S(1)}, s32[]{:S(2)}) async-start(s8[4718592]{0:T(1024)(128)(4,1)} %bitcast.8), calls=%async_computation | async-start | bytes 8388608
  28.6 3.7 %slice-start.1 = ((s8[4718592]{0:T(1024)(128)(4,1)}), s8[524288]{0:T(1024)(128)(4,1)S(1)}, s32[]{:S(2)}) async-start(s8[4718592]{0:T(1024)(128)(4,1)} %bitcast.8), calls=%async_computation.1 | async-start | bytes 1048576
  32.2 0.9 copy-start.2
  41.7 3.5 %collective-permute-start.10 = (bf16[512,1536]{1,0:T(8,128)(2,1)S(1)}, bf16[512,1536]{1,0:T(8,128)(2,1)S(1)}, u32[]{:S(2)}, u32[]{:S(2)}) collective-permute-start(bf16[512,1536]{1,0:T(8,128)(2,1)S(1)} %get-tuple-element.35), channel_id=1, source_target_pairs={{0,16},{16,0},{1,17},{17,1},{2,18},{18,2},{3,19},{19,3},{4,20},{20... | collective-permute-start | bytes 4718600 | tf_op jit(solution)/shard_map/ppermute | solution.py:63
  45.8 19.8 %copy-start = (bf16[128,1536]{1,0:T(8,128)(2,1)S(1)}, bf16[128,1536]{1,0:T(8,128)(2,1)}, u32[]{:S(2)}) copy-start(bf16[128,1536]{1,0:T(8,128)(2,1)} %param.8) | copy-start | bytes 1179652
  45.8 7.9 %collective-permute-start.12 = (bf16[128,1536]{1,0:T(8,128)(2,1)S(1)}, bf16[128,1536]{1,0:T(8,128)(2,1)S(1)}, u32[]{:S(2)}, u32[]{:S(2)}) collective-permute-start(bf16[128,1536]{1,0:T(8,128)(2,1)S(1)} %get-tuple-element.62), channel_id=1, source_target_pairs={{0,32},{16,112},{32,0},{48,80},{64,96},{80,48},{96,64},{112,16},{1... | collective-permute-start | bytes 1179656 | tf_op jit(solution)/shard_map/ppermute | solution.py:48
  47.6 9.1 %collective-permute-start.13 = (bf16[128,1536]{1,0:T(8,128)(2,1)S(1)}, bf16[128,1536]{1,0:T(8,128)(2,1)S(1)}, u32[]{:S(2)}, u32[]{:S(2)}) collective-permute-start(bf16[128,1536]{1,0:T(8,128)(2,1)S(1)} %pad_maximum_fusion.2), channel_id=1, source_target_pairs={{0,12},{1,13},{2,14},{3,15},{4,8},{5,9},{6,10},{7,11},{8,4},{9,5},... | collective-permute-start | bytes 1179656 | tf_op jit(solution)/shard_map/ppermute | solution.py:59
  48.2 13.3 %collective-permute-start.11 = (bf16[128,1536]{1,0:T(8,128)(2,1)S(1)}, bf16[128,1536]{1,0:T(8,128)(2,1)S(1)}, u32[]{:S(2)}, u32[]{:S(2)}) collective-permute-start(bf16[128,1536]{1,0:T(8,128)(2,1)S(1)} %get-tuple-element.61), channel_id=1, source_target_pairs={{0,32},{16,112},{32,0},{48,80},{64,96},{80,48},{96,64},{112,16},{1... | collective-permute-start | bytes 1179656 | tf_op jit(solution)/shard_map/ppermute | solution.py:48
  56.7 9.0 %collective-permute-start.14 = (bf16[128,1536]{1,0:T(8,128)(2,1)S(1)}, bf16[128,1536]{1,0:T(8,128)(2,1)S(1)}, u32[]{:S(2)}, u32[]{:S(2)}) collective-permute-start(bf16[128,1536]{1,0:T(8,128)(2,1)S(1)} %slice_add_fusion), channel_id=1, source_target_pairs={{0,96},{16,48},{32,64},{48,16},{64,32},{80,112},{96,0},{112,80},{1... | collective-permute-start | bytes 1179656 | tf_op jit(solution)/shard_map/ppermute | solution.py:48
  58.9 12.1 %collective-permute-start.16 = (bf16[256,1536]{1,0:T(8,128)(2,1)S(1)}, bf16[256,1536]{1,0:T(8,128)(2,1)S(1)}, u32[]{:S(2)}, u32[]{:S(2)}) collective-permute-start(bf16[256,1536]{1,0:T(8,128)(2,1)S(1)} %constant_dynamic-update-slice_fusion.4.rest_0_), channel_id=1, source_target_pairs={{0,1},{1,0},{2,3},{3,2},{4,5},{5,4},{6,7},{7,6},{8,9},{9,8},{10,11... | collective-permute-start | bytes 2359304 | tf_op jit(solution)/shard_map/ppermute | solution.py:59
  60.9 13.2 %collective-permute-start.17 = (bf16[256,1536]{1,0:T(8,128)(2,1)S(1)}, bf16[256,1536]{1,0:T(8,128)(2,1)S(1)}, u32[]{:S(2)}, u32[]{:S(2)}) collective-permute-start(bf16[256,1536]{1,0:T(8,128)(2,1)S(1)} %constant_dynamic-update-slice_fusion.4.rest_0_), channel_id=1, source_target_pairs={{0,3},{1,2},{2,1},{3,0},{4,7},{5,6},{6,5},{7,4},{8,11},{9,10},{10,... | collective-permute-start | bytes 2359304 | tf_op jit(solution)/shard_map/ppermute | solution.py:59
  61.5 24.6 %collective-permute-start.20 = (bf16[512,1536]{1,0:T(8,128)(2,1)S(1)}, bf16[512,1536]{1,0:T(8,128)(2,1)S(1)}, u32[]{:S(2)}, u32[]{:S(2)}) collective-permute-start(bf16[512,1536]{1,0:T(8,128)(2,1)S(1)} %pad_maximum_fusion.1.refs_0_), channel_id=1, source_target_pairs={{0,16},{16,0},{1,17},{17,1},{2,18},{18,2},{3,19},{19,3},{4,20},{20... | collective-permute-start | bytes 4718600 | tf_op jit(solution)/shard_map/ppermute | solution.py:63
  66.1 12.1 %collective-permute-start.15 = (bf16[128,1536]{1,0:T(8,128)(2,1)S(1)}, bf16[128,1536]{1,0:T(8,128)(2,1)S(1)}, u32[]{:S(2)}, u32[]{:S(2)}) collective-permute-start(bf16[128,1536]{1,0:T(8,128)(2,1)S(1)} %fusion.9), channel_id=1, source_target_pairs={{0,96},{16,48},{32,64},{48,16},{64,32},{80,112},{96,0},{112,80},{1... | collective-permute-start | bytes 1179656 | tf_op jit(solution)/shard_map/ppermute | solution.py:48
  68.4 9.9 %collective-permute-start.18 = (bf16[128,1536]{1,0:T(8,128)(2,1)S(1)}, bf16[128,1536]{1,0:T(8,128)(2,1)S(1)}, u32[]{:S(2)}, u32[]{:S(2)}) collective-permute-start(bf16[128,1536]{1,0:T(8,128)(2,1)S(1)} %fusion.9), channel_id=1, source_target_pairs={{0,32},{16,112},{32,0},{48,80},{64,96},{80,48},{96,64},{112,16},{1... | collective-permute-start | bytes 1179656 | tf_op jit(solution)/shard_map/ppermute | solution.py:48
  78.2 7.8 %collective-permute-start.19 = (bf16[128,1536]{1,0:T(8,128)(2,1)S(1)}, bf16[128,1536]{1,0:T(8,128)(2,1)S(1)}, u32[]{:S(2)}, u32[]{:S(2)}) collective-permute-start(bf16[128,1536]{1,0:T(8,128)(2,1)S(1)} %collective-permute-done.15), channel_id=1, source_target_pairs={{0,32},{16,112},{32,0},{48,80},{64,96},{80,48},{96,64},{112,16},{1... | collective-permute-start | bytes 1179656 | tf_op jit(solution)/shard_map/ppermute | solution.py:48
  86.1 4.5 %collective-permute-start.21 = (bf16[512,1536]{1,0:T(8,128)(2,1)S(1)}, bf16[512,1536]{1,0:T(8,128)(2,1)S(1)}, u32[]{:S(2)}, u32[]{:S(2)}) collective-permute-start(bf16[512,1536]{1,0:T(8,128)(2,1)S(1)} %pad_maximum_fusion.mine), channel_id=1, source_target_pairs={{0,16},{16,0},{1,17},{17,1},{2,18},{18,2},{3,19},{19,3},{4,20},{20... | collective-permute-start | bytes 4718600 | tf_op jit(solution)/shard_map/ppermute | solution.py:63
  86.2 20.4 %collective-permute-start.25 = (bf16[256,1536]{1,0:T(8,128)(2,1)S(1)}, bf16[256,1536]{1,0:T(8,128)(2,1)S(1)}, u32[]{:S(2)}, u32[]{:S(2)}) collective-permute-start(bf16[256,1536]{1,0:T(8,128)(2,1)S(1)} %collective-permute-done.16.rest_1_), channel_id=1, source_target_pairs={{0,3},{1,2},{2,1},{3,0},{4,7},{5,6},{6,5},{7,4},{8,11},{9,10},{10,... | collective-permute-start | bytes 2359304 | tf_op jit(solution)/shard_map/ppermute | solution.py:59
  94.0 21.8 %collective-permute-start.22 = (bf16[256,1536]{1,0:T(8,128)(2,1)S(1)}, bf16[256,1536]{1,0:T(8,128)(2,1)S(1)}, u32[]{:S(2)}, u32[]{:S(2)}) collective-permute-start(bf16[256,1536]{1,0:T(8,128)(2,1)S(1)} %get-tuple-element.48), channel_id=1, source_target_pairs={{0,4},{1,5},{2,6},{3,7},{4,8},{5,9},{6,10},{7,11},{8,12},{9,13},{1... | collective-permute-start | bytes 2359304 | tf_op jit(solution)/shard_map/ppermute | solution.py:40
  94.1 21.6 %collective-permute-start.23 = (bf16[256,1536]{1,0:T(8,128)(2,1)S(1)}, bf16[256,1536]{1,0:T(8,128)(2,1)S(1)}, u32[]{:S(2)}, u32[]{:S(2)}) collective-permute-start(bf16[256,1536]{1,0:T(8,128)(2,1)S(1)} %get-tuple-element.49), channel_id=1, source_target_pairs={{0,8},{1,9},{2,10},{3,11},{4,12},{5,13},{6,14},{7,15},{8,0},{9,1},... | collective-permute-start | bytes 2359304 | tf_op jit(solution)/shard_map/ppermute | solution.py:40
  96.5 20.1 %collective-permute-start.24 = (bf16[256,1536]{1,0:T(8,128)(2,1)S(1)}, bf16[256,1536]{1,0:T(8,128)(2,1)S(1)}, u32[]{:S(2)}, u32[]{:S(2)}) collective-permute-start(bf16[256,1536]{1,0:T(8,128)(2,1)S(1)} %get-tuple-element.50), channel_id=1, source_target_pairs={{0,12},{1,13},{2,14},{3,15},{4,0},{5,1},{6,2},{7,3},{8,4},{9,5},{1... | collective-permute-start | bytes 2359304 | tf_op jit(solution)/shard_map/ppermute | solution.py:40
  117.1 9.1 %collective-permute-start.26 = (bf16[64,1536]{1,0:T(8,128)(2,1)S(1)}, bf16[64,1536]{1,0:T(8,128)(2,1)S(1)}, u32[]{:S(2)}, u32[]{:S(2)}) collective-permute-start(bf16[64,1536]{1,0:T(8,128)(2,1)S(1)} %get-tuple-element.63), channel_id=1, source_target_pairs={{0,1},{1,2},{2,3},{3,0},{4,5},{5,6},{6,7},{7,4},{8,9},{9,10},{10,1... | collective-permute-start | bytes 589832 | tf_op jit(solution)/shard_map/ppermute | solution.py:40
  118.5 7.6 %collective-permute-start.27 = (bf16[64,1536]{1,0:T(8,128)(2,1)S(1)}, bf16[64,1536]{1,0:T(8,128)(2,1)S(1)}, u32[]{:S(2)}, u32[]{:S(2)}) collective-permute-start(bf16[64,1536]{1,0:T(8,128)(2,1)S(1)} %get-tuple-element.65), channel_id=1, source_target_pairs={{0,2},{1,3},{2,0},{3,1},{4,6},{5,7},{6,4},{7,5},{8,10},{9,11},{10,... | collective-permute-start | bytes 589832 | tf_op jit(solution)/shard_map/ppermute | solution.py:40
  120.2 6.8 %collective-permute-start.28 = (bf16[64,1536]{1,0:T(8,128)(2,1)S(1)}, bf16[64,1536]{1,0:T(8,128)(2,1)S(1)}, u32[]{:S(2)}, u32[]{:S(2)}) collective-permute-start(bf16[64,1536]{1,0:T(8,128)(2,1)S(1)} %get-tuple-element.64), channel_id=1, source_target_pairs={{0,3},{1,0},{2,1},{3,2},{4,7},{5,4},{6,5},{7,6},{8,11},{9,8},{10,9... | collective-permute-start | bytes 589832 | tf_op jit(solution)/shard_map/ppermute | solution.py:40

commit v4 on v3

--- a/solution.py
+++ b/solution.py
@@ -127,7 +127,7 @@
     @pl.loop(0, w.shape[0] // TILE, unroll=True)
     def _(n):
         columns = pl.ds(pl.multiple_of(n * TILE, TILE), TILE)
-        out = lax.dot_general(held[512:], w[columns], NT, preferred_element_type=F32)
+        out = lax.dot_general(held[768:], w[columns], NT, preferred_element_type=F32)
         other[:, columns] = out.astype(BF16)
 
 
@@ -135,7 +135,7 @@
     n, depth = weight.shape
     return pl.pallas_call(
         hidden_other_kernel,
-        out_shape=[jax.ShapeDtypeStruct((512, n), BF16), jax.ShapeDtypeStruct((1024, depth), BF16)],
+        out_shape=[jax.ShapeDtypeStruct((256, n), BF16), jax.ShapeDtypeStruct((1024, depth), BF16)],
         in_specs=[WHOLE] * 5,
         out_specs=[WHOLE] * 2,
         compiler_params=params(24),
@@ -148,19 +148,45 @@
     @pl.loop(0, w.shape[0] // TILE, unroll=True)
     def _(n):
         columns = pl.ds(pl.multiple_of(n * TILE, TILE), TILE)
-        own[:, columns] = lax.dot_general(held[:512], w[columns], NT, preferred_element_type=F32)
+        own[:, columns] = lax.dot_general(held[256:512], w[columns], NT, preferred_element_type=F32)
 
 
 def hidden_own(ordered, weight):
     n, depth = weight.shape
     return pl.pallas_call(
         hidden_own_kernel,
-        out_shape=jax.ShapeDtypeStruct((512, n), F32),
+        out_shape=jax.ShapeDtypeStruct((256, n), F32),
         in_specs=[WHOLE] * 2,
         out_specs=WHOLE,
         compiler_params=params(24),
-        cost_estimate=cost(2 * 512 * n * depth, 2 * (1024 + n) * depth + 4 * 512 * n),
+        cost_estimate=cost(2 * 256 * n * depth, 2 * (1024 + n) * depth + 4 * 256 * n),
         name="hidden_own",
+    )(ordered, weight)
+
+
+def hidden_first_kernel(held, w, other, own, rows):
+    rows[:256] = held[:256]
+    rows[256:] = held[512:768]
+
+    @pl.loop(0, w.shape[0] // TILE, unroll=True)
+    def _(n):
+        columns = pl.ds(pl.multiple_of(n * TILE, TILE), TILE)
+        out = lax.dot_general(rows[...], w[columns], NT, preferred_element_type=F32)
+        own[:, columns] = out[:256]
+        other[:, columns] = out[256:].astype(BF16)
+
+
+def hidden_first(ordered, weight):
+    n, depth = weight.shape
+    return pl.pallas_call(
+        hidden_first_kernel,
+        out_shape=[jax.ShapeDtypeStruct((256, n), BF16), jax.ShapeDtypeStruct((256, n), F32)],
+        in_specs=[WHOLE] * 2,
+        out_specs=[WHOLE] * 2,
+        scratch_shapes=[pltpu.VMEM((512, depth), BF16)],
+        compiler_params=params(24),
+        cost_estimate=cost(2 * 512 * n * depth, 2 * (1024 + n) * depth + 6 * 256 * n),
+        name="hidden_first",
     )(ordered, weight)
 
 
@@ -305,9 +331,12 @@
     pieces[1], in0, act1, act2, act3, up_weight = together(pieces[1], in0, act1, act2, act3, up_weight)
     other, ordered = hidden_other(pieces, down_weight)
     chip = hidden_own(ordered, down_weight) + swap_cores(other).astype(F32)
-    onward = chip[128:256] + pair_y(chip[384:].astype(BF16), 0).astype(F32)
+    far, last = pair_y(chip[128:].astype(BF16), 0), pair_y(chip[:128].astype(BF16), 0)
+    other, own = hidden_first(after(ordered, chip), down_weight)
+    first = own + swap_cores(other).astype(F32)
+    onward = first[128:] + far.astype(F32)
     onward, in1 = together(onward, pair_grid(after(in0, chip), 1))
-    hidden_grad = chip[:128] + pair_y(chip[256:384].astype(BF16), 0).astype(F32)
+    hidden_grad = first[:128] + last.astype(F32)
     hidden_grad = hidden_grad + pair_y(onward.astype(BF16), 1).astype(F32)
 
     gated = (gelu_slope * hidden_grad).astype(BF16)

time: 128 us -> 128 us (level)
    ppermute x5, waiting for transfers between devices: 15 us -> 10.2 us  [pair_grid(): return lax.ppermute(value, ('k', 'x', 'z'), pairs)]
    ppermute x12, waiting for transfers between devices: 13.3 us -> 16.3 us  [from_grid(): return lax.ppermute(value, ('k', 'x', 'z'), shift_grid(first, step))]
    ppermute x9, waiting for transfers between devices: 26.3 us -> 28 us  [pair_y(): return lax.ppermute(value, ('y', 'k'), pairs)]
    ppermute x9, starting transfers between devices: 11.6 us -> 13.2 us  [pair_y(): return lax.ppermute(value, ('y', 'k'), pairs)]
    pallas_call x2 -> x3, Pallas kernels: 5.51 us -> 5.7 us  [the longest x1 2.63 us: hidden_first(): pl.pallas_call(hidden_first_kernel, out_shape=[jax.ShapeDtypeStruct((256,...]
  transfers between devices with their start and end apart: 29 -> 30, of which waited for: 20 -> 20; matrix products, arithmetic and copies ran while one was open for 6% -> 6% of each run, Pallas kernels for 18% -> 17%
where the time goes in v4:
time: 128 us
  waiting for transfers between devices  55.5 us (43%)
  starting transfers between devices  36 us (28%)
  Pallas kernels  26.1 us (20%)
  other arithmetic  7.85 us (6%)
  local copies, waits for them, and re-layouts  1.44 us (1%)
    ppermute x9, waiting for transfers between devices, pair_y(): return lax.ppermute(value, ('y', 'k'), pairs)  28 us
    ppermute x12, starting transfers between devices, from_grid(): return lax.ppermute(value, ('k', 'x', 'z'), shift_grid(first, step))  18 us
    ppermute x12, waiting for transfers between devices, from_grid(): return lax.ppermute(value, ('k', 'x', 'z'), shift_grid(first, step))  16.3 us
    ppermute x9, starting transfers between devices, pair_y(): return lax.ppermute(value, ('y', 'k'), pairs)  13.2 us
    ppermute x5, waiting for transfers between devices, pair_grid(): return lax.ppermute(value, ('k', 'x', 'z'), pairs)  10.2 us
    pallas_call x1, Pallas kernels, up_gradient(): pl.pallas_call(up_kernel, grid=(m // TILE,), out_shape=jax.ShapeDtypeStru...  7.36 us
    pallas_call x1, Pallas kernels, down_gradient(): pl.pallas_call(down_kernel, grid=(m // TILE,), out_shape=jax.ShapeDtypeSt...  6.97 us
    ppermute x5, starting transfers between devices, pair_grid(): return lax.ppermute(value, ('k', 'x', 'z'), pairs)  4.4 us
  transfers between devices with their start and end apart: 30, of which 20 were waited for; matrix products, arithmetic and copies ran while one was open for 6% of the time, Pallas kernels for 17%

profile of v4, /device:TPU:0, one launch (start us, length us, event | category | flops | bytes accessed | tf_op | source)
XLA Modules:
  0.0 127.7 jit_solution(7982871191282795442)
XLA Ops:
  0.7 2.9 %collective-permute-start = (bf16[64,1536]{1,0:T(8,128)(2,1)}, bf16[64,1536]{1,0:T(8,128)(2,1)S(1)}, u32[]{:S(2)}, u32[]{:S(2)}) collective-permute-start(bf16[64,1536]{1,0:T(8,128)(2,1)} %param.9), channel_id=1, source_target_pairs={{0,12},{1,13},{2,14},{3,15},{4,0},{5,1},{6,2},{7,3},{8,4},{9,5},{1... | collective-permute-start | bytes 589832 | tf_op jit(solution)/shard_map/ppermute | solution.py:40
  3.6 0.8 collective-permute-start.1
  4.4 0.9 collective-permute-start.2
  5.3 1.2 fusion.10
  6.4 0.9 constant_dynamic-update-slice_fusion.3
  7.4 1.8 %collective-permute-done = bf16[64,1536]{1,0:T(8,128)(2,1)S(1)} collective-permute-done((bf16[64,1536]{1,0:T(8,128)(2,1)}, bf16[64,1536]{1,0:T(8,128)(2,1)S(1)}, u32[]{:S(2)}, u32[]{:S(2)}) %collective-permute-start) | collective-permute-done | bytes 196640 | tf_op jit(solution)/shard_map/ppermute | solution.py:40
  9.2 1.8 %collective-permute-done.1 = bf16[64,1536]{1,0:T(8,128)(2,1)S(1)} collective-permute-done((bf16[64,1536]{1,0:T(8,128)(2,1)}, bf16[64,1536]{1,0:T(8,128)(2,1)S(1)}, u32[]{:S(2)}, u32[]{:S(2)}) %collective-permute-start.1) | collective-permute-done | bytes 196640 | tf_op jit(solution)/shard_map/ppermute | solution.py:40
  11.1 2.0 %collective-permute-done.2 = bf16[64,1536]{1,0:T(8,128)(2,1)S(1)} collective-permute-done((bf16[64,1536]{1,0:T(8,128)(2,1)}, bf16[64,1536]{1,0:T(8,128)(2,1)S(1)}, u32[]{:S(2)}, u32[]{:S(2)}) %collective-permute-start.2) | collective-permute-done | bytes 196640 | tf_op jit(solution)/shard_map/ppermute | solution.py:40
  13.1 4.1 %collective-permute-start.3 = (bf16[256,1536]{1,0:T(8,128)(2,1)S(1)}, bf16[256,1536]{1,0:T(8,128)(2,1)S(1)}, u32[]{:S(2)}, u32[]{:S(2)}) collective-permute-start(bf16[256,1536]{1,0:T(8,128)(2,1)S(1)} %constant_dynamic-update-slice_fusion.p0), channel_id=1, source_target_pairs={{0,3},{1,0},{2,1},{3,2},{4,7},{5,4},{6,5},{7,6},{8,11},{9,8},{10,9... | collective-permute-start | bytes 2359304 | tf_op jit(solution)/shard_map/ppermute | solution.py:40
  17.2 1.3 collective-permute-start.9
  18.5 3.0 %collective-permute-start.5 = (bf16[128,1536]{1,0:T(8,128)(2,1)S(1)}, bf16[128,1536]{1,0:T(8,128)(2,1)S(1)}, u32[]{:S(2)}, u32[]{:S(2)}) collective-permute-start(bf16[128,1536]{1,0:T(8,128)(2,1)S(1)} %fusion.10), channel_id=1, source_target_pairs={{0,96},{16,48},{32,64},{48,16},{64,32},{80,112},{96,0},{112,80},{1... | collective-permute-start | bytes 1179656 | tf_op jit(solution)/shard_map/ppermute | solution.py:48
  21.5 4.8 %collective-permute-done.4 = bf16[64,1536]{1,0:T(8,128)(2,1)S(1)} collective-permute-done((bf16[64,1536]{1,0:T(8,128)(2,1)S(1)}, bf16[64,1536]{1,0:T(8,128)(2,1)S(1)}, u32[]{:S(2)}, u32[]{:S(2)}) %collective-permute-start.4) | collective-permute-done | bytes 196640 | tf_op jit(solution)/shard_map/ppermute | solution.py:59
  26.3 1.6 %collective-permute-start.6 = (bf16[128,1536]{1,0:T(8,128)(2,1)S(1)}, bf16[128,1536]{1,0:T(8,128)(2,1)S(1)}, u32[]{:S(2)}, u32[]{:S(2)}) collective-permute-start(bf16[128,1536]{1,0:T(8,128)(2,1)S(1)} %fusion.10), channel_id=1, source_target_pairs={{0,32},{16,112},{32,0},{48,80},{64,96},{80,48},{96,64},{112,16},{1... | collective-permute-start | bytes 1179656 | tf_op jit(solution)/shard_map/ppermute | solution.py:48
  28.4 3.4 %fusion.1.w = bf16[1536,1536]{1,0:T(8,128)(2,1)S(1)} fusion(bf16[1536,1536]{1,0:T(8,128)(2,1)} %param.10, f32[48,1536]{1,0:T(8,128)S(1)} %multiply_exponential_fusion.1), kind=kLoop, calls=%fused_computation.3 | loop fusion | flops 7077888 | bytes 9732096 | tf_op jit(solution)/shard_map/convert_element_type | solution.py:17
  32.0 0.9 fusion.w
  33.0 1.1 collective-permute-done.6
  34.1 4.2 %collective-permute-done.7 = bf16[128,1536]{1,0:T(8,128)(2,1)S(1)} collective-permute-done((bf16[128,1536]{1,0:T(8,128)(2,1)S(1)}, bf16[128,1536]{1,0:T(8,128)(2,1)S(1)}, u32[]{:S(2)}, u32[]{:S(2)}) %collective-permute-start.7) | collective-permute-done | bytes 393248 | tf_op jit(solution)/shard_map/ppermute | solution.py:48
  38.3 0.5 collective-permute-done.9.p3
  38.8 1.7 %hidden_other.1 = (bf16[256,1536]{1,0:T(8,128)(2,1)S(1)}, bf16[1024,1536]{1,0:T(8,128)(2,1)S(1)}) custom-call(bf16[256,1536]{1,0:T(8,128)(2,1)S(1)} %constant_dynamic-update-slice_fusion.p0, bf16[256,1536]{1,0:T(8,128)(2,1)S(1)} %collective-permute-done.3.p1, bf16[256,1536]{1,0:T(8,128)(2,1)S(1)} %collective-permute-done.8.p2, ...), custom_call_target="tpu_custom_call" | custom-call | flops 2415919104 | bytes 9437184 | tf_op jit(solution)/shard_map/hidden_other/pallas_call | solution.py:136
  40.6 1.4 %hidden_own.1 = f32[256,1536]{1,0:T(8,128)S(1)} custom-call(bf16[1024,1536]{1,0:T(8,128)(2,1)S(1)} %get-tuple-element.39.held.refs_2_, bf16[1536,1536]{1,0:T(8,128)(2,1)S(1)} %fusion.w), custom_call_target="tpu_custom_call" | custom-call | flops 1207959552 | bytes 9437184 | tf_op jit(solution)/shard_map/hidden_own/pallas_call | solution.py:156
  42.0 0.9 collective-permute-done.10
  43.0 2.6 %hidden_first.1 = (bf16[256,1536]{1,0:T(8,128)(2,1)S(1)}, f32[256,1536]{1,0:T(8,128)S(1)}) custom-call(bf16[1024,1536]{1,0:T(8,128)(2,1)S(1)} %get-tuple-element.39.held.refs_2_, bf16[1536,1536]{1,0:T(8,128)(2,1)S(1)} %fusion.w), custom_call_target="tpu_custom_call" | custom-call | flops 2415919104 | bytes 10223616 | tf_op jit(solution)/shard_map/hidden_first/pallas_call | solution.py:181
  46.0 0.7 collective-permute-start.14
  46.7 1.7 %collective-permute-start.13 = (bf16[128,1536]{1,0:T(8,128)(2,1)S(1)}, bf16[128,1536]{1,0:T(8,128)(2,1)S(1)}, u32[]{:S(2)}, u32[]{:S(2)}) collective-permute-start(bf16[128,1536]{1,0:T(8,128)(2,1)S(1)} %get-tuple-element.69), channel_id=1, source_target_pairs={{0,32},{16,112},{32,0},{48,80},{64,96},{80,48},{96,64},{112,16},{1... | collective-permute-start | bytes 1179656 | tf_op jit(solution)/shard_map/ppermute | solution.py:48
  49.0 5.5 %collective-permute-done.13 = bf16[128,1536]{1,0:T(8,128)(2,1)S(1)} collective-permute-done((bf16[128,1536]{1,0:T(8,128)(2,1)S(1)}, bf16[128,1536]{1,0:T(8,128)(2,1)S(1)}, u32[]{:S(2)}, u32[]{:S(2)}) %collective-permute-start.13) | collective-permute-done | bytes 393248 | tf_op jit(solution)/shard_map/ppermute | solution.py:48
  55.1 3.0 %collective-permute-start.15 = (bf16[128,1536]{1,0:T(8,128)(2,1)S(1)}, bf16[128,1536]{1,0:T(8,128)(2,1)S(1)}, u32[]{:S(2)}, u32[]{:S(2)}) collective-permute-start(bf16[128,1536]{1,0:T(8,128)(2,1)S(1)} %slice_add_fusion), channel_id=1, source_target_pairs={{0,96},{16,48},{32,64},{48,16},{64,32},{80,112},{96,0},{112,80},{1... | collective-permute-start | bytes 1179656 | tf_op jit(solution)/shard_map/ppermute | solution.py:48
  58.1 1.9 %collective-permute-start.17 = (bf16[256,1536]{1,0:T(8,128)(2,1)S(1)}, bf16[256,1536]{1,0:T(8,128)(2,1)S(1)}, u32[]{:S(2)}, u32[]{:S(2)}) collective-permute-start(bf16[256,1536]{1,0:T(8,128)(2,1)S(1)} %constant_dynamic-update-slice_fusion.4.rest_0_), channel_id=1, source_target_pairs={{0,1},{1,0},{2,3},{3,2},{4,5},{5,4},{6,7},{7,6},{8,9},{9,8},{10,11... | collective-permute-start | bytes 2359304 | tf_op jit(solution)/shard_map/ppermute | solution.py:59
  60.1 0.5 collective-permute-start.18
  60.6 4.2 %collective-permute-done.15 = bf16[128,1536]{1,0:T(8,128)(2,1)S(1)} collective-permute-done((bf16[128,1536]{1,0:T(8,128)(2,1)S(1)}, bf16[128,1536]{1,0:T(8,128)(2,1)S(1)}, u32[]{:S(2)}, u32[]{:S(2)}) %collective-permute-start.15) | collective-permute-done | bytes 393248 | tf_op jit(solution)/shard_map/ppermute | solution.py:48
  65.2 3.0 %collective-permute-start.16 = (bf16[128,1536]{1,0:T(8,128)(2,1)S(1)}, bf16[128,1536]{1,0:T(8,128)(2,1)S(1)}, u32[]{:S(2)}, u32[]{:S(2)}) collective-permute-start(bf16[128,1536]{1,0:T(8,128)(2,1)S(1)} %fusion.9), channel_id=1, source_target_pairs={{0,96},{16,48},{32,64},{48,16},{64,32},{80,112},{96,0},{112,80},{1... | collective-permute-start | bytes 1179656 | tf_op jit(solution)/shard_map/ppermute | solution.py:48
  68.2 2.0 %collective-permute-done.17.rest_1_ = bf16[256,1536]{1,0:T(8,128)(2,1)S(1)} collective-permute-done((bf16[256,1536]{1,0:T(8,128)(2,1)S(1)}, bf16[256,1536]{1,0:T(8,128)(2,1)S(1)}, u32[]{:S(2)}, u32[]{:S(2)}) %collective-permute-start.17) | collective-permute-done | bytes 786464 | tf_op jit(solution)/shard_map/ppermute | solution.py:59
  70.2 3.0 %collective-permute-done.18.rest_2_ = bf16[256,1536]{1,0:T(8,128)(2,1)S(1)} collective-permute-done((bf16[256,1536]{1,0:T(8,128)(2,1)S(1)}, bf16[256,1536]{1,0:T(8,128)(2,1)S(1)}, u32[]{:S(2)}, u32[]{:S(2)}) %collective-permute-start.18) | collective-permute-done | bytes 786464 | tf_op jit(solution)/shard_map/ppermute | solution.py:59
  73.3 5.2 %collective-permute-done.16 = bf16[128,1536]{1,0:T(8,128)(2,1)S(1)} collective-permute-done((bf16[128,1536]{1,0:T(8,128)(2,1)S(1)}, bf16[128,1536]{1,0:T(8,128)(2,1)S(1)}, u32[]{:S(2)}, u32[]{:S(2)}) %collective-permute-start.16) | collective-permute-done | bytes 393248 | tf_op jit(solution)/shard_map/ppermute | solution.py:48
  78.5 7.8 %collective-permute-done.20 = bf16[128,1536]{1,0:T(8,128)(2,1)S(1)} collective-permute-done((bf16[128,1536]{1,0:T(8,128)(2,1)S(1)}, bf16[128,1536]{1,0:T(8,128)(2,1)S(1)}, u32[]{:S(2)}, u32[]{:S(2)}) %collective-permute-start.20) | collective-permute-done | bytes 393248 | tf_op jit(solution)/shard_map/ppermute | solution.py:48
  86.5 1.3 %collective-permute-start.26 = (bf16[256,1536]{1,0:T(8,128)(2,1)S(1)}, bf16[256,1536]{1,0:T(8,128)(2,1)S(1)}, u32[]{:S(2)}, u32[]{:S(2)}) collective-permute-start(bf16[256,1536]{1,0:T(8,128)(2,1)S(1)} %collective-permute-done.17.rest_1_), channel_id=1, source_target_pairs={{0,3},{1,2},{2,1},{3,0},{4,7},{5,6},{6,5},{7,4},{8,11},{9,10},{10,... | collective-permute-start | bytes 2359304 | tf_op jit(solution)/shard_map/ppermute | solution.py:59
  87.8 2.6 %input_own.1.own = f32[512,1536]{1,0:T(8,128)S(1)} custom-call(bf16[512,1536]{1,0:T(8,128)(2,1)S(1)} %pad_maximum_fusion.mine, bf16[1536,1536]{1,0:T(8,128)(2,1)S(1)} %fusion.1.w), custom_call_target="tpu_custom_call" | custom-call | flops 2415919104 | bytes 9437184 | tf_op jit(solution)/shard_map/input_own/pallas_call | solution.py:202
  90.5 3.4 %input_all.1 = (f32[256,1536]{1,0:T(8,128)S(1)}, bf16[256,1536]{1,0:T(8,128)(2,1)S(1)}, bf16[256,1536]{1,0:T(8,128)(2,1)S(1)}, bf16[256,1536]{1,0:T(8,128)(2,1)S(1)}) custom-call(bf16[512,1536]{1,0:T(8,128)(2,1)S(1)} %collective-permute-done.22.theirs, bf16[1536,1536]{1,0:T(8,128)(2,1)S(1)} %fusion.1.w, f32[512,1536]{1,0:T(8,128)S(1)} %input_own.1.own), custom_call_target="tpu_custom_call" | custom-call | flops 2415919104 | bytes 12582912 | tf_op jit(solution)/shard_map/input_all/pallas_call | solution.py:227
  93.9 3.0 %collective-permute-start.24 = (bf16[256,1536]{1,0:T(8,128)(2,1)S(1)}, bf16[256,1536]{1,0:T(8,128)(2,1)S(1)}, u32[]{:S(2)}, u32[]{:S(2)}) collective-permute-start(bf16[256,1536]{1,0:T(8,128)(2,1)S(1)} %get-tuple-element.55), channel_id=1, source_target_pairs={{0,8},{1,9},{2,10},{3,11},{4,12},{5,13},{6,14},{7,15},{8,0},{9,1},... | collective-permute-start | bytes 2359304 | tf_op jit(solution)/shard_map/ppermute | solution.py:40
  97.4 7.0 %down_gradient.1 = bf16[1536,1536]{1,0:T(8,128)(2,1)} custom-call(bf16[512,1536]{1,0:T(8,128)(2,1)S(1)} %pad_maximum_fusion.1.refs_0_, bf16[512,1536]{1,0:T(8,128)(2,1)S(1)} %collective-permute-done.21.refs_1_, bf16[1024,1536]{1,0:T(8,128)(2,1)S(1)} %get-tuple-element.39.held.refs_2_), custom_call_target="tpu_custom_call" | custom-call | flops 4831838208 | bytes 11010048 | tf_op jit(solution)/shard_map/down_gradient/pallas_call | solution.py:253
  104.4 7.4 %up_gradient.1 = bf16[1536,1536]{1,0:T(8,128)(2,1)} custom-call(bf16[512,1536]{1,0:T(8,128)(2,1)S(1)} %pad_maximum_fusion.mine, bf16[512,1536]{1,0:T(8,128)(2,1)S(1)} %collective-permute-done.22.theirs, bf16[256,1536]{1,0:T(8,128)(2,1)S(1)} %constant_dynamic-update-slice_fusion.4.rest_0_, bf16[256,1536]{1,0:T(8,128)(2,1)S(1)} %collective-permute-done.17.rest_1_, ...), custom_call_target="tpu_custom_call" | custom-call | flops 4831838208 | bytes 11010048 | tf_op jit(solution)/shard_map/up_gradient/pallas_call | solution.py:285
  111.7 4.3 %collective-permute-done.23 = bf16[256,1536]{1,0:T(8,128)(2,1)S(1)} collective-permute-done((bf16[256,1536]{1,0:T(8,128)(2,1)S(1)}, bf16[256,1536]{1,0:T(8,128)(2,1)S(1)}, u32[]{:S(2)}, u32[]{:S(2)}) %collective-permute-start.23) | collective-permute-done | bytes 786464 | tf_op jit(solution)/shard_map/ppermute | solution.py:40
  117.0 0.7 collective-permute-start.27
  117.7 2.8 %collective-permute-start.28 = (bf16[64,1536]{1,0:T(8,128)(2,1)S(1)}, bf16[64,1536]{1,0:T(8,128)(2,1)S(1)}, u32[]{:S(2)}, u32[]{:S(2)}) collective-permute-start(bf16[64,1536]{1,0:T(8,128)(2,1)S(1)} %get-tuple-element.67), channel_id=1, source_target_pairs={{0,2},{1,3},{2,0},{3,1},{4,6},{5,7},{6,4},{7,5},{8,10},{9,11},{10,... | collective-permute-start | bytes 589832 | tf_op jit(solution)/shard_map/ppermute | solution.py:40
  120.5 1.0 collective-permute-start.29
  121.5 2.4 %collective-permute-done.27 = bf16[64,1536]{1,0:T(8,128)(2,1)S(1)} collective-permute-done((bf16[64,1536]{1,0:T(8,128)(2,1)S(1)}, bf16[64,1536]{1,0:T(8,128)(2,1)S(1)}, u32[]{:S(2)}, u32[]{:S(2)}) %collective-permute-start.27) | collective-permute-done | bytes 196640 | tf_op jit(solution)/shard_map/ppermute | solution.py:40
  123.9 2.3 %collective-permute-done.28 = bf16[64,1536]{1,0:T(8,128)(2,1)S(1)} collective-permute-done((bf16[64,1536]{1,0:T(8,128)(2,1)S(1)}, bf16[64,1536]{1,0:T(8,128)(2,1)S(1)}, u32[]{:S(2)}, u32[]{:S(2)}) %collective-permute-start.28) | collective-permute-done | bytes 196640 | tf_op jit(solution)/shard_map/ppermute | solution.py:40
  126.2 0.7 collective-permute-done.29
  126.9 0.8 add_convert_fusion
  (55 shorter events, 4.8 us)
Async XLA Ops:
  0.6 17.8 %copy-start.3 = (bf16[64,1536]{1,0:T(8,128)(2,1)S(1)}, bf16[64,1536]{1,0:T(8,128)(2,1)}, u32[]{:S(2)}) copy-start(bf16[64,1536]{1,0:T(8,128)(2,1)} %param.7) | copy-start | bytes 589828
  0.6 20.8 %copy-start.1 = (s32[48,1536]{1,0:T(8,128)S(1)}, s32[48,1536]{1,0:T(8,128)}, u32[]{:S(2)}) copy-start(s32[48,1536]{1,0:T(8,128)} %param.11) | copy-start | bytes 884740
  0.7 27.7 %copy-start.2 = (s32[48,1536]{1,0:T(8,128)S(1)}, s32[48,1536]{1,0:T(8,128)}, u32[]{:S(2)}) copy-start(s32[48,1536]{1,0:T(8,128)} %param.13) | copy-start | bytes 884740
  0.7 8.6 %collective-permute-start = (bf16[64,1536]{1,0:T(8,128)(2,1)}, bf16[64,1536]{1,0:T(8,128)(2,1)S(1)}, u32[]{:S(2)}, u32[]{:S(2)}) collective-permute-start(bf16[64,1536]{1,0:T(8,128)(2,1)} %param.9), channel_id=1, source_target_pairs={{0,12},{1,13},{2,14},{3,15},{4,0},{5,1},{6,2},{7,3},{8,4},{9,5},{1... | collective-permute-start | bytes 589832 | tf_op jit(solution)/shard_map/ppermute | solution.py:40
  3.6 7.5 %collective-permute-start.1 = (bf16[64,1536]{1,0:T(8,128)(2,1)}, bf16[64,1536]{1,0:T(8,128)(2,1)S(1)}, u32[]{:S(2)}, u32[]{:S(2)}) collective-permute-start(bf16[64,1536]{1,0:T(8,128)(2,1)} %param.9), channel_id=1, source_target_pairs={{0,8},{1,9},{2,10},{3,11},{4,12},{5,13},{6,14},{7,15},{8,0},{9,1},... | collective-permute-start | bytes 589832 | tf_op jit(solution)/shard_map/ppermute | solution.py:40
  4.4 8.7 %collective-permute-start.2 = (bf16[64,1536]{1,0:T(8,128)(2,1)}, bf16[64,1536]{1,0:T(8,128)(2,1)S(1)}, u32[]{:S(2)}, u32[]{:S(2)}) collective-permute-start(bf16[64,1536]{1,0:T(8,128)(2,1)} %param.9), channel_id=1, source_target_pairs={{0,4},{1,5},{2,6},{3,7},{4,8},{5,9},{6,10},{7,11},{8,12},{9,13},{1... | collective-permute-start | bytes 589832 | tf_op jit(solution)/shard_map/ppermute | solution.py:40
  13.1 25.2 %collective-permute-start.3 = (bf16[256,1536]{1,0:T(8,128)(2,1)S(1)}, bf16[256,1536]{1,0:T(8,128)(2,1)S(1)}, u32[]{:S(2)}, u32[]{:S(2)}) collective-permute-start(bf16[256,1536]{1,0:T(8,128)(2,1)S(1)} %constant_dynamic-update-slice_fusion.p0), channel_id=1, source_target_pairs={{0,3},{1,0},{2,1},{3,2},{4,7},{5,4},{6,5},{7,6},{8,11},{9,8},{10,9... | collective-permute-start | bytes 2359304 | tf_op jit(solution)/shard_map/ppermute | solution.py:40
  17.2 21.1 %collective-permute-start.8 = (bf16[256,1536]{1,0:T(8,128)(2,1)S(1)}, bf16[256,1536]{1,0:T(8,128)(2,1)S(1)}, u32[]{:S(2)}, u32[]{:S(2)}) collective-permute-start(bf16[256,1536]{1,0:T(8,128)(2,1)S(1)} %constant_dynamic-update-slice_fusion.p0), channel_id=1, source_target_pairs={{0,2},{1,3},{2,0},{3,1},{4,6},{5,7},{6,4},{7,5},{8,10},{9,11},{10,... | collective-permute-start | bytes 2359304 | tf_op jit(solution)/shard_map/ppermute | solution.py:40
  17.2 21.6 %collective-permute-start.9 = (bf16[256,1536]{1,0:T(8,128)(2,1)S(1)}, bf16[256,1536]{1,0:T(8,128)(2,1)S(1)}, u32[]{:S(2)}, u32[]{:S(2)}) collective-permute-start(bf16[256,1536]{1,0:T(8,128)(2,1)S(1)} %constant_dynamic-update-slice_fusion.p0), channel_id=1, source_target_pairs={{0,1},{1,2},{2,3},{3,0},{4,5},{5,6},{6,7},{7,4},{8,9},{9,10},{10,1... | collective-permute-start | bytes 2359304 | tf_op jit(solution)/shard_map/ppermute | solution.py:40
  18.5 7.8 %collective-permute-start.4 = (bf16[64,1536]{1,0:T(8,128)(2,1)S(1)}, bf16[64,1536]{1,0:T(8,128)(2,1)S(1)}, u32[]{:S(2)}, u32[]{:S(2)}) collective-permute-start(bf16[64,1536]{1,0:T(8,128)(2,1)S(1)} %copy-done.3), channel_id=1, source_target_pairs={{0,4},{1,5},{2,6},{3,7},{4,0},{5,1},{6,2},{7,3},{8,12},{9,13},{10,... | collective-permute-start | bytes 589832 | tf_op jit(solution)/shard_map/ppermute | solution.py:59
  18.5 9.4 %collective-permute-start.5 = (bf16[128,1536]{1,0:T(8,128)(2,1)S(1)}, bf16[128,1536]{1,0:T(8,128)(2,1)S(1)}, u32[]{:S(2)}, u32[]{:S(2)}) collective-permute-start(bf16[128,1536]{1,0:T(8,128)(2,1)S(1)} %fusion.10), channel_id=1, source_target_pairs={{0,96},{16,48},{32,64},{48,16},{64,32},{80,112},{96,0},{112,80},{1... | collective-permute-start | bytes 1179656 | tf_op jit(solution)/shard_map/ppermute | solution.py:48
  26.3 7.8 %collective-permute-start.6 = (bf16[128,1536]{1,0:T(8,128)(2,1)S(1)}, bf16[128,1536]{1,0:T(8,128)(2,1)S(1)}, u32[]{:S(2)}, u32[]{:S(2)}) collective-permute-start(bf16[128,1536]{1,0:T(8,128)(2,1)S(1)} %fusion.10), channel_id=1, source_target_pairs={{0,32},{16,112},{32,0},{48,80},{64,96},{80,48},{96,64},{112,16},{1... | collective-permute-start | bytes 1179656 | tf_op jit(solution)/shard_map/ppermute | solution.py:48
  27.9 10.4 %collective-permute-start.7 = (bf16[128,1536]{1,0:T(8,128)(2,1)S(1)}, bf16[128,1536]{1,0:T(8,128)(2,1)S(1)}, u32[]{:S(2)}, u32[]{:S(2)}) collective-permute-start(bf16[128,1536]{1,0:T(8,128)(2,1)S(1)} %collective-permute-done.5), channel_id=1, source_target_pairs={{0,32},{16,112},{32,0},{48,80},{64,96},{80,48},{96,64},{112,16},{1... | collective-permute-start | bytes 1179656 | tf_op jit(solution)/shard_map/ppermute | solution.py:48
  28.3 3.6 %slice-start = ((s8[4718592]{0:T(1024)(128)(4,1)}), s8[4194304]{0:T(1024)(128)(4,1)S(1)}, s32[]{:S(2)}) async-start(s8[4718592]{0:T(1024)(128)(4,1)} %bitcast.8), calls=%async_computation | async-start | bytes 8388608
  28.4 3.7 %slice-start.1 = ((s8[4718592]{0:T(1024)(128)(4,1)}), s8[524288]{0:T(1024)(128)(4,1)S(1)}, s32[]{:S(2)}) async-start(s8[4718592]{0:T(1024)(128)(4,1)} %bitcast.8), calls=%async_computation.1 | async-start | bytes 1048576
  40.5 2.4 %collective-permute-start.10 = (bf16[256,1536]{1,0:T(8,128)(2,1)S(1)}, bf16[256,1536]{1,0:T(8,128)(2,1)S(1)}, u32[]{:S(2)}, u32[]{:S(2)}) collective-permute-start(bf16[256,1536]{1,0:T(8,128)(2,1)S(1)} %get-tuple-element.38), channel_id=1, source_target_pairs={{0,16},{16,0},{1,17},{17,1},{2,18},{18,2},{3,19},{19,3},{4,20},{20... | collective-permute-start | bytes 2359304 | tf_op jit(solution)/shard_map/ppermute | solution.py:63
  45.7 3.1 %collective-permute-start.11 = (bf16[256,1536]{1,0:T(8,128)(2,1)S(1)}, bf16[256,1536]{1,0:T(8,128)(2,1)S(1)}, u32[]{:S(2)}, u32[]{:S(2)}) collective-permute-start(bf16[256,1536]{1,0:T(8,128)(2,1)S(1)} %get-tuple-element.41), channel_id=1, source_target_pairs={{0,16},{16,0},{1,17},{17,1},{2,18},{18,2},{3,19},{19,3},{4,20},{20... | collective-permute-start | bytes 2359304 | tf_op jit(solution)/shard_map/ppermute | solution.py:63
  46.0 9.1 %collective-permute-start.14 = (bf16[128,1536]{1,0:T(8,128)(2,1)S(1)}, bf16[128,1536]{1,0:T(8,128)(2,1)S(1)}, u32[]{:S(2)}, u32[]{:S(2)}) collective-permute-start(bf16[128,1536]{1,0:T(8,128)(2,1)S(1)} %pad_maximum_fusion.2), channel_id=1, source_target_pairs={{0,12},{1,13},{2,14},{3,15},{4,8},{5,9},{6,10},{7,11},{8,4},{9,5},... | collective-permute-start | bytes 1179656 | tf_op jit(solution)/shard_map/ppermute | solution.py:59
  46.7 7.9 %collective-permute-start.13 = (bf16[128,1536]{1,0:T(8,128)(2,1)S(1)}, bf16[128,1536]{1,0:T(8,128)(2,1)S(1)}, u32[]{:S(2)}, u32[]{:S(2)}) collective-permute-start(bf16[128,1536]{1,0:T(8,128)(2,1)S(1)} %get-tuple-element.69), channel_id=1, source_target_pairs={{0,32},{16,112},{32,0},{48,80},{64,96},{80,48},{96,64},{112,16},{1... | collective-permute-start | bytes 1179656 | tf_op jit(solution)/shard_map/ppermute | solution.py:48
  48.4 12.2 %collective-permute-start.12 = (bf16[128,1536]{1,0:T(8,128)(2,1)S(1)}, bf16[128,1536]{1,0:T(8,128)(2,1)S(1)}, u32[]{:S(2)}, u32[]{:S(2)}) collective-permute-start(bf16[128,1536]{1,0:T(8,128)(2,1)S(1)} %get-tuple-element.68), channel_id=1, source_target_pairs={{0,32},{16,112},{32,0},{48,80},{64,96},{80,48},{96,64},{112,16},{1... | collective-permute-start | bytes 1179656 | tf_op jit(solution)/shard_map/ppermute | solution.py:48
  49.0 15.7 %copy-start = (bf16[128,1536]{1,0:T(8,128)(2,1)S(1)}, bf16[128,1536]{1,0:T(8,128)(2,1)}, u32[]{:S(2)}) copy-start(bf16[128,1536]{1,0:T(8,128)(2,1)} %param.8) | copy-start | bytes 1179652
  55.1 9.6 %collective-permute-start.15 = (bf16[128,1536]{1,0:T(8,128)(2,1)S(1)}, bf16[128,1536]{1,0:T(8,128)(2,1)S(1)}, u32[]{:S(2)}, u32[]{:S(2)}) collective-permute-start(bf16[128,1536]{1,0:T(8,128)(2,1)S(1)} %slice_add_fusion), channel_id=1, source_target_pairs={{0,96},{16,48},{32,64},{48,16},{64,32},{80,112},{96,0},{112,80},{1... | collective-permute-start | bytes 1179656 | tf_op jit(solution)/shard_map/ppermute | solution.py:48
  58.1 12.1 %collective-permute-start.17 = (bf16[256,1536]{1,0:T(8,128)(2,1)S(1)}, bf16[256,1536]{1,0:T(8,128)(2,1)S(1)}, u32[]{:S(2)}, u32[]{:S(2)}) collective-permute-start(bf16[256,1536]{1,0:T(8,128)(2,1)S(1)} %constant_dynamic-update-slice_fusion.4.rest_0_), channel_id=1, source_target_pairs={{0,1},{1,0},{2,3},{3,2},{4,5},{5,4},{6,7},{7,6},{8,9},{9,8},{10,11... | collective-permute-start | bytes 2359304 | tf_op jit(solution)/shard_map/ppermute | solution.py:59
  60.1 13.2 %collective-permute-start.18 = (bf16[256,1536]{1,0:T(8,128)(2,1)S(1)}, bf16[256,1536]{1,0:T(8,128)(2,1)S(1)}, u32[]{:S(2)}, u32[]{:S(2)}) collective-permute-start(bf16[256,1536]{1,0:T(8,128)(2,1)S(1)} %constant_dynamic-update-slice_fusion.4.rest_0_), channel_id=1, source_target_pairs={{0,3},{1,2},{2,1},{3,0},{4,7},{5,6},{6,5},{7,4},{8,11},{9,10},{10,... | collective-permute-start | bytes 2359304 | tf_op jit(solution)/shard_map/ppermute | solution.py:59
  60.5 25.8 %collective-permute-start.21 = (bf16[512,1536]{1,0:T(8,128)(2,1)S(1)}, bf16[512,1536]{1,0:T(8,128)(2,1)S(1)}, u32[]{:S(2)}, u32[]{:S(2)}) collective-permute-start(bf16[512,1536]{1,0:T(8,128)(2,1)S(1)} %pad_maximum_fusion.1.refs_0_), channel_id=1, source_target_pairs={{0,16},{16,0},{1,17},{17,1},{2,18},{18,2},{3,19},{19,3},{4,20},{20... | collective-permute-start | bytes 4718600 | tf_op jit(solution)/shard_map/ppermute | solution.py:63
  65.2 13.3 %collective-permute-start.16 = (bf16[128,1536]{1,0:T(8,128)(2,1)S(1)}, bf16[128,1536]{1,0:T(8,128)(2,1)S(1)}, u32[]{:S(2)}, u32[]{:S(2)}) collective-permute-start(bf16[128,1536]{1,0:T(8,128)(2,1)S(1)} %fusion.9), channel_id=1, source_target_pairs={{0,96},{16,48},{32,64},{48,16},{64,32},{80,112},{96,0},{112,80},{1... | collective-permute-start | bytes 1179656 | tf_op jit(solution)/shard_map/ppermute | solution.py:48
  68.2 10.3 %collective-permute-start.19 = (bf16[128,1536]{1,0:T(8,128)(2,1)S(1)}, bf16[128,1536]{1,0:T(8,128)(2,1)S(1)}, u32[]{:S(2)}, u32[]{:S(2)}) collective-permute-start(bf16[128,1536]{1,0:T(8,128)(2,1)S(1)} %fusion.9), channel_id=1, source_target_pairs={{0,32},{16,112},{32,0},{48,80},{64,96},{80,48},{96,64},{112,16},{1... | collective-permute-start | bytes 1179656 | tf_op jit(solution)/shard_map/ppermute | solution.py:48
  78.5 7.8 %collective-permute-start.20 = (bf16[128,1536]{1,0:T(8,128)(2,1)S(1)}, bf16[128,1536]{1,0:T(8,128)(2,1)S(1)}, u32[]{:S(2)}, u32[]{:S(2)}) collective-permute-start(bf16[128,1536]{1,0:T(8,128)(2,1)S(1)} %collective-permute-done.16), channel_id=1, source_target_pairs={{0,32},{16,112},{32,0},{48,80},{64,96},{80,48},{96,64},{112,16},{1... | collective-permute-start | bytes 1179656 | tf_op jit(solution)/shard_map/ppermute | solution.py:48
  86.4 4.1 %collective-permute-start.22 = (bf16[512,1536]{1,0:T(8,128)(2,1)S(1)}, bf16[512,1536]{1,0:T(8,128)(2,1)S(1)}, u32[]{:S(2)}, u32[]{:S(2)}) collective-permute-start(bf16[512,1536]{1,0:T(8,128)(2,1)S(1)} %pad_maximum_fusion.mine), channel_id=1, source_target_pairs={{0,16},{16,0},{1,17},{17,1},{2,18},{18,2},{3,19},{19,3},{4,20},{20... | collective-permute-start | bytes 4718600 | tf_op jit(solution)/shard_map/ppermute | solution.py:63
  86.5 17.9 %collective-permute-start.26 = (bf16[256,1536]{1,0:T(8,128)(2,1)S(1)}, bf16[256,1536]{1,0:T(8,128)(2,1)S(1)}, u32[]{:S(2)}, u32[]{:S(2)}) collective-permute-start(bf16[256,1536]{1,0:T(8,128)(2,1)S(1)} %collective-permute-done.17.rest_1_), channel_id=1, source_target_pairs={{0,3},{1,2},{2,1},{3,0},{4,7},{5,6},{6,5},{7,4},{8,11},{9,10},{10,... | collective-permute-start | bytes 2359304 | tf_op jit(solution)/shard_map/ppermute | solution.py:59
  93.9 22.2 %collective-permute-start.23 = (bf16[256,1536]{1,0:T(8,128)(2,1)S(1)}, bf16[256,1536]{1,0:T(8,128)(2,1)S(1)}, u32[]{:S(2)}, u32[]{:S(2)}) collective-permute-start(bf16[256,1536]{1,0:T(8,128)(2,1)S(1)} %get-tuple-element.54), channel_id=1, source_target_pairs={{0,4},{1,5},{2,6},{3,7},{4,8},{5,9},{6,10},{7,11},{8,12},{9,13},{1... | collective-permute-start | bytes 2359304 | tf_op jit(solution)/shard_map/ppermute | solution.py:40
  93.9 22.1 %collective-permute-start.24 = (bf16[256,1536]{1,0:T(8,128)(2,1)S(1)}, bf16[256,1536]{1,0:T(8,128)(2,1)S(1)}, u32[]{:S(2)}, u32[]{:S(2)}) collective-permute-start(bf16[256,1536]{1,0:T(8,128)(2,1)S(1)} %get-tuple-element.55), channel_id=1, source_target_pairs={{0,8},{1,9},{2,10},{3,11},{4,12},{5,13},{6,14},{7,15},{8,0},{9,1},... | collective-permute-start | bytes 2359304 | tf_op jit(solution)/shard_map/ppermute | solution.py:40
  97.0 19.5 %collective-permute-start.25 = (bf16[256,1536]{1,0:T(8,128)(2,1)S(1)}, bf16[256,1536]{1,0:T(8,128)(2,1)S(1)}, u32[]{:S(2)}, u32[]{:S(2)}) collective-permute-start(bf16[256,1536]{1,0:T(8,128)(2,1)S(1)} %get-tuple-element.56), channel_id=1, source_target_pairs={{0,12},{1,13},{2,14},{3,15},{4,0},{5,1},{6,2},{7,3},{8,4},{9,5},{1... | collective-permute-start | bytes 2359304 | tf_op jit(solution)/shard_map/ppermute | solution.py:40
  117.0 7.0 %collective-permute-start.27 = (bf16[64,1536]{1,0:T(8,128)(2,1)S(1)}, bf16[64,1536]{1,0:T(8,128)(2,1)S(1)}, u32[]{:S(2)}, u32[]{:S(2)}) collective-permute-start(bf16[64,1536]{1,0:T(8,128)(2,1)S(1)} %get-tuple-element.65), channel_id=1, source_target_pairs={{0,1},{1,2},{2,3},{3,0},{4,5},{5,6},{6,7},{7,4},{8,9},{9,10},{10,1... | collective-permute-start | bytes 589832 | tf_op jit(solution)/shard_map/ppermute | solution.py:40
  117.7 8.6 %collective-permute-start.28 = (bf16[64,1536]{1,0:T(8,128)(2,1)S(1)}, bf16[64,1536]{1,0:T(8,128)(2,1)S(1)}, u32[]{:S(2)}, u32[]{:S(2)}) collective-permute-start(bf16[64,1536]{1,0:T(8,128)(2,1)S(1)} %get-tuple-element.67), channel_id=1, source_target_pairs={{0,2},{1,3},{2,0},{3,1},{4,6},{5,7},{6,4},{7,5},{8,10},{9,11},{10,... | collective-permute-start | bytes 589832 | tf_op jit(solution)/shard_map/ppermute | solution.py:40
  120.5 6.4 %collective-permute-start.29 = (bf16[64,1536]{1,0:T(8,128)(2,1)S(1)}, bf16[64,1536]{1,0:T(8,128)(2,1)S(1)}, u32[]{:S(2)}, u32[]{:S(2)}) collective-permute-start(bf16[64,1536]{1,0:T(8,128)(2,1)S(1)} %get-tuple-element.66), channel_id=1, source_target_pairs={{0,3},{1,0},{2,1},{3,2},{4,7},{5,4},{6,5},{7,6},{8,11},{9,8},{10,9... | collective-permute-start | bytes 589832 | tf_op jit(solution)/shard_map/ppermute | solution.py:40

commit v5 on v4

--- a/solution.py
+++ b/solution.py
@@ -68,7 +68,7 @@
 
 
 def gather_second(stage):
-    received = {step: from_grid(stage, False, step) for step in (2, 1, 3)}
+    received = {step: from_grid(stage, False, step) for step in (3, 2, 1)}
     return [stage] + [received[step] for step in (1, 2, 3)]
 
 

time: 128 us -> 128 us (level)
  no operation moved by 1% of the time
where the time goes in v5:
time: 128 us
  waiting for transfers between devices  55.5 us (43%)
  starting transfers between devices  36 us (28%)
  Pallas kernels  26.1 us (20%)
  other arithmetic  7.85 us (6%)
  local copies, waits for them, and re-layouts  1.44 us (1%)
    ppermute x9, waiting for transfers between devices, pair_y(): return lax.ppermute(value, ('y', 'k'), pairs)  28 us
    ppermute x12, starting transfers between devices, from_grid(): return lax.ppermute(value, ('k', 'x', 'z'), shift_grid(first, step))  18 us
    ppermute x12, waiting for transfers between devices, from_grid(): return lax.ppermute(value, ('k', 'x', 'z'), shift_grid(first, step))  16.3 us
    ppermute x9, starting transfers between devices, pair_y(): return lax.ppermute(value, ('y', 'k'), pairs)  13.2 us
    ppermute x5, waiting for transfers between devices, pair_grid(): return lax.ppermute(value, ('k', 'x', 'z'), pairs)  10.2 us
    pallas_call x1, Pallas kernels, up_gradient(): pl.pallas_call(up_kernel, grid=(m // TILE,), out_shape=jax.ShapeDtypeStru...  7.36 us
    pallas_call x1, Pallas kernels, down_gradient(): pl.pallas_call(down_kernel, grid=(m // TILE,), out_shape=jax.ShapeDtypeSt...  6.97 us
    ppermute x5, starting transfers between devices, pair_grid(): return lax.ppermute(value, ('k', 'x', 'z'), pairs)  4.4 us
  transfers between devices with their start and end apart: 30, of which 20 were waited for; matrix products, arithmetic and copies ran while one was open for 6% of the time, Pallas kernels for 17%

profile of v5, /device:TPU:0, one launch (start us, length us, event | category | flops | bytes accessed | tf_op | source)
XLA Modules:
  0.0 127.7 jit_solution(7982871191282795442)
XLA Ops:
  0.7 2.9 %collective-permute-start = (bf16[64,1536]{1,0:T(8,128)(2,1)}, bf16[64,1536]{1,0:T(8,128)(2,1)S(1)}, u32[]{:S(2)}, u32[]{:S(2)}) collective-permute-start(bf16[64,1536]{1,0:T(8,128)(2,1)} %param.9), channel_id=1, source_target_pairs={{0,12},{1,13},{2,14},{3,15},{4,0},{5,1},{6,2},{7,3},{8,4},{9,5},{1... | collective-permute-start | bytes 589832 | tf_op jit(solution)/shard_map/ppermute | solution.py:40
  3.6 0.8 collective-permute-start.1
  4.4 0.9 collective-permute-start.2
  5.3 1.2 fusion.10
  6.4 0.9 constant_dynamic-update-slice_fusion.3
  7.4 1.8 %collective-permute-done = bf16[64,1536]{1,0:T(8,128)(2,1)S(1)} collective-permute-done((bf16[64,1536]{1,0:T(8,128)(2,1)}, bf16[64,1536]{1,0:T(8,128)(2,1)S(1)}, u32[]{:S(2)}, u32[]{:S(2)}) %collective-permute-start) | collective-permute-done | bytes 196640 | tf_op jit(solution)/shard_map/ppermute | solution.py:40
  9.2 1.8 %collective-permute-done.1 = bf16[64,1536]{1,0:T(8,128)(2,1)S(1)} collective-permute-done((bf16[64,1536]{1,0:T(8,128)(2,1)}, bf16[64,1536]{1,0:T(8,128)(2,1)S(1)}, u32[]{:S(2)}, u32[]{:S(2)}) %collective-permute-start.1) | collective-permute-done | bytes 196640 | tf_op jit(solution)/shard_map/ppermute | solution.py:40
  11.1 2.0 %collective-permute-done.2 = bf16[64,1536]{1,0:T(8,128)(2,1)S(1)} collective-permute-done((bf16[64,1536]{1,0:T(8,128)(2,1)}, bf16[64,1536]{1,0:T(8,128)(2,1)S(1)}, u32[]{:S(2)}, u32[]{:S(2)}) %collective-permute-start.2) | collective-permute-done | bytes 196640 | tf_op jit(solution)/shard_map/ppermute | solution.py:40
  13.1 4.1 %collective-permute-start.3 = (bf16[256,1536]{1,0:T(8,128)(2,1)S(1)}, bf16[256,1536]{1,0:T(8,128)(2,1)S(1)}, u32[]{:S(2)}, u32[]{:S(2)}) collective-permute-start(bf16[256,1536]{1,0:T(8,128)(2,1)S(1)} %constant_dynamic-update-slice_fusion.p0), channel_id=1, source_target_pairs={{0,3},{1,0},{2,1},{3,2},{4,7},{5,4},{6,5},{7,6},{8,11},{9,8},{10,9... | collective-permute-start | bytes 2359304 | tf_op jit(solution)/shard_map/ppermute | solution.py:40
  17.2 1.3 collective-permute-start.9
  18.5 3.0 %collective-permute-start.5 = (bf16[128,1536]{1,0:T(8,128)(2,1)S(1)}, bf16[128,1536]{1,0:T(8,128)(2,1)S(1)}, u32[]{:S(2)}, u32[]{:S(2)}) collective-permute-start(bf16[128,1536]{1,0:T(8,128)(2,1)S(1)} %fusion.10), channel_id=1, source_target_pairs={{0,96},{16,48},{32,64},{48,16},{64,32},{80,112},{96,0},{112,80},{1... | collective-permute-start | bytes 1179656 | tf_op jit(solution)/shard_map/ppermute | solution.py:48
  21.5 4.8 %collective-permute-done.4 = bf16[64,1536]{1,0:T(8,128)(2,1)S(1)} collective-permute-done((bf16[64,1536]{1,0:T(8,128)(2,1)S(1)}, bf16[64,1536]{1,0:T(8,128)(2,1)S(1)}, u32[]{:S(2)}, u32[]{:S(2)}) %collective-permute-start.4) | collective-permute-done | bytes 196640 | tf_op jit(solution)/shard_map/ppermute | solution.py:59
  26.3 1.6 %collective-permute-start.6 = (bf16[128,1536]{1,0:T(8,128)(2,1)S(1)}, bf16[128,1536]{1,0:T(8,128)(2,1)S(1)}, u32[]{:S(2)}, u32[]{:S(2)}) collective-permute-start(bf16[128,1536]{1,0:T(8,128)(2,1)S(1)} %fusion.10), channel_id=1, source_target_pairs={{0,32},{16,112},{32,0},{48,80},{64,96},{80,48},{96,64},{112,16},{1... | collective-permute-start | bytes 1179656 | tf_op jit(solution)/shard_map/ppermute | solution.py:48
  28.4 3.4 %fusion.1.w = bf16[1536,1536]{1,0:T(8,128)(2,1)S(1)} fusion(bf16[1536,1536]{1,0:T(8,128)(2,1)} %param.10, f32[48,1536]{1,0:T(8,128)S(1)} %multiply_exponential_fusion.1), kind=kLoop, calls=%fused_computation.3 | loop fusion | flops 7077888 | bytes 9732096 | tf_op jit(solution)/shard_map/convert_element_type | solution.py:17
  32.0 0.9 fusion.w
  33.0 1.1 collective-permute-done.6
  34.1 4.2 %collective-permute-done.7 = bf16[128,1536]{1,0:T(8,128)(2,1)S(1)} collective-permute-done((bf16[128,1536]{1,0:T(8,128)(2,1)S(1)}, bf16[128,1536]{1,0:T(8,128)(2,1)S(1)}, u32[]{:S(2)}, u32[]{:S(2)}) %collective-permute-start.7) | collective-permute-done | bytes 393248 | tf_op jit(solution)/shard_map/ppermute | solution.py:48
  38.3 0.5 collective-permute-done.9.p3
  38.8 1.7 %hidden_other.1 = (bf16[256,1536]{1,0:T(8,128)(2,1)S(1)}, bf16[1024,1536]{1,0:T(8,128)(2,1)S(1)}) custom-call(bf16[256,1536]{1,0:T(8,128)(2,1)S(1)} %constant_dynamic-update-slice_fusion.p0, bf16[256,1536]{1,0:T(8,128)(2,1)S(1)} %collective-permute-done.3.p1, bf16[256,1536]{1,0:T(8,128)(2,1)S(1)} %collective-permute-done.8.p2, ...), custom_call_target="tpu_custom_call" | custom-call | flops 2415919104 | bytes 9437184 | tf_op jit(solution)/shard_map/hidden_other/pallas_call | solution.py:136
  40.6 1.4 %hidden_own.1 = f32[256,1536]{1,0:T(8,128)S(1)} custom-call(bf16[1024,1536]{1,0:T(8,128)(2,1)S(1)} %get-tuple-element.39.held.refs_2_, bf16[1536,1536]{1,0:T(8,128)(2,1)S(1)} %fusion.w), custom_call_target="tpu_custom_call" | custom-call | flops 1207959552 | bytes 9437184 | tf_op jit(solution)/shard_map/hidden_own/pallas_call | solution.py:156
  42.0 0.9 collective-permute-done.10
  43.0 2.6 %hidden_first.1 = (bf16[256,1536]{1,0:T(8,128)(2,1)S(1)}, f32[256,1536]{1,0:T(8,128)S(1)}) custom-call(bf16[1024,1536]{1,0:T(8,128)(2,1)S(1)} %get-tuple-element.39.held.refs_2_, bf16[1536,1536]{1,0:T(8,128)(2,1)S(1)} %fusion.w), custom_call_target="tpu_custom_call" | custom-call | flops 2415919104 | bytes 10223616 | tf_op jit(solution)/shard_map/hidden_first/pallas_call | solution.py:181
  46.0 0.7 collective-permute-start.14
  46.7 1.7 %collective-permute-start.13 = (bf16[128,1536]{1,0:T(8,128)(2,1)S(1)}, bf16[128,1536]{1,0:T(8,128)(2,1)S(1)}, u32[]{:S(2)}, u32[]{:S(2)}) collective-permute-start(bf16[128,1536]{1,0:T(8,128)(2,1)S(1)} %get-tuple-element.69), channel_id=1, source_target_pairs={{0,32},{16,112},{32,0},{48,80},{64,96},{80,48},{96,64},{112,16},{1... | collective-permute-start | bytes 1179656 | tf_op jit(solution)/shard_map/ppermute | solution.py:48
  49.0 5.5 %collective-permute-done.13 = bf16[128,1536]{1,0:T(8,128)(2,1)S(1)} collective-permute-done((bf16[128,1536]{1,0:T(8,128)(2,1)S(1)}, bf16[128,1536]{1,0:T(8,128)(2,1)S(1)}, u32[]{:S(2)}, u32[]{:S(2)}) %collective-permute-start.13) | collective-permute-done | bytes 393248 | tf_op jit(solution)/shard_map/ppermute | solution.py:48
  55.1 3.0 %collective-permute-start.15 = (bf16[128,1536]{1,0:T(8,128)(2,1)S(1)}, bf16[128,1536]{1,0:T(8,128)(2,1)S(1)}, u32[]{:S(2)}, u32[]{:S(2)}) collective-permute-start(bf16[128,1536]{1,0:T(8,128)(2,1)S(1)} %slice_add_fusion), channel_id=1, source_target_pairs={{0,96},{16,48},{32,64},{48,16},{64,32},{80,112},{96,0},{112,80},{1... | collective-permute-start | bytes 1179656 | tf_op jit(solution)/shard_map/ppermute | solution.py:48
  58.1 1.9 %collective-permute-start.17 = (bf16[256,1536]{1,0:T(8,128)(2,1)S(1)}, bf16[256,1536]{1,0:T(8,128)(2,1)S(1)}, u32[]{:S(2)}, u32[]{:S(2)}) collective-permute-start(bf16[256,1536]{1,0:T(8,128)(2,1)S(1)} %constant_dynamic-update-slice_fusion.4.rest_0_), channel_id=1, source_target_pairs={{0,1},{1,0},{2,3},{3,2},{4,5},{5,4},{6,7},{7,6},{8,9},{9,8},{10,11... | collective-permute-start | bytes 2359304 | tf_op jit(solution)/shard_map/ppermute | solution.py:59
  60.1 0.5 collective-permute-start.18
  60.6 4.2 %collective-permute-done.15 = bf16[128,1536]{1,0:T(8,128)(2,1)S(1)} collective-permute-done((bf16[128,1536]{1,0:T(8,128)(2,1)S(1)}, bf16[128,1536]{1,0:T(8,128)(2,1)S(1)}, u32[]{:S(2)}, u32[]{:S(2)}) %collective-permute-start.15) | collective-permute-done | bytes 393248 | tf_op jit(solution)/shard_map/ppermute | solution.py:48
  65.2 3.0 %collective-permute-start.16 = (bf16[128,1536]{1,0:T(8,128)(2,1)S(1)}, bf16[128,1536]{1,0:T(8,128)(2,1)S(1)}, u32[]{:S(2)}, u32[]{:S(2)}) collective-permute-start(bf16[128,1536]{1,0:T(8,128)(2,1)S(1)} %fusion.9), channel_id=1, source_target_pairs={{0,96},{16,48},{32,64},{48,16},{64,32},{80,112},{96,0},{112,80},{1... | collective-permute-start | bytes 1179656 | tf_op jit(solution)/shard_map/ppermute | solution.py:48
  68.2 2.0 %collective-permute-done.17.rest_1_ = bf16[256,1536]{1,0:T(8,128)(2,1)S(1)} collective-permute-done((bf16[256,1536]{1,0:T(8,128)(2,1)S(1)}, bf16[256,1536]{1,0:T(8,128)(2,1)S(1)}, u32[]{:S(2)}, u32[]{:S(2)}) %collective-permute-start.17) | collective-permute-done | bytes 786464 | tf_op jit(solution)/shard_map/ppermute | solution.py:59
  70.2 3.0 %collective-permute-done.18.rest_2_ = bf16[256,1536]{1,0:T(8,128)(2,1)S(1)} collective-permute-done((bf16[256,1536]{1,0:T(8,128)(2,1)S(1)}, bf16[256,1536]{1,0:T(8,128)(2,1)S(1)}, u32[]{:S(2)}, u32[]{:S(2)}) %collective-permute-start.18) | collective-permute-done | bytes 786464 | tf_op jit(solution)/shard_map/ppermute | solution.py:59
  73.3 5.2 %collective-permute-done.16 = bf16[128,1536]{1,0:T(8,128)(2,1)S(1)} collective-permute-done((bf16[128,1536]{1,0:T(8,128)(2,1)S(1)}, bf16[128,1536]{1,0:T(8,128)(2,1)S(1)}, u32[]{:S(2)}, u32[]{:S(2)}) %collective-permute-start.16) | collective-permute-done | bytes 393248 | tf_op jit(solution)/shard_map/ppermute | solution.py:48
  78.5 7.8 %collective-permute-done.20 = bf16[128,1536]{1,0:T(8,128)(2,1)S(1)} collective-permute-done((bf16[128,1536]{1,0:T(8,128)(2,1)S(1)}, bf16[128,1536]{1,0:T(8,128)(2,1)S(1)}, u32[]{:S(2)}, u32[]{:S(2)}) %collective-permute-start.20) | collective-permute-done | bytes 393248 | tf_op jit(solution)/shard_map/ppermute | solution.py:48
  86.5 1.3 %collective-permute-start.26 = (bf16[256,1536]{1,0:T(8,128)(2,1)S(1)}, bf16[256,1536]{1,0:T(8,128)(2,1)S(1)}, u32[]{:S(2)}, u32[]{:S(2)}) collective-permute-start(bf16[256,1536]{1,0:T(8,128)(2,1)S(1)} %collective-permute-done.17.rest_1_), channel_id=1, source_target_pairs={{0,3},{1,2},{2,1},{3,0},{4,7},{5,6},{6,5},{7,4},{8,11},{9,10},{10,... | collective-permute-start | bytes 2359304 | tf_op jit(solution)/shard_map/ppermute | solution.py:59
  87.8 2.6 %input_own.1.own = f32[512,1536]{1,0:T(8,128)S(1)} custom-call(bf16[512,1536]{1,0:T(8,128)(2,1)S(1)} %pad_maximum_fusion.mine, bf16[1536,1536]{1,0:T(8,128)(2,1)S(1)} %fusion.1.w), custom_call_target="tpu_custom_call" | custom-call | flops 2415919104 | bytes 9437184 | tf_op jit(solution)/shard_map/input_own/pallas_call | solution.py:202
  90.5 3.4 %input_all.1 = (f32[256,1536]{1,0:T(8,128)S(1)}, bf16[256,1536]{1,0:T(8,128)(2,1)S(1)}, bf16[256,1536]{1,0:T(8,128)(2,1)S(1)}, bf16[256,1536]{1,0:T(8,128)(2,1)S(1)}) custom-call(bf16[512,1536]{1,0:T(8,128)(2,1)S(1)} %collective-permute-done.22.theirs, bf16[1536,1536]{1,0:T(8,128)(2,1)S(1)} %fusion.1.w, f32[512,1536]{1,0:T(8,128)S(1)} %input_own.1.own), custom_call_target="tpu_custom_call" | custom-call | flops 2415919104 | bytes 12582912 | tf_op jit(solution)/shard_map/input_all/pallas_call | solution.py:227
  93.9 3.0 %collective-permute-start.24 = (bf16[256,1536]{1,0:T(8,128)(2,1)S(1)}, bf16[256,1536]{1,0:T(8,128)(2,1)S(1)}, u32[]{:S(2)}, u32[]{:S(2)}) collective-permute-start(bf16[256,1536]{1,0:T(8,128)(2,1)S(1)} %get-tuple-element.55), channel_id=1, source_target_pairs={{0,8},{1,9},{2,10},{3,11},{4,12},{5,13},{6,14},{7,15},{8,0},{9,1},... | collective-permute-start | bytes 2359304 | tf_op jit(solution)/shard_map/ppermute | solution.py:40
  97.4 7.0 %down_gradient.1 = bf16[1536,1536]{1,0:T(8,128)(2,1)} custom-call(bf16[512,1536]{1,0:T(8,128)(2,1)S(1)} %pad_maximum_fusion.1.refs_0_, bf16[512,1536]{1,0:T(8,128)(2,1)S(1)} %collective-permute-done.21.refs_1_, bf16[1024,1536]{1,0:T(8,128)(2,1)S(1)} %get-tuple-element.39.held.refs_2_), custom_call_target="tpu_custom_call" | custom-call | flops 4831838208 | bytes 11010048 | tf_op jit(solution)/shard_map/down_gradient/pallas_call | solution.py:253
  104.4 7.4 %up_gradient.1 = bf16[1536,1536]{1,0:T(8,128)(2,1)} custom-call(bf16[512,1536]{1,0:T(8,128)(2,1)S(1)} %pad_maximum_fusion.mine, bf16[512,1536]{1,0:T(8,128)(2,1)S(1)} %collective-permute-done.22.theirs, bf16[256,1536]{1,0:T(8,128)(2,1)S(1)} %constant_dynamic-update-slice_fusion.4.rest_0_, bf16[256,1536]{1,0:T(8,128)(2,1)S(1)} %collective-permute-done.17.rest_1_, ...), custom_call_target="tpu_custom_call" | custom-call | flops 4831838208 | bytes 11010048 | tf_op jit(solution)/shard_map/up_gradient/pallas_call | solution.py:285
  111.7 4.3 %collective-permute-done.23 = bf16[256,1536]{1,0:T(8,128)(2,1)S(1)} collective-permute-done((bf16[256,1536]{1,0:T(8,128)(2,1)S(1)}, bf16[256,1536]{1,0:T(8,128)(2,1)S(1)}, u32[]{:S(2)}, u32[]{:S(2)}) %collective-permute-start.23) | collective-permute-done | bytes 786464 | tf_op jit(solution)/shard_map/ppermute | solution.py:40
  117.0 0.7 collective-permute-start.27
  117.7 2.8 %collective-permute-start.28 = (bf16[64,1536]{1,0:T(8,128)(2,1)S(1)}, bf16[64,1536]{1,0:T(8,128)(2,1)S(1)}, u32[]{:S(2)}, u32[]{:S(2)}) collective-permute-start(bf16[64,1536]{1,0:T(8,128)(2,1)S(1)} %get-tuple-element.67), channel_id=1, source_target_pairs={{0,2},{1,3},{2,0},{3,1},{4,6},{5,7},{6,4},{7,5},{8,10},{9,11},{10,... | collective-permute-start | bytes 589832 | tf_op jit(solution)/shard_map/ppermute | solution.py:40
  120.5 1.0 collective-permute-start.29
  121.5 2.4 %collective-permute-done.27 = bf16[64,1536]{1,0:T(8,128)(2,1)S(1)} collective-permute-done((bf16[64,1536]{1,0:T(8,128)(2,1)S(1)}, bf16[64,1536]{1,0:T(8,128)(2,1)S(1)}, u32[]{:S(2)}, u32[]{:S(2)}) %collective-permute-start.27) | collective-permute-done | bytes 196640 | tf_op jit(solution)/shard_map/ppermute | solution.py:40
  123.9 2.3 %collective-permute-done.28 = bf16[64,1536]{1,0:T(8,128)(2,1)S(1)} collective-permute-done((bf16[64,1536]{1,0:T(8,128)(2,1)S(1)}, bf16[64,1536]{1,0:T(8,128)(2,1)S(1)}, u32[]{:S(2)}, u32[]{:S(2)}) %collective-permute-start.28) | collective-permute-done | bytes 196640 | tf_op jit(solution)/shard_map/ppermute | solution.py:40
  126.2 0.7 collective-permute-done.29
  126.9 0.8 add_convert_fusion
  (55 shorter events, 4.8 us)
Async XLA Ops:
  0.6 17.8 %copy-start.3 = (bf16[64,1536]{1,0:T(8,128)(2,1)S(1)}, bf16[64,1536]{1,0:T(8,128)(2,1)}, u32[]{:S(2)}) copy-start(bf16[64,1536]{1,0:T(8,128)(2,1)} %param.7) | copy-start | bytes 589828
  0.6 20.8 %copy-start.1 = (s32[48,1536]{1,0:T(8,128)S(1)}, s32[48,1536]{1,0:T(8,128)}, u32[]{:S(2)}) copy-start(s32[48,1536]{1,0:T(8,128)} %param.11) | copy-start | bytes 884740
  0.7 27.7 %copy-start.2 = (s32[48,1536]{1,0:T(8,128)S(1)}, s32[48,1536]{1,0:T(8,128)}, u32[]{:S(2)}) copy-start(s32[48,1536]{1,0:T(8,128)} %param.13) | copy-start | bytes 884740
  0.7 8.6 %collective-permute-start = (bf16[64,1536]{1,0:T(8,128)(2,1)}, bf16[64,1536]{1,0:T(8,128)(2,1)S(1)}, u32[]{:S(2)}, u32[]{:S(2)}) collective-permute-start(bf16[64,1536]{1,0:T(8,128)(2,1)} %param.9), channel_id=1, source_target_pairs={{0,12},{1,13},{2,14},{3,15},{4,0},{5,1},{6,2},{7,3},{8,4},{9,5},{1... | collective-permute-start | bytes 589832 | tf_op jit(solution)/shard_map/ppermute | solution.py:40
  3.6 7.5 %collective-permute-start.1 = (bf16[64,1536]{1,0:T(8,128)(2,1)}, bf16[64,1536]{1,0:T(8,128)(2,1)S(1)}, u32[]{:S(2)}, u32[]{:S(2)}) collective-permute-start(bf16[64,1536]{1,0:T(8,128)(2,1)} %param.9), channel_id=1, source_target_pairs={{0,8},{1,9},{2,10},{3,11},{4,12},{5,13},{6,14},{7,15},{8,0},{9,1},... | collective-permute-start | bytes 589832 | tf_op jit(solution)/shard_map/ppermute | solution.py:40
  4.4 8.7 %collective-permute-start.2 = (bf16[64,1536]{1,0:T(8,128)(2,1)}, bf16[64,1536]{1,0:T(8,128)(2,1)S(1)}, u32[]{:S(2)}, u32[]{:S(2)}) collective-permute-start(bf16[64,1536]{1,0:T(8,128)(2,1)} %param.9), channel_id=1, source_target_pairs={{0,4},{1,5},{2,6},{3,7},{4,8},{5,9},{6,10},{7,11},{8,12},{9,13},{1... | collective-permute-start | bytes 589832 | tf_op jit(solution)/shard_map/ppermute | solution.py:40
  13.1 25.2 %collective-permute-start.3 = (bf16[256,1536]{1,0:T(8,128)(2,1)S(1)}, bf16[256,1536]{1,0:T(8,128)(2,1)S(1)}, u32[]{:S(2)}, u32[]{:S(2)}) collective-permute-start(bf16[256,1536]{1,0:T(8,128)(2,1)S(1)} %constant_dynamic-update-slice_fusion.p0), channel_id=1, source_target_pairs={{0,3},{1,0},{2,1},{3,2},{4,7},{5,4},{6,5},{7,6},{8,11},{9,8},{10,9... | collective-permute-start | bytes 2359304 | tf_op jit(solution)/shard_map/ppermute | solution.py:40
  17.2 21.1 %collective-permute-start.8 = (bf16[256,1536]{1,0:T(8,128)(2,1)S(1)}, bf16[256,1536]{1,0:T(8,128)(2,1)S(1)}, u32[]{:S(2)}, u32[]{:S(2)}) collective-permute-start(bf16[256,1536]{1,0:T(8,128)(2,1)S(1)} %constant_dynamic-update-slice_fusion.p0), channel_id=1, source_target_pairs={{0,2},{1,3},{2,0},{3,1},{4,6},{5,7},{6,4},{7,5},{8,10},{9,11},{10,... | collective-permute-start | bytes 2359304 | tf_op jit(solution)/shard_map/ppermute | solution.py:40
  17.2 21.6 %collective-permute-start.9 = (bf16[256,1536]{1,0:T(8,128)(2,1)S(1)}, bf16[256,1536]{1,0:T(8,128)(2,1)S(1)}, u32[]{:S(2)}, u32[]{:S(2)}) collective-permute-start(bf16[256,1536]{1,0:T(8,128)(2,1)S(1)} %constant_dynamic-update-slice_fusion.p0), channel_id=1, source_target_pairs={{0,1},{1,2},{2,3},{3,0},{4,5},{5,6},{6,7},{7,4},{8,9},{9,10},{10,1... | collective-permute-start | bytes 2359304 | tf_op jit(solution)/shard_map/ppermute | solution.py:40
  18.5 7.8 %collective-permute-start.4 = (bf16[64,1536]{1,0:T(8,128)(2,1)S(1)}, bf16[64,1536]{1,0:T(8,128)(2,1)S(1)}, u32[]{:S(2)}, u32[]{:S(2)}) collective-permute-start(bf16[64,1536]{1,0:T(8,128)(2,1)S(1)} %copy-done.3), channel_id=1, source_target_pairs={{0,4},{1,5},{2,6},{3,7},{4,0},{5,1},{6,2},{7,3},{8,12},{9,13},{10,... | collective-permute-start | bytes 589832 | tf_op jit(solution)/shard_map/ppermute | solution.py:59
  18.5 9.4 %collective-permute-start.5 = (bf16[128,1536]{1,0:T(8,128)(2,1)S(1)}, bf16[128,1536]{1,0:T(8,128)(2,1)S(1)}, u32[]{:S(2)}, u32[]{:S(2)}) collective-permute-start(bf16[128,1536]{1,0:T(8,128)(2,1)S(1)} %fusion.10), channel_id=1, source_target_pairs={{0,96},{16,48},{32,64},{48,16},{64,32},{80,112},{96,0},{112,80},{1... | collective-permute-start | bytes 1179656 | tf_op jit(solution)/shard_map/ppermute | solution.py:48
  26.3 7.8 %collective-permute-start.6 = (bf16[128,1536]{1,0:T(8,128)(2,1)S(1)}, bf16[128,1536]{1,0:T(8,128)(2,1)S(1)}, u32[]{:S(2)}, u32[]{:S(2)}) collective-permute-start(bf16[128,1536]{1,0:T(8,128)(2,1)S(1)} %fusion.10), channel_id=1, source_target_pairs={{0,32},{16,112},{32,0},{48,80},{64,96},{80,48},{96,64},{112,16},{1... | collective-permute-start | bytes 1179656 | tf_op jit(solution)/shard_map/ppermute | solution.py:48
  27.9 10.4 %collective-permute-start.7 = (bf16[128,1536]{1,0:T(8,128)(2,1)S(1)}, bf16[128,1536]{1,0:T(8,128)(2,1)S(1)}, u32[]{:S(2)}, u32[]{:S(2)}) collective-permute-start(bf16[128,1536]{1,0:T(8,128)(2,1)S(1)} %collective-permute-done.5), channel_id=1, source_target_pairs={{0,32},{16,112},{32,0},{48,80},{64,96},{80,48},{96,64},{112,16},{1... | collective-permute-start | bytes 1179656 | tf_op jit(solution)/shard_map/ppermute | solution.py:48
  28.3 3.6 %slice-start = ((s8[4718592]{0:T(1024)(128)(4,1)}), s8[4194304]{0:T(1024)(128)(4,1)S(1)}, s32[]{:S(2)}) async-start(s8[4718592]{0:T(1024)(128)(4,1)} %bitcast.8), calls=%async_computation | async-start | bytes 8388608
  28.4 3.7 %slice-start.1 = ((s8[4718592]{0:T(1024)(128)(4,1)}), s8[524288]{0:T(1024)(128)(4,1)S(1)}, s32[]{:S(2)}) async-start(s8[4718592]{0:T(1024)(128)(4,1)} %bitcast.8), calls=%async_computation.1 | async-start | bytes 1048576
  40.5 2.4 %collective-permute-start.10 = (bf16[256,1536]{1,0:T(8,128)(2,1)S(1)}, bf16[256,1536]{1,0:T(8,128)(2,1)S(1)}, u32[]{:S(2)}, u32[]{:S(2)}) collective-permute-start(bf16[256,1536]{1,0:T(8,128)(2,1)S(1)} %get-tuple-element.38), channel_id=1, source_target_pairs={{0,16},{16,0},{1,17},{17,1},{2,18},{18,2},{3,19},{19,3},{4,20},{20... | collective-permute-start | bytes 2359304 | tf_op jit(solution)/shard_map/ppermute | solution.py:63
  45.7 3.1 %collective-permute-start.11 = (bf16[256,1536]{1,0:T(8,128)(2,1)S(1)}, bf16[256,1536]{1,0:T(8,128)(2,1)S(1)}, u32[]{:S(2)}, u32[]{:S(2)}) collective-permute-start(bf16[256,1536]{1,0:T(8,128)(2,1)S(1)} %get-tuple-element.41), channel_id=1, source_target_pairs={{0,16},{16,0},{1,17},{17,1},{2,18},{18,2},{3,19},{19,3},{4,20},{20... | collective-permute-start | bytes 2359304 | tf_op jit(solution)/shard_map/ppermute | solution.py:63
  46.0 9.1 %collective-permute-start.14 = (bf16[128,1536]{1,0:T(8,128)(2,1)S(1)}, bf16[128,1536]{1,0:T(8,128)(2,1)S(1)}, u32[]{:S(2)}, u32[]{:S(2)}) collective-permute-start(bf16[128,1536]{1,0:T(8,128)(2,1)S(1)} %pad_maximum_fusion.2), channel_id=1, source_target_pairs={{0,12},{1,13},{2,14},{3,15},{4,8},{5,9},{6,10},{7,11},{8,4},{9,5},... | collective-permute-start | bytes 1179656 | tf_op jit(solution)/shard_map/ppermute | solution.py:59
  46.7 7.9 %collective-permute-start.13 = (bf16[128,1536]{1,0:T(8,128)(2,1)S(1)}, bf16[128,1536]{1,0:T(8,128)(2,1)S(1)}, u32[]{:S(2)}, u32[]{:S(2)}) collective-permute-start(bf16[128,1536]{1,0:T(8,128)(2,1)S(1)} %get-tuple-element.69), channel_id=1, source_target_pairs={{0,32},{16,112},{32,0},{48,80},{64,96},{80,48},{96,64},{112,16},{1... | collective-permute-start | bytes 1179656 | tf_op jit(solution)/shard_map/ppermute | solution.py:48
  48.4 12.2 %collective-permute-start.12 = (bf16[128,1536]{1,0:T(8,128)(2,1)S(1)}, bf16[128,1536]{1,0:T(8,128)(2,1)S(1)}, u32[]{:S(2)}, u32[]{:S(2)}) collective-permute-start(bf16[128,1536]{1,0:T(8,128)(2,1)S(1)} %get-tuple-element.68), channel_id=1, source_target_pairs={{0,32},{16,112},{32,0},{48,80},{64,96},{80,48},{96,64},{112,16},{1... | collective-permute-start | bytes 1179656 | tf_op jit(solution)/shard_map/ppermute | solution.py:48
  49.0 15.7 %copy-start = (bf16[128,1536]{1,0:T(8,128)(2,1)S(1)}, bf16[128,1536]{1,0:T(8,128)(2,1)}, u32[]{:S(2)}) copy-start(bf16[128,1536]{1,0:T(8,128)(2,1)} %param.8) | copy-start | bytes 1179652
  55.1 9.6 %collective-permute-start.15 = (bf16[128,1536]{1,0:T(8,128)(2,1)S(1)}, bf16[128,1536]{1,0:T(8,128)(2,1)S(1)}, u32[]{:S(2)}, u32[]{:S(2)}) collective-permute-start(bf16[128,1536]{1,0:T(8,128)(2,1)S(1)} %slice_add_fusion), channel_id=1, source_target_pairs={{0,96},{16,48},{32,64},{48,16},{64,32},{80,112},{96,0},{112,80},{1... | collective-permute-start | bytes 1179656 | tf_op jit(solution)/shard_map/ppermute | solution.py:48
  58.1 12.1 %collective-permute-start.17 = (bf16[256,1536]{1,0:T(8,128)(2,1)S(1)}, bf16[256,1536]{1,0:T(8,128)(2,1)S(1)}, u32[]{:S(2)}, u32[]{:S(2)}) collective-permute-start(bf16[256,1536]{1,0:T(8,128)(2,1)S(1)} %constant_dynamic-update-slice_fusion.4.rest_0_), channel_id=1, source_target_pairs={{0,1},{1,0},{2,3},{3,2},{4,5},{5,4},{6,7},{7,6},{8,9},{9,8},{10,11... | collective-permute-start | bytes 2359304 | tf_op jit(solution)/shard_map/ppermute | solution.py:59
  60.1 13.2 %collective-permute-start.18 = (bf16[256,1536]{1,0:T(8,128)(2,1)S(1)}, bf16[256,1536]{1,0:T(8,128)(2,1)S(1)}, u32[]{:S(2)}, u32[]{:S(2)}) collective-permute-start(bf16[256,1536]{1,0:T(8,128)(2,1)S(1)} %constant_dynamic-update-slice_fusion.4.rest_0_), channel_id=1, source_target_pairs={{0,3},{1,2},{2,1},{3,0},{4,7},{5,6},{6,5},{7,4},{8,11},{9,10},{10,... | collective-permute-start | bytes 2359304 | tf_op jit(solution)/shard_map/ppermute | solution.py:59
  60.5 25.8 %collective-permute-start.21 = (bf16[512,1536]{1,0:T(8,128)(2,1)S(1)}, bf16[512,1536]{1,0:T(8,128)(2,1)S(1)}, u32[]{:S(2)}, u32[]{:S(2)}) collective-permute-start(bf16[512,1536]{1,0:T(8,128)(2,1)S(1)} %pad_maximum_fusion.1.refs_0_), channel_id=1, source_target_pairs={{0,16},{16,0},{1,17},{17,1},{2,18},{18,2},{3,19},{19,3},{4,20},{20... | collective-permute-start | bytes 4718600 | tf_op jit(solution)/shard_map/ppermute | solution.py:63
  65.2 13.3 %collective-permute-start.16 = (bf16[128,1536]{1,0:T(8,128)(2,1)S(1)}, bf16[128,1536]{1,0:T(8,128)(2,1)S(1)}, u32[]{:S(2)}, u32[]{:S(2)}) collective-permute-start(bf16[128,1536]{1,0:T(8,128)(2,1)S(1)} %fusion.9), channel_id=1, source_target_pairs={{0,96},{16,48},{32,64},{48,16},{64,32},{80,112},{96,0},{112,80},{1... | collective-permute-start | bytes 1179656 | tf_op jit(solution)/shard_map/ppermute | solution.py:48
  68.2 10.3 %collective-permute-start.19 = (bf16[128,1536]{1,0:T(8,128)(2,1)S(1)}, bf16[128,1536]{1,0:T(8,128)(2,1)S(1)}, u32[]{:S(2)}, u32[]{:S(2)}) collective-permute-start(bf16[128,1536]{1,0:T(8,128)(2,1)S(1)} %fusion.9), channel_id=1, source_target_pairs={{0,32},{16,112},{32,0},{48,80},{64,96},{80,48},{96,64},{112,16},{1... | collective-permute-start | bytes 1179656 | tf_op jit(solution)/shard_map/ppermute | solution.py:48
  78.5 7.8 %collective-permute-start.20 = (bf16[128,1536]{1,0:T(8,128)(2,1)S(1)}, bf16[128,1536]{1,0:T(8,128)(2,1)S(1)}, u32[]{:S(2)}, u32[]{:S(2)}) collective-permute-start(bf16[128,1536]{1,0:T(8,128)(2,1)S(1)} %collective-permute-done.16), channel_id=1, source_target_pairs={{0,32},{16,112},{32,0},{48,80},{64,96},{80,48},{96,64},{112,16},{1... | collective-permute-start | bytes 1179656 | tf_op jit(solution)/shard_map/ppermute | solution.py:48
  86.4 4.1 %collective-permute-start.22 = (bf16[512,1536]{1,0:T(8,128)(2,1)S(1)}, bf16[512,1536]{1,0:T(8,128)(2,1)S(1)}, u32[]{:S(2)}, u32[]{:S(2)}) collective-permute-start(bf16[512,1536]{1,0:T(8,128)(2,1)S(1)} %pad_maximum_fusion.mine), channel_id=1, source_target_pairs={{0,16},{16,0},{1,17},{17,1},{2,18},{18,2},{3,19},{19,3},{4,20},{20... | collective-permute-start | bytes 4718600 | tf_op jit(solution)/shard_map/ppermute | solution.py:63
  86.5 17.9 %collective-permute-start.26 = (bf16[256,1536]{1,0:T(8,128)(2,1)S(1)}, bf16[256,1536]{1,0:T(8,128)(2,1)S(1)}, u32[]{:S(2)}, u32[]{:S(2)}) collective-permute-start(bf16[256,1536]{1,0:T(8,128)(2,1)S(1)} %collective-permute-done.17.rest_1_), channel_id=1, source_target_pairs={{0,3},{1,2},{2,1},{3,0},{4,7},{5,6},{6,5},{7,4},{8,11},{9,10},{10,... | collective-permute-start | bytes 2359304 | tf_op jit(solution)/shard_map/ppermute | solution.py:59
  93.9 22.2 %collective-permute-start.23 = (bf16[256,1536]{1,0:T(8,128)(2,1)S(1)}, bf16[256,1536]{1,0:T(8,128)(2,1)S(1)}, u32[]{:S(2)}, u32[]{:S(2)}) collective-permute-start(bf16[256,1536]{1,0:T(8,128)(2,1)S(1)} %get-tuple-element.54), channel_id=1, source_target_pairs={{0,4},{1,5},{2,6},{3,7},{4,8},{5,9},{6,10},{7,11},{8,12},{9,13},{1... | collective-permute-start | bytes 2359304 | tf_op jit(solution)/shard_map/ppermute | solution.py:40
  93.9 22.1 %collective-permute-start.24 = (bf16[256,1536]{1,0:T(8,128)(2,1)S(1)}, bf16[256,1536]{1,0:T(8,128)(2,1)S(1)}, u32[]{:S(2)}, u32[]{:S(2)}) collective-permute-start(bf16[256,1536]{1,0:T(8,128)(2,1)S(1)} %get-tuple-element.55), channel_id=1, source_target_pairs={{0,8},{1,9},{2,10},{3,11},{4,12},{5,13},{6,14},{7,15},{8,0},{9,1},... | collective-permute-start | bytes 2359304 | tf_op jit(solution)/shard_map/ppermute | solution.py:40
  97.0 19.5 %collective-permute-start.25 = (bf16[256,1536]{1,0:T(8,128)(2,1)S(1)}, bf16[256,1536]{1,0:T(8,128)(2,1)S(1)}, u32[]{:S(2)}, u32[]{:S(2)}) collective-permute-start(bf16[256,1536]{1,0:T(8,128)(2,1)S(1)} %get-tuple-element.56), channel_id=1, source_target_pairs={{0,12},{1,13},{2,14},{3,15},{4,0},{5,1},{6,2},{7,3},{8,4},{9,5},{1... | collective-permute-start | bytes 2359304 | tf_op jit(solution)/shard_map/ppermute | solution.py:40
  117.0 7.0 %collective-permute-start.27 = (bf16[64,1536]{1,0:T(8,128)(2,1)S(1)}, bf16[64,1536]{1,0:T(8,128)(2,1)S(1)}, u32[]{:S(2)}, u32[]{:S(2)}) collective-permute-start(bf16[64,1536]{1,0:T(8,128)(2,1)S(1)} %get-tuple-element.65), channel_id=1, source_target_pairs={{0,1},{1,2},{2,3},{3,0},{4,5},{5,6},{6,7},{7,4},{8,9},{9,10},{10,1... | collective-permute-start | bytes 589832 | tf_op jit(solution)/shard_map/ppermute | solution.py:40
  117.7 8.6 %collective-permute-start.28 = (bf16[64,1536]{1,0:T(8,128)(2,1)S(1)}, bf16[64,1536]{1,0:T(8,128)(2,1)S(1)}, u32[]{:S(2)}, u32[]{:S(2)}) collective-permute-start(bf16[64,1536]{1,0:T(8,128)(2,1)S(1)} %get-tuple-element.67), channel_id=1, source_target_pairs={{0,2},{1,3},{2,0},{3,1},{4,6},{5,7},{6,4},{7,5},{8,10},{9,11},{10,... | collective-permute-start | bytes 589832 | tf_op jit(solution)/shard_map/ppermute | solution.py:40
  120.5 6.4 %collective-permute-start.29 = (bf16[64,1536]{1,0:T(8,128)(2,1)S(1)}, bf16[64,1536]{1,0:T(8,128)(2,1)S(1)}, u32[]{:S(2)}, u32[]{:S(2)}) collective-permute-start(bf16[64,1536]{1,0:T(8,128)(2,1)S(1)} %get-tuple-element.66), channel_id=1, source_target_pairs={{0,3},{1,0},{2,1},{3,2},{4,7},{5,4},{6,5},{7,6},{8,11},{9,8},{10,9... | collective-permute-start | bytes 589832 | tf_op jit(solution)/shard_map/ppermute | solution.py:40
